TPU v7x, 512 devices: a whole 4x8x8 slice. The times are simulated.
512 devices in a mesh: fft: 32 (over x, z), band: 16 (over y, core).
Axes of the slice: x: 4, y: 8, z: 8, core: 2. Of those that a mesh axis runs over, the one named last changes fastest.
Arguments:
- psi_real: float32 [16, 64, 64, 128], P('band', 'fft'), may hold values from -6 to 6
- psi_imag: float32 [16, 64, 64, 128], P('band', 'fft'), may hold values from -6 to 6
- potential: float32 [64, 64, 128], P('fft'), may hold values from -3 to 3
- vector_potential: float32 [3], replicated, may hold values from -2 to 2
- occupation: float32 [16], P('band'), may hold values from 0.2 to 2
- projectors: float32 [128, 8, 4096], P('fft'), may hold values from -1.5 to 1.5
- box_offsets: int32 [3, 128], P(None, 'fft'), may hold values from 0 to 127, as said below
- species: int32 [128], P('fft'), may hold values from 0 to 3
- channels: int32 [128, 8], P('fft'), may hold values 0 or 1
- coupling: float32 [4, 8, 8], replicated, may hold values from -8 to 8
Outputs:
- new_real: float32 [16, 64, 64, 128], P('band', 'fft')
- new_imag: float32 [16, 64, 64, 128], P('band', 'fft')
- density: float32 [64, 64, 128], P('fft', 'band')
Inputs may be any that keep to these rules, and one draw needn't show every extreme that they name: Atom a's box starts in slab a // 4: (a // 4) * 2 <= box_offsets[0, a] < (a // 4 + 1) * 2; box_offsets[1, a] < 64 and box_offsets[2, a] < 128. Both ends of the range are reached.
All inputs are finite; a program needn't handle non-finite values. No bound on the sum of `channels` on one device may be relied on, other than what follows from the above.
Results may differ from a plain program's by a relative error of at most 0.00011.
Values sent between devices are 32-bit elements; how exact they have to be, the bound alone decides.
No kernel may reach another device: no remote copies, remote signals or barrier semaphores. Data moves between devices by JAX's collectives and lax.ppermute only.
A program may use at most 64 MiB of HBM per device.

v0:
```python
import math

import jax
import jax.numpy as jnp
from jax import lax
from jax.sharding import PartitionSpec as P

NX = 64
NY = 64
NZ = 128
BX = 16
BY = 16
BZ = 16
NPROJ = 8


time_step = 0.01
kinetic_scale = 0.5 * (2.0 * math.pi / 38.0) ** 2
highest = lax.Precision.HIGHEST


def shifted(block, axis, distance):
    devices = range(lax.axis_size(axis))
    route = [((i - distance) % len(devices), i) for i in devices]
    return lax.ppermute(block, axis, route)


def signed_modes(values, length):
    return jnp.where(values < length // 2, values, values - length).astype(jnp.float32)


def dft_tables(length, sign):
    steps = jnp.arange(length, dtype=jnp.int32)
    turns = steps[:, None] * steps[None, :] % length
    angle = 2.0 * math.pi / length * turns.astype(jnp.float32)
    return (jnp.cos(angle), sign * jnp.sin(angle))


def turn_last(real_part, imag_part, tables):
    cosine, sine = tables
    shape = real_part.shape
    flat_real = real_part.reshape(-1, shape[-1])
    flat_imag = imag_part.reshape(-1, shape[-1])
    out_real = jnp.dot(flat_real, cosine, precision=highest) - jnp.dot(
        flat_imag, sine, precision=highest
    )
    out_imag = jnp.dot(flat_imag, cosine, precision=highest) + jnp.dot(
        flat_real, sine, precision=highest
    )
    return (out_real.reshape(shape), out_imag.reshape(shape))


def turn_axis(real_part, imag_part, tables, form):
    cosine, sine = tables
    out_real = jnp.einsum(form, cosine, real_part, precision=highest) - jnp.einsum(
        form, sine, imag_part, precision=highest
    )
    out_imag = jnp.einsum(form, cosine, imag_part, precision=highest) + jnp.einsum(
        form, sine, real_part, precision=highest
    )
    return (out_real, out_imag)


def kinetic_energy(modes_x, modes_y, modes_z, vector_potential):
    shift_x = modes_x + vector_potential[0]
    shift_y = modes_y + vector_potential[1]
    shift_z = modes_z + vector_potential[2]
    total = shift_x[:, None, None] ** 2 + shift_y[None, :, None] ** 2 + shift_z[None, None, :] ** 2
    return kinetic_scale * total / (NX * NY * NZ)


def box_geometry(boxes, planes, span, vector_potential):
    cell = jnp.arange(BX * BY * BZ, dtype=jnp.int32)
    step_x = cell // (BY * BZ)
    step_y = cell // BZ % BY
    step_z = cell % BZ
    grid_x = (boxes[0][:, None] + step_x) % NX
    grid_y = (boxes[1][:, None] + step_y) % NY
    grid_z = (boxes[2][:, None] + step_z) % NZ
    theta = (
        2.0
        * math.pi
        * (
            vector_potential[0] * grid_x.astype(jnp.float32) / NX
            + vector_potential[1] * grid_y.astype(jnp.float32) / NY
            + vector_potential[2] * grid_z.astype(jnp.float32) / NZ
        )
    )
    local = boxes[0][:, None] % planes + step_x
    valid = ((local >= 0) & (local < span)).astype(jnp.float32)
    flat = (jnp.clip(local, 0, span - 1) * NY + grid_y) * NZ + grid_z
    return (flat, jnp.cos(theta), jnp.sin(theta), valid)


def project(real_part, imag_part, geometry, beta):
    flat, cosine, sine, valid = geometry
    orbs = real_part.shape[0]
    take_real = real_part.reshape(orbs, -1)[:, flat] * valid
    take_imag = imag_part.reshape(orbs, -1)[:, flat] * valid
    turned_real = cosine * take_real - sine * take_imag
    turned_imag = sine * take_real + cosine * take_imag
    coef_real = jnp.einsum("apc,oac->oap", beta, turned_real, precision=highest)
    coef_imag = jnp.einsum("apc,oac->oap", beta, turned_imag, precision=highest)
    return (coef_real, coef_imag)


def couple(coef_real, coef_imag, table):
    dual_real = jnp.einsum("apq,oaq->oap", table, coef_real, precision=highest)
    dual_imag = jnp.einsum("apq,oaq->oap", table, coef_imag, precision=highest)
    return (dual_real, dual_imag)


def spread(dual_real, dual_imag, geometry, beta, span_cells):
    flat, cosine, sine, valid = geometry
    back_real = jnp.einsum("apc,oap->oac", beta, dual_real, precision=highest)
    back_imag = jnp.einsum("apc,oap->oac", beta, dual_imag, precision=highest)
    placed_real = (cosine * back_real + sine * back_imag) * valid
    placed_imag = (cosine * back_imag - sine * back_real) * valid
    zeroed = jnp.zeros((dual_real.shape[0], span_cells), jnp.float32)
    return (zeroed.at[:, flat].add(placed_real), zeroed.at[:, flat].add(placed_imag))


def per_device(
    psi_real,
    psi_imag,
    potential,
    vector_potential,
    occupation,
    projectors,
    box_offsets,
    species,
    channels,
    coupling,
):
    orbs, planes, rows, depth = psi_real.shape
    index = lax.axis_index("fft")
    owned = projectors.shape[0]
    kinds = coupling.shape[0]
    reach = (planes + BX - 2) // planes
    gates = channels.astype(jnp.float32)
    picks = (species[:, None] == jnp.arange(kinds, dtype=jnp.int32)[None, :]).astype(jnp.float32)
    table = jnp.dot(picks, coupling.reshape(kinds, -1), precision=highest).reshape(
        owned, NPROJ, NPROJ
    )
    table = table * gates[:, :, None] * gates[:, None, :]
    forward_z = dft_tables(depth, -1.0)
    inverse_z = dft_tables(depth, 1.0)
    forward_y = dft_tables(rows, -1.0)
    inverse_y = dft_tables(rows, 1.0)
    modes_z = signed_modes(jnp.arange(depth, dtype=jnp.int32), NZ)
    forward_x = dft_tables(NX, -1.0)
    inverse_x = dft_tables(NX, 1.0)
    modes_x = signed_modes(jnp.arange(NX, dtype=jnp.int32), NX)

    def columns(pieces):
        col_real, col_imag = turn_axis(pieces[0], pieces[1], forward_x, "kx,oxyz->okyz")
        width = col_real.shape[2]
        modes_y = signed_modes(jnp.arange(width, dtype=jnp.int32) + index * width, NY)
        energy = kinetic_energy(modes_x, modes_y, modes_z, vector_potential)
        col_real, col_imag = turn_axis(
            col_real * energy, col_imag * energy, inverse_x, "kx,oxyz->okyz"
        )
        return (
            lax.all_to_all(col_real, "fft", split_axis=1, concat_axis=2, tiled=True),
            lax.all_to_all(col_imag, "fft", split_axis=1, concat_axis=2, tiled=True),
        )

    def kinetic_term(real_part, imag_part):
        work_real, work_imag = turn_last(real_part, imag_part, forward_z)
        work_real, work_imag = turn_axis(work_real, work_imag, forward_y, "ky,oxyz->oxkz")
        work_real, work_imag = columns(
            (
                lax.all_to_all(work_real, "fft", split_axis=2, concat_axis=1, tiled=True),
                lax.all_to_all(work_imag, "fft", split_axis=2, concat_axis=1, tiled=True),
            )
        )
        work_real, work_imag = turn_axis(work_real, work_imag, inverse_y, "ky,oxyz->oxkz")
        return turn_last(work_real, work_imag, inverse_z)

    span_planes = planes * (reach + 1)
    geometry = box_geometry(box_offsets, planes, span_planes, vector_potential)

    def nonlocal_term(real_part, imag_part):
        wide_real = [real_part]
        wide_imag = [imag_part]
        for distance in range(1, reach + 1):
            borrowed_real, borrowed_imag = shifted((real_part, imag_part), "fft", -distance)
            wide_real.append(borrowed_real)
            wide_imag.append(borrowed_imag)
        coef_real, coef_imag = project(
            jnp.concatenate(wide_real, 1), jnp.concatenate(wide_imag, 1), geometry, projectors
        )
        dual_real, dual_imag = couple(coef_real, coef_imag, table)
        placed_real, placed_imag = spread(
            dual_real, dual_imag, geometry, projectors, span_planes * rows * depth
        )
        placed_real = placed_real.reshape(orbs, span_planes, rows, depth)
        placed_imag = placed_imag.reshape(orbs, span_planes, rows, depth)
        own_real = placed_real[:, :planes]
        own_imag = placed_imag[:, :planes]
        for distance in range(1, reach + 1):
            lower = distance * planes
            extra_real, extra_imag = shifted(
                (placed_real[:, lower : lower + planes], placed_imag[:, lower : lower + planes]),
                "fft",
                distance,
            )
            own_real = own_real + extra_real
            own_imag = own_imag + extra_imag
        return (own_real, own_imag)

    def hamiltonian(real_part, imag_part):
        kin_real, kin_imag = kinetic_term(real_part, imag_part)
        far_real, far_imag = nonlocal_term(real_part, imag_part)
        return (
            kin_real + potential * real_part + far_real,
            kin_imag + potential * imag_part + far_imag,
        )

    first_real, first_imag = hamiltonian(psi_real, psi_imag)
    step_real = time_step * first_imag
    step_imag = -time_step * first_real
    second_real, second_imag = hamiltonian(step_real, step_imag)
    new_real = psi_real + step_real + 0.5 * time_step * second_imag
    new_imag = psi_imag + step_imag - 0.5 * time_step * second_real
    weighted = jnp.sum(
        occupation[:, None, None, None] * (new_real * new_real + new_imag * new_imag), axis=0
    )
    density = lax.psum_scatter(weighted, "band", scatter_dimension=1, tiled=True)
    return (new_real, new_imag, density)


def solution(mesh):
    placed = (
        P("band", "fft", None, None),
        P("band", "fft", None, None),
        P("fft", None, None),
        P(),
        P("band"),
        P("fft", None, None),
        P(None, "fft"),
        P("fft"),
        P("fft", None),
        P(),
    )
    return jax.shard_map(
        per_device,
        mesh=mesh,
        in_specs=placed,
        out_specs=(
            P("band", "fft", None, None),
            P("band", "fft", None, None),
            P("fft", "band", None),
        ),
        check_vma=False,
    )
```

profile of v0, /device:TPU:1, one launch (start us, length us, event | category | flops | bytes accessed | tf_op | source)
XLA Modules:
  0.0 1369.0 jit_solution(14072568467195710699)
XLA Ops:
  7.2 13.8 %collective-permute-start.8 = (f32[1,2,64,128]{3,2,1,0:T(8,128)}, f32[1,2,64,128]{3,2,1,0:T(8,128)S(1)}, u32[]{:S(2)}, u32[]{:S(2)}) collective-permute-start(f32[1,2,64,128]{3,2,1,0:T(8,128)} %param.11), channel_id=1, source_target_pairs={{16,0},{32,16},{48,32},{64,48},{80,64},{96,80},{112,96},{128,112},... | collective-permute-start | bytes 196616 | tf_op jit(solution)/shard_map/ppermute | solution.py:25
  25.1 7.5 collective-permute-start.11
  39.2 6.8 all-to-all-start.1
  55.2 6.2 collective-permute-start.13
  72.7 6.1 collective-permute-start.2
  81.9 7.1 collective-permute-start.4
  89.0 90.5 %gather_fusion.1 = f32[16384]{0:T(1024)S(1)} fusion(f32[147456]{0:T(1024)S(1)} %bitcast.451, s32[16384]{0:T(1024)S(1)} %broadcast_clamp_fusion), kind=kCustom, calls=%fused_computation.1 | custom fusion | bytes 196608 | tf_op jit(solution)/shard_map/gather | solution.py:99
  179.6 3.7 collective-permute-start.5
  190.2 90.5 %gather_fusion = f32[16384]{0:T(1024)S(1)} fusion(f32[147456]{0:T(1024)S(1)} %bitcast.448, s32[16384]{0:T(1024)S(1)} %broadcast_clamp_fusion), kind=kCustom, calls=%fused_computation | custom fusion | bytes 196608 | tf_op jit(solution)/shard_map/gather | solution.py:98
  290.1 113.1 %scatter_custom_fusion.1 = f32[147456]{0:T(1024)S(1)} fusion(s32[16384]{0:T(1024)S(1)} %bitcast.477, f32[16384]{0:T(1024)S(1)} %bitcast.518, f32[]{:T(128)} %constant.177.clone.1), kind=kCustom, calls=%fused_computation.66 | custom fusion | flops 16384 | bytes 589828 | tf_op jit(solution)/shard_map/scatter-add | solution.py:120
  406.5 4.2 collective-permute-start.30
  413.6 4.2 collective-permute-start.28
  417.8 6.4 collective-permute-start.27
  424.2 113.1 %scatter_custom_fusion = f32[147456]{0:T(1024)S(1)} fusion(s32[16384]{0:T(1024)S(1)} %bitcast.478, f32[16384]{0:T(1024)S(1)} %bitcast.519, f32[]{:T(128)} %constant.177.clone.1), kind=kCustom, calls=%fused_computation.68 | custom fusion | flops 16384 | bytes 589828 | tf_op jit(solution)/shard_map/scatter-add | solution.py:120
  538.0 5.5 all-to-all-start
  544.2 8.2 all-to-all-done
  555.6 3.9 all-to-all-start.3
  560.8 7.5 all-to-all-done.3
  568.4 3.9 all-to-all-start.2
  572.6 8.5 all-to-all-done.2
  598.0 4.0 collective-permute-start.21
  602.0 7.3 collective-permute-start.20
  612.5 4.2 collective-permute-start.18
  616.7 4.9 collective-permute-start.17
  624.1 6.7 collective-permute-start.40
  636.1 7.5 collective-permute-start.43
  648.7 6.2 all-to-all-start.5
  655.9 6.2 collective-permute-start.45
  673.4 6.3 collective-permute-start.34
  682.9 7.1 collective-permute-start.36
  690.0 90.5 %gather_fusion.3 = f32[16384]{0:T(1024)S(1)} fusion(f32[147456]{0:T(1024)S(1)} %bitcast.450, s32[16384]{0:T(1024)S(1)} %broadcast_clamp_fusion), kind=kCustom, calls=%fused_computation.3 | custom fusion | bytes 196608 | tf_op jit(solution)/shard_map/gather | solution.py:99
  791.2 90.5 %gather_fusion.2 = f32[16384]{0:T(1024)S(1)} fusion(f32[147456]{0:T(1024)S(1)} %bitcast.449, s32[16384]{0:T(1024)S(1)} %broadcast_clamp_fusion), kind=kCustom, calls=%fused_computation.2 | custom fusion | bytes 196608 | tf_op jit(solution)/shard_map/gather | solution.py:98
  891.1 113.1 %scatter_custom_fusion.3 = f32[147456]{0:T(1024)S(1)} fusion(s32[16384]{0:T(1024)S(1)} %bitcast.479, f32[16384]{0:T(1024)S(1)} %bitcast.520, f32[]{:T(128)} %constant.177.clone.1), kind=kCustom, calls=%fused_computation.62 | custom fusion | flops 16384 | bytes 589828 | tf_op jit(solution)/shard_map/scatter-add | solution.py:120
  1007.8 4.5 collective-permute-start.62
  1015.2 4.2 collective-permute-start.60
  1019.3 6.0 collective-permute-start.59
  1025.4 113.1 %scatter_custom_fusion.2 = f32[147456]{0:T(1024)S(1)} fusion(s32[16384]{0:T(1024)S(1)} %bitcast.480, f32[16384]{0:T(1024)S(1)} %bitcast.515, f32[]{:T(128)} %constant.177.clone.1), kind=kCustom, calls=%fused_computation.64 | custom fusion | flops 16384 | bytes 589828 | tf_op jit(solution)/shard_map/scatter-add | solution.py:120
  1138.6 5.0 all-to-all-start.4
  1144.5 7.9 all-to-all-done.4
  1155.6 4.0 all-to-all-start.7
  1161.0 7.5 all-to-all-done.7
  1168.5 3.9 all-to-all-start.6
  1173.6 7.6 all-to-all-done.6
  1198.0 4.0 collective-permute-start.53
  1202.5 7.3 collective-permute-start.52
  1212.4 4.2 collective-permute-start.50
  1216.7 4.9 collective-permute-start.49
  1233.0 127.4 %all-reduce.3.cloned.1.call-done = f32[2,64,128]{2,1,0:T(8,128)} async-done(((f32[2,64,128]{2,1,0:T(8,128)}), f32[2,64,128]{2,1,0:T(8,128)}) %all-reduce.3.cloned.1.call-update) | async-done | bytes 65552
  (294 shorter events, 174.6 us)
Async XLA Ops:
  7.2 48.0 %collective-permute-start.8 = (f32[1,2,64,128]{3,2,1,0:T(8,128)}, f32[1,2,64,128]{3,2,1,0:T(8,128)S(1)}, u32[]{:S(2)}, u32[]{:S(2)}) collective-permute-start(f32[1,2,64,128]{3,2,1,0:T(8,128)} %param.11), channel_id=1, source_target_pairs={{16,0},{32,16},{48,32},{64,48},{80,64},{96,80},{112,96},{128,112},... | collective-permute-start | bytes 196616 | tf_op jit(solution)/shard_map/ppermute | solution.py:25
  21.0 40.4 %collective-permute-start.9 = (f32[1,2,64,128]{3,2,1,0:T(8,128)}, f32[1,2,64,128]{3,2,1,0:T(8,128)S(1)}, u32[]{:S(2)}, u32[]{:S(2)}) collective-permute-start(f32[1,2,64,128]{3,2,1,0:T(8,128)} %param.11), channel_id=1, source_target_pairs={{32,0},{48,16},{64,32},{80,48},{96,64},{112,80},{128,96},{144,112}... | collective-permute-start | bytes 196616 | tf_op jit(solution)/shard_map/ppermute | solution.py:25
  23.2 41.6 %collective-permute-start.10 = (f32[1,2,64,128]{3,2,1,0:T(8,128)}, f32[1,2,64,128]{3,2,1,0:T(8,128)S(1)}, u32[]{:S(2)}, u32[]{:S(2)}) collective-permute-start(f32[1,2,64,128]{3,2,1,0:T(8,128)} %param.11), channel_id=1, source_target_pairs={{48,0},{64,16},{80,32},{96,48},{112,64},{128,80},{144,96},{160,112... | collective-permute-start | bytes 196616 | tf_op jit(solution)/shard_map/ppermute | solution.py:25
  25.1 41.9 %collective-permute-start.11 = (f32[1,2,64,128]{3,2,1,0:T(8,128)}, f32[1,2,64,128]{3,2,1,0:T(8,128)S(1)}, u32[]{:S(2)}, u32[]{:S(2)}) collective-permute-start(f32[1,2,64,128]{3,2,1,0:T(8,128)} %param.11), channel_id=1, source_target_pairs={{64,0},{80,16},{96,32},{112,48},{128,64},{144,80},{160,96},{176,11... | collective-permute-start | bytes 196616 | tf_op jit(solution)/shard_map/ppermute | solution.py:25
  32.7 37.8 %collective-permute-start.12 = (f32[1,2,64,128]{3,2,1,0:T(8,128)}, f32[1,2,64,128]{3,2,1,0:T(8,128)S(1)}, u32[]{:S(2)}, u32[]{:S(2)}) collective-permute-start(f32[1,2,64,128]{3,2,1,0:T(8,128)} %param.11), channel_id=1, source_target_pairs={{80,0},{96,16},{112,32},{128,48},{144,64},{160,80},{176,96},{192,1... | collective-permute-start | bytes 196616 | tf_op jit(solution)/shard_map/ppermute | solution.py:25
  39.2 498.8 %all-to-all-start.1 = ((f32[1,2,64,128]{3,1,0,2:T(2,128)}), f32[1,2,64,128]{3,1,0,2:T(2,128)S(1)}, u32[]{:S(2)}, u32[]{:S(2)}) async-start(f32[1,2,64,128]{3,1,0,2:T(2,128)} %copy.34), calls=%async_computation.1 | async-start | bytes 131072 | tf_op jit(solution)/shard_map/all_to_all | solution.py:173
  67.0 112.6 %collective-permute-start = (f32[1,2,64,128]{3,2,1,0:T(8,128)S(1)}, f32[1,2,64,128]{3,2,1,0:T(8,128)S(1)}, u32[]{:S(2)}, u32[]{:S(2)}) collective-permute-start(f32[1,2,64,128]{3,2,1,0:T(8,128)S(1)} %copy-done.3), channel_id=1, source_target_pairs={{16,0},{32,16},{48,32},{64,48},{80,64},{96,80},{112,96},{128,112},... | collective-permute-start | bytes 196616 | tf_op jit(solution)/shard_map/ppermute | solution.py:25
  70.4 112.8 %collective-permute-start.1 = (f32[1,2,64,128]{3,2,1,0:T(8,128)S(1)}, f32[1,2,64,128]{3,2,1,0:T(8,128)S(1)}, u32[]{:S(2)}, u32[]{:S(2)}) collective-permute-start(f32[1,2,64,128]{3,2,1,0:T(8,128)S(1)} %copy-done.3), channel_id=1, source_target_pairs={{32,0},{48,16},{64,32},{80,48},{96,64},{112,80},{128,96},{144,112}... | collective-permute-start | bytes 196616 | tf_op jit(solution)/shard_map/ppermute | solution.py:25
  72.7 112.6 %collective-permute-start.2 = (f32[1,2,64,128]{3,2,1,0:T(8,128)S(1)}, f32[1,2,64,128]{3,2,1,0:T(8,128)S(1)}, u32[]{:S(2)}, u32[]{:S(2)}) collective-permute-start(f32[1,2,64,128]{3,2,1,0:T(8,128)S(1)} %copy-done.3), channel_id=1, source_target_pairs={{48,0},{64,16},{80,32},{96,48},{112,64},{128,80},{144,96},{160,112... | collective-permute-start | bytes 196616 | tf_op jit(solution)/shard_map/ppermute | solution.py:25
  78.8 108.6 %collective-permute-start.3 = (f32[1,2,64,128]{3,2,1,0:T(8,128)S(1)}, f32[1,2,64,128]{3,2,1,0:T(8,128)S(1)}, u32[]{:S(2)}, u32[]{:S(2)}) collective-permute-start(f32[1,2,64,128]{3,2,1,0:T(8,128)S(1)} %copy-done.3), channel_id=1, source_target_pairs={{64,0},{80,16},{96,32},{112,48},{128,64},{144,80},{160,96},{176,11... | collective-permute-start | bytes 196616 | tf_op jit(solution)/shard_map/ppermute | solution.py:25
  81.9 105.5 %collective-permute-start.4 = (f32[1,2,64,128]{3,2,1,0:T(8,128)S(1)}, f32[1,2,64,128]{3,2,1,0:T(8,128)S(1)}, u32[]{:S(2)}, u32[]{:S(2)}) collective-permute-start(f32[1,2,64,128]{3,2,1,0:T(8,128)S(1)} %copy-done.3), channel_id=1, source_target_pairs={{80,0},{96,16},{112,32},{128,48},{144,64},{160,80},{176,96},{192,1... | collective-permute-start | bytes 196616 | tf_op jit(solution)/shard_map/ppermute | solution.py:25
  403.3 179.7 %collective-permute-start.31 = (f32[1,2,64,128]{3,2,1,0:T(8,128)S(1)}, f32[1,2,64,128]{3,2,1,0:T(8,128)S(1)}, u32[]{:S(2)}, u32[]{:S(2)}) collective-permute-start(f32[1,2,64,128]{3,2,1,0:T(8,128)S(1)} %get-tuple-element.35), channel_id=1, source_target_pairs={{384,0},{400,16},{416,32},{432,48},{448,64},{464,80},{480,96},{496... | collective-permute-start | bytes 196616 | tf_op jit(solution)/shard_map/ppermute | solution.py:25
  406.5 179.1 %collective-permute-start.30 = (f32[1,2,64,128]{3,2,1,0:T(8,128)S(1)}, f32[1,2,64,128]{3,2,1,0:T(8,128)S(1)}, u32[]{:S(2)}, u32[]{:S(2)}) collective-permute-start(f32[1,2,64,128]{3,2,1,0:T(8,128)S(1)} %get-tuple-element.36), channel_id=1, source_target_pairs={{400,0},{416,16},{432,32},{448,48},{464,64},{480,80},{496,96},{0,1... | collective-permute-start | bytes 196616 | tf_op jit(solution)/shard_map/ppermute | solution.py:25
  410.7 177.9 %collective-permute-start.29 = (f32[1,2,64,128]{3,2,1,0:T(8,128)S(1)}, f32[1,2,64,128]{3,2,1,0:T(8,128)S(1)}, u32[]{:S(2)}, u32[]{:S(2)}) collective-permute-start(f32[1,2,64,128]{3,2,1,0:T(8,128)S(1)} %get-tuple-element.37), channel_id=1, source_target_pairs={{416,0},{432,16},{448,32},{464,48},{480,64},{496,80},{0,96},{16,11... | collective-permute-start | bytes 196616 | tf_op jit(solution)/shard_map/ppermute | solution.py:25
  413.6 178.8 %collective-permute-start.28 = (f32[1,2,64,128]{3,2,1,0:T(8,128)S(1)}, f32[1,2,64,128]{3,2,1,0:T(8,128)S(1)}, u32[]{:S(2)}, u32[]{:S(2)}) collective-permute-start(f32[1,2,64,128]{3,2,1,0:T(8,128)S(1)} %get-tuple-element.38), channel_id=1, source_target_pairs={{432,0},{448,16},{464,32},{480,48},{496,64},{0,80},{16,96},{32,112... | collective-permute-start | bytes 196616 | tf_op jit(solution)/shard_map/ppermute | solution.py:25
  417.8 176.9 %collective-permute-start.27 = (f32[1,2,64,128]{3,2,1,0:T(8,128)S(1)}, f32[1,2,64,128]{3,2,1,0:T(8,128)S(1)}, u32[]{:S(2)}, u32[]{:S(2)}) collective-permute-start(f32[1,2,64,128]{3,2,1,0:T(8,128)S(1)} %get-tuple-element.39), channel_id=1, source_target_pairs={{448,0},{464,16},{480,32},{496,48},{0,64},{16,80},{32,96},{48,112}... | collective-permute-start | bytes 196616 | tf_op jit(solution)/shard_map/ppermute | solution.py:25
  588.6 20.7 %collective-permute-start.24 = (f32[1,2,64,128]{3,2,1,0:T(8,128)S(1)}, f32[1,2,64,128]{3,2,1,0:T(8,128)S(1)}, u32[]{:S(2)}, u32[]{:S(2)}) collective-permute-start(f32[1,2,64,128]{3,2,1,0:T(8,128)S(1)} %get-tuple-element.34), channel_id=1, source_target_pairs={{496,0},{0,16},{16,32},{32,48},{48,64},{64,80},{80,96},{96,112},{1... | collective-permute-start | bytes 196616 | tf_op jit(solution)/shard_map/ppermute | solution.py:25
  592.4 20.0 %collective-permute-start.23 = (f32[1,2,64,128]{3,2,1,0:T(8,128)}, f32[1,2,64,128]{3,2,1,0:T(8,128)S(1)}, u32[]{:S(2)}, u32[]{:S(2)}) collective-permute-start(f32[1,2,64,128]{3,2,1,0:T(8,128)} %get-tuple-element.27), channel_id=1, source_target_pairs={{384,0},{400,16},{416,32},{432,48},{448,64},{464,80},{480,96},{496... | collective-permute-start | bytes 196616 | tf_op jit(solution)/shard_map/ppermute | solution.py:25
  594.7 22.0 %collective-permute-start.22 = (f32[1,2,64,128]{3,2,1,0:T(8,128)}, f32[1,2,64,128]{3,2,1,0:T(8,128)S(1)}, u32[]{:S(2)}, u32[]{:S(2)}) collective-permute-start(f32[1,2,64,128]{3,2,1,0:T(8,128)} %get-tuple-element.28), channel_id=1, source_target_pairs={{400,0},{416,16},{432,32},{448,48},{464,64},{480,80},{496,96},{0,1... | collective-permute-start | bytes 196616 | tf_op jit(solution)/shard_map/ppermute | solution.py:25
  598.0 23.6 %collective-permute-start.21 = (f32[1,2,64,128]{3,2,1,0:T(8,128)S(1)}, f32[1,2,64,128]{3,2,1,0:T(8,128)S(1)}, u32[]{:S(2)}, u32[]{:S(2)}) collective-permute-start(f32[1,2,64,128]{3,2,1,0:T(8,128)S(1)} %get-tuple-element.29), channel_id=1, source_target_pairs={{416,0},{432,16},{448,32},{464,48},{480,64},{496,80},{0,96},{16,11... | collective-permute-start | bytes 196616 | tf_op jit(solution)/shard_map/ppermute | solution.py:25
  602.0 22.1 %collective-permute-start.20 = (f32[1,2,64,128]{3,2,1,0:T(8,128)S(1)}, f32[1,2,64,128]{3,2,1,0:T(8,128)S(1)}, u32[]{:S(2)}, u32[]{:S(2)}) collective-permute-start(f32[1,2,64,128]{3,2,1,0:T(8,128)S(1)} %get-tuple-element.30), channel_id=1, source_target_pairs={{432,0},{448,16},{464,32},{480,48},{496,64},{0,80},{16,96},{32,112... | collective-permute-start | bytes 196616 | tf_op jit(solution)/shard_map/ppermute | solution.py:25
  609.3 21.4 %collective-permute-start.19 = (f32[1,2,64,128]{3,2,1,0:T(8,128)S(1)}, f32[1,2,64,128]{3,2,1,0:T(8,128)S(1)}, u32[]{:S(2)}, u32[]{:S(2)}) collective-permute-start(f32[1,2,64,128]{3,2,1,0:T(8,128)S(1)} %get-tuple-element.31), channel_id=1, source_target_pairs={{448,0},{464,16},{480,32},{496,48},{0,64},{16,80},{32,96},{48,112}... | collective-permute-start | bytes 196616 | tf_op jit(solution)/shard_map/ppermute | solution.py:25
  612.5 20.8 %collective-permute-start.18 = (f32[1,2,64,128]{3,2,1,0:T(8,128)S(1)}, f32[1,2,64,128]{3,2,1,0:T(8,128)S(1)}, u32[]{:S(2)}, u32[]{:S(2)}) collective-permute-start(f32[1,2,64,128]{3,2,1,0:T(8,128)S(1)} %get-tuple-element.32), channel_id=1, source_target_pairs={{464,0},{480,16},{496,32},{0,48},{16,64},{32,80},{48,96},{64,112},... | collective-permute-start | bytes 196616 | tf_op jit(solution)/shard_map/ppermute | solution.py:25
  616.7 19.4 %collective-permute-start.17 = (f32[1,2,64,128]{3,2,1,0:T(8,128)S(1)}, f32[1,2,64,128]{3,2,1,0:T(8,128)S(1)}, u32[]{:S(2)}, u32[]{:S(2)}) collective-permute-start(f32[1,2,64,128]{3,2,1,0:T(8,128)S(1)} %get-tuple-element.33), channel_id=1, source_target_pairs={{480,0},{496,16},{0,32},{16,48},{32,64},{48,80},{64,96},{80,112},{... | collective-permute-start | bytes 196616 | tf_op jit(solution)/shard_map/ppermute | solution.py:25
  621.7 22.0 %collective-permute-start.16 = (f32[1,2,64,128]{3,2,1,0:T(8,128)S(1)}, f32[1,2,64,128]{3,2,1,0:T(8,128)S(1)}, u32[]{:S(2)}, u32[]{:S(2)}) collective-permute-start(f32[1,2,64,128]{3,2,1,0:T(8,128)S(1)} %get-tuple-element.26), channel_id=1, source_target_pairs={{496,0},{0,16},{16,32},{32,48},{48,64},{64,80},{80,96},{96,112},{1... | collective-permute-start | bytes 196616 | tf_op jit(solution)/shard_map/ppermute | solution.py:25
  624.1 31.8 %collective-permute-start.40 = (f32[1,2,64,128]{3,2,1,0:T(8,128)S(1)}, f32[1,2,64,128]{3,2,1,0:T(8,128)S(1)}, u32[]{:S(2)}, u32[]{:S(2)}) collective-permute-start(f32[1,2,64,128]{3,2,1,0:T(8,128)S(1)} %get-tuple-element.9), channel_id=1, source_target_pairs={{16,0},{32,16},{48,32},{64,48},{80,64},{96,80},{112,96},{128,112},... | collective-permute-start | bytes 196616 | tf_op jit(solution)/shard_map/ppermute | solution.py:25
  630.8 31.4 %collective-permute-start.41 = (f32[1,2,64,128]{3,2,1,0:T(8,128)S(1)}, f32[1,2,64,128]{3,2,1,0:T(8,128)S(1)}, u32[]{:S(2)}, u32[]{:S(2)}) collective-permute-start(f32[1,2,64,128]{3,2,1,0:T(8,128)S(1)} %get-tuple-element.9), channel_id=1, source_target_pairs={{32,0},{48,16},{64,32},{80,48},{96,64},{112,80},{128,96},{144,112}... | collective-permute-start | bytes 196616 | tf_op jit(solution)/shard_map/ppermute | solution.py:25
  633.3 32.2 %collective-permute-start.42 = (f32[1,2,64,128]{3,2,1,0:T(8,128)S(1)}, f32[1,2,64,128]{3,2,1,0:T(8,128)S(1)}, u32[]{:S(2)}, u32[]{:S(2)}) collective-permute-start(f32[1,2,64,128]{3,2,1,0:T(8,128)S(1)} %get-tuple-element.9), channel_id=1, source_target_pairs={{48,0},{64,16},{80,32},{96,48},{112,64},{128,80},{144,96},{160,112... | collective-permute-start | bytes 196616 | tf_op jit(solution)/shard_map/ppermute | solution.py:25
  636.1 31.6 %collective-permute-start.43 = (f32[1,2,64,128]{3,2,1,0:T(8,128)S(1)}, f32[1,2,64,128]{3,2,1,0:T(8,128)S(1)}, u32[]{:S(2)}, u32[]{:S(2)}) collective-permute-start(f32[1,2,64,128]{3,2,1,0:T(8,128)S(1)} %get-tuple-element.9), channel_id=1, source_target_pairs={{64,0},{80,16},{96,32},{112,48},{128,64},{144,80},{160,96},{176,11... | collective-permute-start | bytes 196616 | tf_op jit(solution)/shard_map/ppermute | solution.py:25
  643.7 27.5 %collective-permute-start.44 = (f32[1,2,64,128]{3,2,1,0:T(8,128)S(1)}, f32[1,2,64,128]{3,2,1,0:T(8,128)S(1)}, u32[]{:S(2)}, u32[]{:S(2)}) collective-permute-start(f32[1,2,64,128]{3,2,1,0:T(8,128)S(1)} %get-tuple-element.9), channel_id=1, source_target_pairs={{80,0},{96,16},{112,32},{128,48},{144,64},{160,80},{176,96},{192,1... | collective-permute-start | bytes 196616 | tf_op jit(solution)/shard_map/ppermute | solution.py:25
  648.7 489.8 %all-to-all-start.5 = ((f32[1,2,64,128]{3,1,0,2:T(2,128)}), f32[1,2,64,128]{3,1,0,2:T(2,128)S(1)}, u32[]{:S(2)}, u32[]{:S(2)}) async-start(f32[1,2,64,128]{3,1,0,2:T(2,128)} %copy.44), calls=%async_computation.5 | async-start | bytes 131072 | tf_op jit(solution)/shard_map/all_to_all | solution.py:173
  662.2 17.6 %collective-permute-start.46 = (f32[1,2,64,128]{3,2,1,0:T(8,128)S(1)}, f32[1,2,64,128]{3,2,1,0:T(8,128)S(1)}, u32[]{:S(2)}, u32[]{:S(2)}) collective-permute-start(f32[1,2,64,128]{3,2,1,0:T(8,128)S(1)} %get-tuple-element.9), channel_id=1, source_target_pairs={{112,0},{128,16},{144,32},{160,48},{176,64},{192,80},{208,96},{224... | collective-permute-start | bytes 196616 | tf_op jit(solution)/shard_map/ppermute | solution.py:25
  667.7 112.8 %collective-permute-start.32 = (f32[1,2,64,128]{3,2,1,0:T(8,128)S(1)}, f32[1,2,64,128]{3,2,1,0:T(8,128)S(1)}, u32[]{:S(2)}, u32[]{:S(2)}) collective-permute-start(f32[1,2,64,128]{3,2,1,0:T(8,128)S(1)} %get-tuple-element.7), channel_id=1, source_target_pairs={{16,0},{32,16},{48,32},{64,48},{80,64},{96,80},{112,96},{128,112},... | collective-permute-start | bytes 196616 | tf_op jit(solution)/shard_map/ppermute | solution.py:25
  671.2 113.1 %collective-permute-start.33 = (f32[1,2,64,128]{3,2,1,0:T(8,128)S(1)}, f32[1,2,64,128]{3,2,1,0:T(8,128)S(1)}, u32[]{:S(2)}, u32[]{:S(2)}) collective-permute-start(f32[1,2,64,128]{3,2,1,0:T(8,128)S(1)} %get-tuple-element.7), channel_id=1, source_target_pairs={{32,0},{48,16},{64,32},{80,48},{96,64},{112,80},{128,96},{144,112}... | collective-permute-start | bytes 196616 | tf_op jit(solution)/shard_map/ppermute | solution.py:25
  673.4 112.8 %collective-permute-start.34 = (f32[1,2,64,128]{3,2,1,0:T(8,128)S(1)}, f32[1,2,64,128]{3,2,1,0:T(8,128)S(1)}, u32[]{:S(2)}, u32[]{:S(2)}) collective-permute-start(f32[1,2,64,128]{3,2,1,0:T(8,128)S(1)} %get-tuple-element.7), channel_id=1, source_target_pairs={{48,0},{64,16},{80,32},{96,48},{112,64},{128,80},{144,96},{160,112... | collective-permute-start | bytes 196616 | tf_op jit(solution)/shard_map/ppermute | solution.py:25
  679.7 108.6 %collective-permute-start.35 = (f32[1,2,64,128]{3,2,1,0:T(8,128)S(1)}, f32[1,2,64,128]{3,2,1,0:T(8,128)S(1)}, u32[]{:S(2)}, u32[]{:S(2)}) collective-permute-start(f32[1,2,64,128]{3,2,1,0:T(8,128)S(1)} %get-tuple-element.7), channel_id=1, source_target_pairs={{64,0},{80,16},{96,32},{112,48},{128,64},{144,80},{160,96},{176,11... | collective-permute-start | bytes 196616 | tf_op jit(solution)/shard_map/ppermute | solution.py:25
  682.9 105.5 %collective-permute-start.36 = (f32[1,2,64,128]{3,2,1,0:T(8,128)S(1)}, f32[1,2,64,128]{3,2,1,0:T(8,128)S(1)}, u32[]{:S(2)}, u32[]{:S(2)}) collective-permute-start(f32[1,2,64,128]{3,2,1,0:T(8,128)S(1)} %get-tuple-element.7), channel_id=1, source_target_pairs={{80,0},{96,16},{112,32},{128,48},{144,64},{160,80},{176,96},{192,1... | collective-permute-start | bytes 196616 | tf_op jit(solution)/shard_map/ppermute | solution.py:25
  1004.9 178.3 %collective-permute-start.63 = (f32[1,2,64,128]{3,2,1,0:T(8,128)}, f32[1,2,64,128]{3,2,1,0:T(8,128)S(1)}, u32[]{:S(2)}, u32[]{:S(2)}) collective-permute-start(f32[1,2,64,128]{3,2,1,0:T(8,128)} %get-tuple-element.19), channel_id=1, source_target_pairs={{384,0},{400,16},{416,32},{432,48},{448,64},{464,80},{480,96},{496... | collective-permute-start | bytes 196616 | tf_op jit(solution)/shard_map/ppermute | solution.py:25
  1007.8 178.4 %collective-permute-start.62 = (f32[1,2,64,128]{3,2,1,0:T(8,128)S(1)}, f32[1,2,64,128]{3,2,1,0:T(8,128)S(1)}, u32[]{:S(2)}, u32[]{:S(2)}) collective-permute-start(f32[1,2,64,128]{3,2,1,0:T(8,128)S(1)} %get-tuple-element.20), channel_id=1, source_target_pairs={{400,0},{416,16},{432,32},{448,48},{464,64},{480,80},{496,96},{0,1... | collective-permute-start | bytes 196616 | tf_op jit(solution)/shard_map/ppermute | solution.py:25
  1012.2 176.9 %collective-permute-start.61 = (f32[1,2,64,128]{3,2,1,0:T(8,128)S(1)}, f32[1,2,64,128]{3,2,1,0:T(8,128)S(1)}, u32[]{:S(2)}, u32[]{:S(2)}) collective-permute-start(f32[1,2,64,128]{3,2,1,0:T(8,128)S(1)} %get-tuple-element.21), channel_id=1, source_target_pairs={{416,0},{432,16},{448,32},{464,48},{480,64},{496,80},{0,96},{16,11... | collective-permute-start | bytes 196616 | tf_op jit(solution)/shard_map/ppermute | solution.py:25
  1015.2 177.3 %collective-permute-start.60 = (f32[1,2,64,128]{3,2,1,0:T(8,128)S(1)}, f32[1,2,64,128]{3,2,1,0:T(8,128)S(1)}, u32[]{:S(2)}, u32[]{:S(2)}) collective-permute-start(f32[1,2,64,128]{3,2,1,0:T(8,128)S(1)} %get-tuple-element.22), channel_id=1, source_target_pairs={{432,0},{448,16},{464,32},{480,48},{496,64},{0,80},{16,96},{32,112... | collective-permute-start | bytes 196616 | tf_op jit(solution)/shard_map/ppermute | solution.py:25
  1019.3 175.4 %collective-permute-start.59 = (f32[1,2,64,128]{3,2,1,0:T(8,128)S(1)}, f32[1,2,64,128]{3,2,1,0:T(8,128)S(1)}, u32[]{:S(2)}, u32[]{:S(2)}) collective-permute-start(f32[1,2,64,128]{3,2,1,0:T(8,128)S(1)} %get-tuple-element.23), channel_id=1, source_target_pairs={{448,0},{464,16},{480,32},{496,48},{0,64},{16,80},{32,96},{48,112}... | collective-permute-start | bytes 196616 | tf_op jit(solution)/shard_map/ppermute | solution.py:25
  1172.3 188.1 %all-reduce.3.cloned.1.call-start = ((), (), s32[]{:S(2)}) async-start(), calls=%async_computation.8 | async-start | bytes 131072
  1189.2 20.6 %collective-permute-start.56 = (f32[1,2,64,128]{3,2,1,0:T(8,128)S(1)}, f32[1,2,64,128]{3,2,1,0:T(8,128)S(1)}, u32[]{:S(2)}, u32[]{:S(2)}) collective-permute-start(f32[1,2,64,128]{3,2,1,0:T(8,128)S(1)} %get-tuple-element.18), channel_id=1, source_target_pairs={{496,0},{0,16},{16,32},{32,48},{48,64},{64,80},{80,96},{96,112},{1... | collective-permute-start | bytes 196616 | tf_op jit(solution)/shard_map/ppermute | solution.py:25
  1192.4 19.9 %collective-permute-start.55 = (f32[1,2,64,128]{3,2,1,0:T(8,128)S(1)}, f32[1,2,64,128]{3,2,1,0:T(8,128)S(1)}, u32[]{:S(2)}, u32[]{:S(2)}) collective-permute-start(f32[1,2,64,128]{3,2,1,0:T(8,128)S(1)} %get-tuple-element.11), channel_id=1, source_target_pairs={{384,0},{400,16},{416,32},{432,48},{448,64},{464,80},{480,96},{496... | collective-permute-start | bytes 196616 | tf_op jit(solution)/shard_map/ppermute | solution.py:25
  1194.7 21.9 %collective-permute-start.54 = (f32[1,2,64,128]{3,2,1,0:T(8,128)S(1)}, f32[1,2,64,128]{3,2,1,0:T(8,128)S(1)}, u32[]{:S(2)}, u32[]{:S(2)}) collective-permute-start(f32[1,2,64,128]{3,2,1,0:T(8,128)S(1)} %get-tuple-element.12), channel_id=1, source_target_pairs={{400,0},{416,16},{432,32},{448,48},{464,64},{480,80},{496,96},{0,1... | collective-permute-start | bytes 196616 | tf_op jit(solution)/shard_map/ppermute | solution.py:25
  1198.0 23.6 %collective-permute-start.53 = (f32[1,2,64,128]{3,2,1,0:T(8,128)S(1)}, f32[1,2,64,128]{3,2,1,0:T(8,128)S(1)}, u32[]{:S(2)}, u32[]{:S(2)}) collective-permute-start(f32[1,2,64,128]{3,2,1,0:T(8,128)S(1)} %get-tuple-element.13), channel_id=1, source_target_pairs={{416,0},{432,16},{448,32},{464,48},{480,64},{496,80},{0,96},{16,11... | collective-permute-start | bytes 196616 | tf_op jit(solution)/shard_map/ppermute | solution.py:25
  1202.5 21.5 %collective-permute-start.52 = (f32[1,2,64,128]{3,2,1,0:T(8,128)S(1)}, f32[1,2,64,128]{3,2,1,0:T(8,128)S(1)}, u32[]{:S(2)}, u32[]{:S(2)}) collective-permute-start(f32[1,2,64,128]{3,2,1,0:T(8,128)S(1)} %get-tuple-element.14), channel_id=1, source_target_pairs={{432,0},{448,16},{464,32},{480,48},{496,64},{0,80},{16,96},{32,112... | collective-permute-start | bytes 196616 | tf_op jit(solution)/shard_map/ppermute | solution.py:25
  (44 other events, 630.8 us)
Sparse Core Ops, SparseCore 0:
  1231.2 129.1 all-reduce.2
where the time goes:
time: 1380 us; the launch traced here: 1370 us
  other arithmetic  468 us (34%)
  local copies, waits for them, and re-layouts  379 us (27%)
  starting transfers between devices  291 us (21%)
  waiting for transfers between devices  186 us (13%)
  matrix products  27.7 us (2%)
  between operations  17.8 us (1%)
    ppermute x64, starting transfers between devices, shifted(): return lax.ppermute(block, axis, route)  252 us
    scatter-add x2, other arithmetic, spread(): zeroed.at[:, flat].add(placed_imag)  226 us
    scatter-add x2, other arithmetic, spread(): zeroed.at[:, flat].add(placed_real)  226 us
    gather x4, local copies, waits for them, and re-layouts, project(): take_imag = imag_part.reshape(orbs, -1)[:, flat] * valid  181 us
    gather x4, local copies, waits for them, and re-layouts, project(): take_real = real_part.reshape(orbs, -1)[:, flat] * valid  181 us
    unnamed x2, waiting for transfers between devices  127 us
  transfers between devices with their start and end apart: 73, of which 14 were waited for; matrix products, arithmetic and copies ran while one was open for 63% of the time, Pallas kernels for 0%

commit v1 on v0

v1 whole, which is shorter than its diff:
```python
import functools
import math

import jax
import jax.numpy as jnp
import numpy as np
from jax import lax
from jax.experimental import pallas as pl
from jax.experimental.pallas import tpu as pltpu
from jax.sharding import PartitionSpec as P

NX = 64
NY = 64
NZ = 128
BOX = 16
NPROJ = 8
SLABS = 32
BANDS = 16
REACH = 9
KINDS = 4
LANES = 128
IMAG = 64

time_step = 0.01
kinetic_scale = 0.5 * (2.0 * math.pi / 38.0) ** 2
highest = lax.Precision.HIGHEST
f32 = jnp.float32
i32 = jnp.int32


def circulant(length):
    modes = np.arange(length)
    modes = np.where(modes < length // 2, modes, modes - length).astype(np.float64)
    steps = np.arange(length)
    wave = np.exp(2j * np.pi * np.outer(steps, modes) / length) / length
    apart = (steps[:, None] - steps[None, :]) % length
    return (wave @ modes**2)[apart] * kinetic_scale, (wave @ modes)[apart] * 2.0 * kinetic_scale


def blocks(matrix):
    return np.array([[matrix.real, -matrix.imag], [matrix.imag, matrix.real]])


def along_x(matrix):
    whole = blocks(matrix).reshape(2, 2, SLABS, 2, SLABS, 2)
    out = np.einsum("cdipjq,yz->iycpjzdq", whole, np.eye(2))
    return out.reshape(256, 256).astype(np.float32)


def along_y(matrix):
    out = np.einsum("cdyz,pq->cpydqz", blocks(matrix), np.eye(2))
    return out.reshape(256, 256).astype(np.float32)


def along_z(matrix):
    return np.einsum("cdyz->dzcy", blocks(matrix)).reshape(256, 256).astype(np.float32)


def tables():
    x2, x1 = circulant(NX)
    y2, y1 = circulant(NY)
    z2, z1 = circulant(NZ)
    return (
        np.stack([along_x(x2), along_x(x1)]),
        np.stack([along_y(y2), along_y(y1)]),
        np.stack([along_z(z2), along_z(z1)]),
    )


def halves(value):
    high = value.astype(jnp.bfloat16)
    low = (value - high.astype(f32)).astype(jnp.bfloat16)
    return high, low


def dot3(left, right):
    left_high, left_low = halves(left)
    right_high, right_low = halves(right)
    dot = functools.partial(jnp.dot, preferred_element_type=f32)
    return dot(left_high, right_high) + (dot(left_high, right_low) + dot(left_low, right_high))


def group_matrix():
    row = lax.broadcasted_iota(i32, (NPROJ, LANES), 0)
    lane = lax.broadcasted_iota(i32, (NPROJ, LANES), 1)
    return (lane // BOX == row).astype(f32)


def kinetic_x(field, table_ref, shift):
    moved = dot3(table_ref[0] + shift * table_ref[1], field)
    return moved + (kinetic_scale * shift * shift) * field


def kinetic_yz(field, y_ref, z_ref, shift_y, shift_z):
    along = dot3(y_ref[0] + shift_y * y_ref[1], field)
    wide = jnp.concatenate([field[:128], field[128:]], axis=1)
    across = dot3(wide, z_ref[0] + shift_z * z_ref[1])
    across = jnp.concatenate([across[:, :128], across[:, 128:]], axis=0)
    constant = kinetic_scale * (shift_y * shift_y + shift_z * shift_z)
    return along + across + constant * field


def pack_body(index_ref, boxes_ref, species_ref, channels_ref, real_ref, imag_ref, proj_ref, out_ref, rows_ref):
    slab = index_ref[0]
    band = index_ref[1]
    out_ref[...] = jnp.zeros_like(out_ref)
    rows_ref[...] = jnp.zeros_like(rows_ref)
    for y in range(2):
        for part, ref in enumerate((real_ref, imag_ref)):
            for plane in range(2):
                row = y * 4 + part * 2 + plane
                out_ref[pl.ds(row, SLABS, stride=24), :] = ref[pl.ds(plane * NY + y, SLABS, stride=2), :]
    sub = lax.broadcasted_iota(i32, (NPROJ, LANES), 0)
    lane = lax.broadcasted_iota(i32, (NPROJ, LANES), 1)
    own = lane // BOX == sub
    pick = (band % 8) * BOX + lane % BOX
    for atom in range(4):
        for cut in range(BOX):
            start = pl.multiple_of((2 * cut + band // 8) * LANES, LANES)
            tile = proj_ref[atom, :, pl.ds(start, LANES)]
            tile = jnp.take_along_axis(tile, pick, axis=1)
            line = jnp.sum(jnp.where(own, tile, 0.0), axis=0, keepdims=True)
            rows_ref[pl.ds(atom * 24 + 1 + cut, 1), :] = line
    facts = jnp.zeros((NPROJ, LANES), f32)
    for atom in range(4):
        for channel in range(NPROJ):
            here = (sub == channel) & (lane == atom)
            facts = jnp.where(here, channels_ref[atom, channel].astype(f32), facts)
        facts = jnp.where(lane == 4 + atom, species_ref[atom].astype(f32), facts)
        facts = jnp.where(lane == 8 + atom, boxes_ref[1, atom].astype(f32), facts)
        facts = jnp.where(lane == 12 + atom, boxes_ref[2, atom].astype(f32), facts)
    for distance in range(REACH):
        target = (slab + distance) % SLABS
        for atom in range(4):
            start = 2 * distance + 1 - boxes_ref[0, atom] % 2
            out_ref[pl.ds(target * 24 + 8 + 2 * atom, 2), :] = rows_ref[pl.ds(atom * 24 + start, 2), :]
        out_ref[pl.ds(pl.multiple_of(target * 24 + 16, 8), 8), :] = facts


def pick_body(index_ref, got_ref, coupling_ref, proj_ref, table_ref, boxes_ref):
    slab = index_ref[0]
    lane = lax.broadcasted_iota(i32, (NPROJ, LANES), 1)
    zero = jnp.zeros((NPROJ, LANES), f32)
    gates, kind, first_y, first_z = zero, zero, zero, zero
    for distance in range(REACH):
        source = (slab + SLABS - distance) % SLABS
        proj_ref[pl.ds(distance * 8, 8), :] = got_ref[pl.ds(pl.multiple_of(source * 24 + 8, 8), 8), :]
        facts = got_ref[pl.ds(pl.multiple_of(source * 24 + 16, 8), 8), :]
        here = lane // 4 == distance

        def moved(offset):
            return jnp.where(here, pltpu.roll(facts, (4 * distance - offset) % LANES, 1), 0.0)

        gates += moved(0)
        kind += moved(4)
        first_y += moved(8)
        first_z += moved(12)
    gates += pltpu.roll(gates, IMAG, 1)
    kind += pltpu.roll(kind, IMAG, 1)
    for other in range(NPROJ):
        value = zero
        for which in range(KINDS):
            column = coupling_ref[which][:, other : other + 1]
            value = jnp.where(kind == float(which), column, value)
        table_ref[pl.ds(other * 8, 8), :] = value * gates * gates[other : other + 1, :]
    sub = lax.broadcasted_iota(i32, (NPROJ, LANES), 0)
    boxes_ref[...] = jnp.where(sub == 0, first_y, first_z).astype(i32)


def local_body(index_ref, vector_ref, real_ref, imag_ref, pot_ref, y_ref, z_ref, out_ref, turn_ref):
    slab = index_ref[0]
    field = jnp.concatenate([real_ref[...], imag_ref[...]], axis=0)
    out = kinetic_yz(field, y_ref, z_ref, vector_ref[1], vector_ref[2])
    pot = pot_ref[...]
    out_ref[...] = out + jnp.concatenate([pot, pot], axis=0) * field
    row = lax.broadcasted_iota(i32, (128, LANES), 0)
    x = (slab * 2 + row // NY).astype(f32)
    y = (row % NY).astype(f32)
    z = lax.broadcasted_iota(i32, (128, LANES), 1).astype(f32)
    turns = vector_ref[0] * x / NX + vector_ref[1] * y / NY + vector_ref[2] * z / NZ
    turns = turns - jnp.floor(turns + 0.5)
    theta = (2.0 * math.pi) * turns
    turn_ref[0] = jnp.cos(theta)
    turn_ref[1] = jnp.sin(theta)


def columns_body(width, vector_ref, got_ref, x_ref, out_ref):
    field = got_ref[:, 0:8, :].reshape(256, LANES)
    out_ref[...] = kinetic_x(field, x_ref, vector_ref[0])


def project(boxes_ref, proj_ref, real, imag, turn_ref, field_ref, sums_ref):
    cosine, sine = turn_ref[0], turn_ref[1]
    turned = (cosine * real - sine * imag, sine * real + cosine * imag)
    for part in range(2):
        for plane in range(2):
            base = (part * 2 + plane) * 80
            field_ref[pl.ds(base, 64), :] = turned[part][plane * 64 : plane * 64 + 64]
            field_ref[pl.ds(base + 64, 16), :] = turned[part][plane * 64 : plane * 64 + 16]
    sums_ref[...] = jnp.zeros_like(sums_ref)
    lane = lax.broadcasted_iota(i32, (BOX, LANES), 1)

    def one(atom, carry):
        first_y = boxes_ref[0, atom]
        first_z = boxes_ref[1, atom]
        pick = (first_z + lane % BOX) % LANES
        total = [None, None]
        for plane in range(2):
            beta = proj_ref[pl.ds(atom * 2 + plane, BOX, stride=72), :]
            for part in range(2):
                rows = field_ref[pl.ds((part * 2 + plane) * 80 + first_y, BOX), :]
                term = beta * jnp.take_along_axis(rows, pick, axis=1)
                total[part] = term if plane == 0 else total[part] + term
        for part in range(2):
            sums_ref[pl.ds(part * IMAG + atom, 1), :] = jnp.sum(total[part], axis=0, keepdims=True)
        return carry

    lax.fori_loop(0, 4 * REACH, one, 0, unroll=4)
    return lax.dot_general(
        group_matrix(), sums_ref[...], (((1,), (1,)), ((), ())), precision=highest, preferred_element_type=f32
    )


def spread(slab, boxes_ref, proj_ref, table_ref, got_ref, width, turn_ref, place_ref, dual_ref):
    lane = lax.broadcasted_iota(i32, (NPROJ, LANES), 1)
    box = (lane % IMAG) // 4
    coef = jnp.zeros((NPROJ, LANES), f32)
    for offset in range(1 - REACH, REACH):
        source = (slab + SLABS + offset) % SLABS
        share = got_ref[source, width - 8 : width, :]
        if offset != 0:
            share = pltpu.roll(share, (-4 * offset) % LANES, 1)
        sent = box + offset
        coef += jnp.where((box < REACH) & (sent >= 0) & (sent < REACH), share, 0.0)
    dual = jnp.zeros((NPROJ, LANES), f32)
    for other in range(NPROJ):
        dual += table_ref[pl.ds(other * 8, 8), :] * coef[other : other + 1, :]
    dual_ref[...] = lax.dot_general(
        dual, group_matrix(), (((0,), (0,)), ((), ())), precision=highest, preferred_element_type=f32
    )
    place_ref[...] = jnp.zeros_like(place_ref)
    wide = lax.broadcasted_iota(i32, (BOX, LANES), 1)

    def one(atom, carry):
        first_y = boxes_ref[0, atom]
        first_z = boxes_ref[1, atom]
        inside = (wide + LANES - first_z) % LANES < BOX
        for plane in range(2):
            beta = proj_ref[pl.ds(atom * 2 + plane, BOX, stride=72), :]
            for part in range(2):
                value = beta * dual_ref[pl.ds(part * IMAG + atom, 1), :]
                value += pltpu.roll(value, 64, 1)
                value += pltpu.roll(value, 32, 1)
                value += pltpu.roll(value, 16, 1)
                value = jnp.where(inside, pltpu.roll(value, first_z, 1), 0.0)
                place_ref[pl.ds((part * 2 + plane) * 80 + first_y, BOX), :] += value
        return carry

    lax.fori_loop(0, 4 * REACH, one, 0, unroll=2)
    for block in range(4):
        place_ref[pl.ds(block * 80, 16), :] += place_ref[pl.ds(block * 80 + 64, 16), :]
    back_real = jnp.concatenate([place_ref[pl.ds(0, 64), :], place_ref[pl.ds(80, 64), :]], axis=0)
    back_imag = jnp.concatenate([place_ref[pl.ds(160, 64), :], place_ref[pl.ds(240, 64), :]], axis=0)
    cosine, sine = turn_ref[0], turn_ref[1]
    return cosine * back_real + sine * back_imag, cosine * back_imag - sine * back_real


def unpack(got_ref, width, field_ref):
    for y in range(2):
        for part in range(2):
            for plane in range(2):
                row = y * 4 + part * 2 + plane
                start = part * 128 + plane * 64 + y
                field_ref[pl.ds(start, SLABS, stride=2), :] = got_ref[:, row, :]


def coef_body(boxes_ref, proj_ref, real_ref, imag_ref, turn_ref, moved_ref, out_ref, field_ref, sums_ref):
    coef = project(boxes_ref, proj_ref, real_ref[...], imag_ref[...], turn_ref, field_ref, sums_ref)
    out_ref[:, 0:8, :] = moved_ref[...].reshape(SLABS, 8, LANES)
    out_ref[:, 8:16, :] = jnp.broadcast_to(coef[None], (SLABS, 8, LANES))


def first_body(
    index_ref, boxes_ref, proj_ref, table_ref, got_ref, turn_ref, local_ref,
    first_ref, out_ref, field_ref, sums_ref, place_ref, dual_ref,
):
    slab = index_ref[0]
    unpack(got_ref, 16, first_ref)
    far_real, far_imag = spread(
        slab, boxes_ref, proj_ref, table_ref, got_ref, 16, turn_ref, place_ref, dual_ref
    )
    real = first_ref[0:128, :] + local_ref[0:128, :] + far_real
    imag = first_ref[128:256, :] + local_ref[128:256, :] + far_imag
    first_ref[0:128, :] = real
    first_ref[128:256, :] = imag
    for y in range(2):
        for part in range(2):
            for plane in range(2):
                row = y * 4 + part * 2 + plane
                start = part * 128 + plane * 64 + y
                out_ref[:, row, :] = first_ref[pl.ds(start, SLABS, stride=2), :]
    coef = project(boxes_ref, proj_ref, real, imag, turn_ref, field_ref, sums_ref)
    out_ref[:, 8:16, :] = jnp.broadcast_to(coef[None], (SLABS, 8, LANES))


def second_body(
    index_ref, vector_ref, boxes_ref, proj_ref, table_ref, got_ref, turn_ref, first_ref, pot_ref, y_ref, z_ref,
    out_ref, place_ref, dual_ref,
):
    slab = index_ref[0]
    field = first_ref[...]
    near = kinetic_yz(field, y_ref, z_ref, vector_ref[1], vector_ref[2])
    far_real, far_imag = spread(
        slab, boxes_ref, proj_ref, table_ref, got_ref, 16, turn_ref, place_ref, dual_ref
    )
    pot = pot_ref[...]
    out_ref[0:128, :] = near[:128] + pot * field[:128] + far_real
    out_ref[128:256, :] = near[128:] + pot * field[128:] + far_imag


def final_body(occupation_ref, real_ref, imag_ref, first_ref, near_ref, got_ref, new_real_ref, new_imag_ref, out_ref, field_ref):
    unpack(got_ref, 8, field_ref)
    half = 0.5 * time_step * time_step
    new_real = real_ref[...] + time_step * first_ref[128:256, :] - half * (near_ref[0:128, :] + field_ref[0:128, :])
    new_imag = imag_ref[...] - time_step * first_ref[0:128, :] - half * (near_ref[128:256, :] + field_ref[128:256, :])
    new_real_ref[...] = new_real
    new_imag_ref[...] = new_imag
    weighted = occupation_ref[0] * (new_real * new_real + new_imag * new_imag)
    weighted = weighted.reshape(2, BANDS, 4, LANES)
    for plane in range(2):
        out_ref[:, pl.ds(plane * 4, 4), :] = weighted[plane]


def smem():
    return pl.BlockSpec(memory_space=pltpu.SMEM)


def vmem():
    return pl.BlockSpec(memory_space=pltpu.VMEM)


def call(body, scalars, arrays, outs, scratch=()):
    several = isinstance(outs, tuple)
    return pl.pallas_call(
        body,
        out_shape=outs,
        in_specs=[smem()] * len(scalars) + [vmem()] * len(arrays),
        out_specs=tuple(vmem() for _ in outs) if several else vmem(),
        scratch_shapes=list(scratch),
        compiler_params=pltpu.CompilerParams(vmem_limit_bytes=24 * 1024 * 1024),
    )(*scalars, *arrays)


def shape(*dims, dtype=f32):
    return jax.ShapeDtypeStruct(dims, dtype)


def exchange(value, axis):
    return lax.all_to_all(value, axis, split_axis=0, concat_axis=0, tiled=True)


def per_device(
    psi_real, psi_imag, potential, vector_potential, occupation, projectors, box_offsets, species, channels, coupling
):
    x_table, y_table, z_table = (jnp.asarray(table) for table in tables())
    index = jnp.stack([lax.axis_index("fft"), lax.axis_index("band")]).astype(i32)
    real = psi_real.reshape(128, LANES)
    imag = psi_imag.reshape(128, LANES)
    pot = potential.reshape(128, LANES)

    packed = call(
        pack_body, (index, box_offsets, species, channels), (real, imag, projectors),
        shape(SLABS * 24, LANES), (pltpu.VMEM((96, LANES), f32),),
    )
    got = exchange(packed.reshape(SLABS, 24, LANES), "fft")
    local, turn = call(
        local_body, (index, vector_potential), (real, imag, pot, y_table, z_table),
        (shape(256, LANES), shape(2, 128, LANES)),
    )
    picked, table, boxes = call(
        pick_body, (index,), (got.reshape(SLABS * 24, LANES), coupling),
        (shape(72, LANES), shape(64, LANES), shape(8, LANES, dtype=i32)),
    )
    beta = lax.all_gather(picked, "band").reshape(BANDS * 72, LANES)
    moved = call(
        functools.partial(columns_body, 24), (vector_potential,), (got, x_table), shape(256, LANES)
    )
    window = pltpu.VMEM((320, LANES), f32)
    square = pltpu.VMEM((128, LANES), f32)
    shares = call(
        coef_body, (boxes,), (beta, real, imag, turn, moved), shape(SLABS, 16, LANES), (window, square)
    )
    got = exchange(shares, "fft")
    first, shares = call(
        first_body, (index, boxes), (beta, table, got, turn, local),
        (shape(256, LANES), shape(SLABS, 16, LANES)), (window, square, window, square),
    )
    got = exchange(shares, "fft")
    moved = call(
        functools.partial(columns_body, 16), (vector_potential,), (got, x_table), shape(256, LANES)
    )
    back = exchange(moved.reshape(SLABS, 8, LANES), "fft")
    near = call(
        second_body, (index, vector_potential, boxes),
        (beta, table, got, turn, first, pot, y_table, z_table), shape(256, LANES), (window, square),
    )
    new_real, new_imag, weighted = call(
        final_body, (occupation,), (real, imag, first, near, back),
        (shape(128, LANES), shape(128, LANES), shape(BANDS, 8, LANES)), (pltpu.VMEM((256, LANES), f32),),
    )
    density = jnp.sum(exchange(weighted, "band"), axis=0).reshape(2, 4, LANES)
    whole = (1, 2, NY, NZ)
    return new_real.reshape(whole), new_imag.reshape(whole), density


def solution(mesh):
    placed = (
        P("band", "fft", None, None),
        P("band", "fft", None, None),
        P("fft", None, None),
        P(),
        P("band"),
        P("fft", None, None),
        P(None, "fft"),
        P("fft"),
        P("fft", None),
        P(),
    )
    return jax.shard_map(
        per_device,
        mesh=mesh,
        in_specs=placed,
        out_specs=(
            P("band", "fft", None, None),
            P("band", "fft", None, None),
            P("fft", "band", None),
        ),
        check_vma=False,
    )
```

time: 1380 us -> 130 us (0.09)
  other arithmetic: 468 us -> 0.68 us
  local copies, waits for them, and re-layouts: 379 us -> 4.03 us
  starting transfers between devices: 291 us -> 19.9 us
  waiting for transfers between devices: 186 us -> 12 us
  blocking collectives: 0 us -> 68.9 us
  matrix products: 27.7 us -> 0 us
  Pallas kernels: 0 us -> 22.8 us
  between operations: 17.8 us -> 1.43 us
    scatter-add x4 -> x0, other arithmetic: 452 us -> none  [the longest x2 226 us: spread(): zeroed.at[:, flat].add(placed_imag)]
    gather x8 -> x0, local copies, waits for them, and re-layouts: 362 us -> none  [the longest x4 181 us: project(): take_imag = imag_part.reshape(orbs, -1)[:, flat] * valid]
    ppermute x64 -> x0, starting transfers between devices: 252 us -> none  [shifted(): return lax.ppermute(block, axis, route)]
    unnamed x2 -> x0, waiting for transfers between devices: 127 us -> none
    all_to_all x0 -> x3, blocking collectives: none -> 46 us  [exchange(): return lax.all_to_all(value, axis, split_axis=0, concat_axis=0, tiled=True)]
    all_to_all x8 -> x2, waiting for transfers between devices: 47.1 us -> 12 us  [exchange(): return lax.all_to_all(value, axis, split_axis=0, concat_axis=0, tiled=True)]
    dot_general x61 -> x0, matrix products: 27.7 us -> none  [the longest x8 3.87 us: turn_axis(): jnp.einsum(form, cosine, real_part, precision=highest)]
    all_gather x0 -> x1, blocking collectives: none -> 22.9 us  [per_device(): beta = lax.all_gather(picked, 'band').reshape(BANDS * 72, LANES)]
  transfers between devices with their start and end apart: 73 -> 2, of which waited for: 14 -> 2; matrix products, arithmetic and copies ran while one was open for 63% -> 0% of each run, Pallas kernels for 0% -> 6%
where the time goes in v1:
time: 130 us
  blocking collectives  68.9 us (53%)
  Pallas kernels  22.8 us (18%)
  starting transfers between devices  19.9 us (15%)
  waiting for transfers between devices  12 us (9%)
  local copies, waits for them, and re-layouts  4.03 us (3%)
  between operations  1.43 us (1%)
    all_to_all x3, blocking collectives, exchange(): return lax.all_to_all(value, axis, split_axis=0, concat_axis=0, tiled=True)  46 us
    all_gather x1, blocking collectives, per_device(): beta = lax.all_gather(picked, 'band').reshape(BANDS * 72, LANES)  22.9 us
    pallas_call x9, Pallas kernels, call(): pl.pallas_call(body, out_shape=outs, in_specs=[smem()] * len(scalars) + [...  22.8 us
    all_to_all x2, starting transfers between devices, exchange(): return lax.all_to_all(value, axis, split_axis=0, concat_axis=0, tiled=True)  19.9 us
    all_to_all x2, waiting for transfers between devices, exchange(): return lax.all_to_all(value, axis, split_axis=0, concat_axis=0, tiled=True)  12 us
    unnamed x28, local copies, waits for them, and re-layouts  4.03 us
  transfers between devices with their start and end apart: 2, of which 2 were waited for; matrix products, arithmetic and copies ran while one was open for 0% of the time, Pallas kernels for 6%

profile of v1, /device:TPU:1, one launch (start us, length us, event | category | flops | bytes accessed | tf_op | source)
XLA Modules:
  0.0 129.7 jit_solution(3464537721346508521)
XLA Ops:
  0.6 0.0 copy-start.12
  0.6 0.1 pad_add_fusion.index_ref
  0.7 0.0 copy-start.11
  0.7 0.0 copy-start.13
  0.7 0.6 copy-done.12
  1.3 0.1 copy-done.11
  1.4 0.0 copy-done.13
  1.4 0.0 copy-start.3
  1.4 0.8 copy-done.3
  2.2 0.0 copy-start.5
  2.2 0.8 copy-done.5
  3.1 0.0 copy-start.7
  3.1 1.0 copy-done.7
  4.1 0.0 copy-start.2
  4.1 1.6 %shard_map.148 = f32[768,128]{1,0:T(8,128)} custom-call(s32[2]{0:T(128)S(1)} %pad_add_fusion.index_ref, s32[3,4]{1,0:T(4,128)S(1)} %copy-done.11, s32[4]{0:T(128)S(1)} %copy-done.13, s32[4,8]{1,0:T(4,128)S(1)} %copy-done.12, f32[128,128]{1,0:T(8,128)S(1)} %bitcast.12, f32[128,128]{1,0:T(8,128)S(1)} %bitcast.16, f32[4,8,4096]{2,1,0:T(8,128)S(1)} %copy-done.7), custom_call_target="tpu_custom_call" | custom-call | tf_op jit(solution)/shard_map/pallas_call | solution.py:344
  5.7 0.0 copy-start.1
  5.7 0.0 copy-start.4
  5.7 0.0 copy-start.6
  5.7 0.0 copy-start.8
  5.7 13.9 %all-to-all-start = ((f32[32,24,128]{2,1,0:T(8,128)}), f32[32,24,128]{2,1,0:T(8,128)S(1)}, u32[]{:S(2)}, u32[]{:S(2)}) async-start(f32[32,24,128]{2,1,0:T(8,128)} %bitcast.4), calls=%async_computation | async-start | bytes 786432 | tf_op jit(solution)/shard_map/all_to_all | solution.py:359
  19.6 0.0 copy-start.10
  19.6 0.0 copy-done.2
  19.6 0.0 copy-done.1
  19.6 0.0 copy-done.4
  19.6 0.0 copy-done.6
  19.6 0.0 copy-done.8
  19.7 0.6 copy-done.10
  20.3 0.0 copy-start.9
  20.3 1.0 shard_map.150
  21.3 0.0 copy-start
  21.3 9.9 %all-to-all-done.got_ref = f32[32,24,128]{2,1,0:T(8,128)S(1)} async-done(((f32[32,24,128]{2,1,0:T(8,128)}), f32[32,24,128]{2,1,0:T(8,128)S(1)}, u32[]{:S(2)}, u32[]{:S(2)}) %all-to-all-start) | async-done | bytes 393248 | tf_op jit(solution)/shard_map/all_to_all | solution.py:359
  31.2 0.0 copy-done.9
  31.2 0.7 shard_map.149
  32.0 22.9 %all-gather.proj_ref = f32[1152,128]{1,0:T(8,128)S(1)} all-gather(f32[72,128]{1,0:T(8,128)S(1)} %get-tuple-element.14), channel_id=2, replica_groups=mesh['fft'=32,'band'=16] {'band'}, dimensions={0}, use_global_device_ids=true | all-gather | bytes 626688 | tf_op jit(solution)/shard_map/all_gather | solution.py:384
  54.9 0.0 copy-done
  54.9 0.8 shard_map.151.moved_ref
  55.7 2.0 %shard_map.152 = f32[32,16,128]{2,1,0:T(8,128)S(1)} custom-call(s32[8,128]{1,0:T(8,128)S(1)} %get-tuple-element.13.boxes_ref, f32[1152,128]{1,0:T(8,128)S(1)} %all-gather.proj_ref, f32[128,128]{1,0:T(8,128)S(1)} %bitcast.14, f32[128,128]{1,0:T(8,128)S(1)} %bitcast.18, f32[2,128,128]{2,1,0:T(8,128)S(1)} %get-tuple-element.16.turn_ref, ...), custom_call_target="tpu_custom_call" | custom-call | tf_op jit(solution)/shard_map/pallas_call | solution.py:344
  57.7 14.7 %all_to_all.25.got_ref = f32[32,16,128]{2,1,0:T(8,128)S(1)} all-to-all(f32[32,16,128]{2,1,0:T(8,128)S(1)} %shard_map.152), channel_id=1, replica_groups=mesh['fft'=32,'band'=16] {'fft'}, dimensions={0} | all-to-all | bytes 524288 | tf_op jit(solution)/shard_map/all_to_all | solution.py:359
  72.5 7.9 %shard_map.153 = (f32[256,128]{1,0:T(8,128)S(1)}, f32[32,16,128]{2,1,0:T(8,128)S(1)}) custom-call(s32[2]{0:T(128)S(1)} %pad_add_fusion.index_ref, s32[8,128]{1,0:T(8,128)S(1)} %get-tuple-element.13.boxes_ref, f32[1152,128]{1,0:T(8,128)S(1)} %all-gather.proj_ref, f32[64,128]{1,0:T(8,128)S(1)} %get-tuple-element.15.table_ref, ...), custom_call_target="tpu_custom_call" | custom-call | tf_op jit(solution)/shard_map/pallas_call | solution.py:344
  80.4 16.0 %all_to_all.26.got_ref = f32[32,16,128]{2,1,0:T(8,128)S(1)} all-to-all(f32[32,16,128]{2,1,0:T(8,128)S(1)} %get-tuple-element.19), channel_id=1, replica_groups=mesh['fft'=32,'band'=16] {'fft'}, dimensions={0} | all-to-all | bytes 524288 | tf_op jit(solution)/shard_map/all_to_all | solution.py:359
  96.4 1.5 %shard_map.155 = f32[256,128]{1,0:T(8,128)} custom-call(f32[3]{0:T(128)S(1)} %copy-done.10, f32[32,16,128]{2,1,0:T(8,128)S(1)} %all_to_all.26.got_ref, f32[2,256,256]{2,1,0:T(8,128)S(1)} %copy-done), custom_call_target="tpu_custom_call" | custom-call | tf_op jit(solution)/shard_map/pallas_call | solution.py:344
  97.9 6.0 %all-to-all-start.3 = ((f32[32,8,128]{2,1,0:T(8,128)}), f32[32,8,128]{2,1,0:T(8,128)S(1)}, u32[]{:S(2)}, u32[]{:S(2)}) async-start(f32[32,8,128]{2,1,0:T(8,128)} %bitcast.7), calls=%async_computation.3 | async-start | bytes 262144 | tf_op jit(solution)/shard_map/all_to_all | solution.py:359
  104.6 6.4 %shard_map.154.near_ref = f32[256,128]{1,0:T(8,128)S(1)} custom-call(s32[2]{0:T(128)S(1)} %pad_add_fusion.index_ref, f32[3]{0:T(128)S(1)} %copy-done.10, s32[8,128]{1,0:T(8,128)S(1)} %get-tuple-element.13.boxes_ref, f32[1152,128]{1,0:T(8,128)S(1)} %all-gather.proj_ref, f32[64,128]{1,0:T(8,128)S(1)} %get-tuple-element.15.table_ref, ...), custom_call_target="tpu_custom_call" | custom-call | tf_op jit(solution)/shard_map/pallas_call | solution.py:344
  111.0 2.0 %all-to-all-done.3.got_ref = f32[32,8,128]{2,1,0:T(8,128)S(1)} async-done(((f32[32,8,128]{2,1,0:T(8,128)}), f32[32,8,128]{2,1,0:T(8,128)S(1)}, u32[]{:S(2)}, u32[]{:S(2)}) %all-to-all-start.3) | async-done | bytes 131104 | tf_op jit(solution)/shard_map/all_to_all | solution.py:359
  113.1 0.7 shard_map.156
  113.8 15.2 %all_to_all.27 = f32[16,8,128]{2,1,0:T(8,128)S(1)} all-to-all(f32[16,8,128]{2,1,0:T(8,128)S(1)} %get-tuple-element.22), channel_id=1, replica_groups=mesh['fft'=32,'band'=16] {'band'}, dimensions={0} | all-to-all | bytes 131072 | tf_op jit(solution)/shard_map/all_to_all | solution.py:359
  129.0 0.6 reduce_sum.9
Async XLA Ops:
  0.6 0.7 copy-start.12
  0.7 0.7 copy-start.11
  0.7 0.7 copy-start.13
  1.4 0.8 copy-start.3
  2.2 0.8 copy-start.5
  3.1 1.0 copy-start.7
  4.1 15.5 %copy-start.2 = (f32[2,256,256]{2,1,0:T(8,128)S(1)}, f32[2,256,256]{2,1,0:T(8,128)}, u32[]{:S(2)}) copy-start(f32[2,256,256]{2,1,0:T(8,128)} %constant.19.clone.z_ref) | copy-start | bytes 1572868
  5.7 13.9 %copy-start.1 = (f32[2,256,256]{2,1,0:T(8,128)S(1)}, f32[2,256,256]{2,1,0:T(8,128)}, u32[]{:S(2)}) copy-start(f32[2,256,256]{2,1,0:T(8,128)} %constant.18.clone.y_ref) | copy-start | bytes 1572868
  5.7 13.9 %copy-start.4 = (f32[1,2,64,128]{3,2,1,0:T(8,128)S(1)}, f32[1,2,64,128]{3,2,1,0:T(8,128)}, u32[]{:S(2)}) copy-start(f32[1,2,64,128]{3,2,1,0:T(8,128)} %param.13) | copy-start | bytes 196612
  5.7 13.9 %copy-start.6 = (f32[1,2,64,128]{3,2,1,0:T(8,128)S(1)}, f32[1,2,64,128]{3,2,1,0:T(8,128)}, u32[]{:S(2)}) copy-start(f32[1,2,64,128]{3,2,1,0:T(8,128)} %param.14) | copy-start | bytes 196612
  5.7 13.9 %copy-start.8 = (f32[2,64,128]{2,1,0:T(8,128)S(1)}, f32[2,64,128]{2,1,0:T(8,128)}, u32[]{:S(2)}) copy-start(f32[2,64,128]{2,1,0:T(8,128)} %param.15) | copy-start | bytes 196612
  5.7 25.5 %all-to-all-start = ((f32[32,24,128]{2,1,0:T(8,128)}), f32[32,24,128]{2,1,0:T(8,128)S(1)}, u32[]{:S(2)}, u32[]{:S(2)}) async-start(f32[32,24,128]{2,1,0:T(8,128)} %bitcast.4), calls=%async_computation | async-start | bytes 786432 | tf_op jit(solution)/shard_map/all_to_all | solution.py:359
  19.6 0.7 copy-start.10
  20.3 11.0 %copy-start.9 = (f32[4,8,8]{2,1,0:T(8,128)S(1)}, f32[4,8,8]{2,1,0:T(8,128)}, u32[]{:S(2)}) copy-start(f32[4,8,8]{2,1,0:T(8,128)} %coupling_ref.1) | copy-start | bytes 3076
  21.3 33.5 %copy-start = (f32[2,256,256]{2,1,0:T(8,128)S(1)}, f32[2,256,256]{2,1,0:T(8,128)}, u32[]{:S(2)}) copy-start(f32[2,256,256]{2,1,0:T(8,128)} %constant.17.clone.x_ref) | copy-start | bytes 1572868
  97.9 15.2 %all-to-all-start.3 = ((f32[32,8,128]{2,1,0:T(8,128)}), f32[32,8,128]{2,1,0:T(8,128)S(1)}, u32[]{:S(2)}, u32[]{:S(2)}) async-start(f32[32,8,128]{2,1,0:T(8,128)} %bitcast.7), calls=%async_computation.3 | async-start | bytes 262144 | tf_op jit(solution)/shard_map/all_to_all | solution.py:359

commit v2 on v1

v2 whole, which is shorter than its diff:
```python
import functools
import math

import jax
import jax.numpy as jnp
import numpy as np
from jax import lax
from jax.experimental import pallas as pl
from jax.experimental.pallas import tpu as pltpu
from jax.sharding import PartitionSpec as P

NX = 64
NY = 64
NZ = 128
BOX = 16
NPROJ = 8
SLABS = 32
BANDS = 16
REACH = 9
KINDS = 4
LANES = 128
IMAG = 64

time_step = 0.01
kinetic_scale = 0.5 * (2.0 * math.pi / 38.0) ** 2
highest = lax.Precision.HIGHEST
f32 = jnp.float32
i32 = jnp.int32


def circulant(length):
    modes = np.arange(length)
    modes = np.where(modes < length // 2, modes, modes - length).astype(np.float64)
    steps = np.arange(length)
    wave = np.exp(2j * np.pi * np.outer(steps, modes) / length) / length
    apart = (steps[:, None] - steps[None, :]) % length
    return (wave @ modes**2)[apart] * kinetic_scale, (wave @ modes)[apart] * 2.0 * kinetic_scale


def blocks(matrix):
    return np.array([[matrix.real, -matrix.imag], [matrix.imag, matrix.real]])


def along_x(matrix):
    whole = blocks(matrix).reshape(2, 2, SLABS, 2, SLABS, 2)
    out = np.einsum("cdipjq,yz->iycpjzdq", whole, np.eye(2))
    return out.reshape(256, 256).astype(np.float32)


def along_y(matrix):
    out = np.einsum("cdyz,pq->cpydqz", blocks(matrix), np.eye(2))
    return out.reshape(256, 256).astype(np.float32)


def along_z(matrix):
    return np.einsum("cdyz->dzcy", blocks(matrix)).reshape(256, 256).astype(np.float32)


def tables():
    x2, x1 = circulant(NX)
    y2, y1 = circulant(NY)
    z2, z1 = circulant(NZ)
    return (
        np.stack([along_x(x2), along_x(x1)]),
        np.stack([along_y(y2), along_y(y1)]),
        np.stack([along_z(z2), along_z(z1)]),
    )


def halves(value):
    high = value.astype(jnp.bfloat16)
    low = (value - high.astype(f32)).astype(jnp.bfloat16)
    return high, low


def dot3(left, right):
    left_high, left_low = halves(left)
    right_high, right_low = halves(right)
    dot = functools.partial(jnp.dot, preferred_element_type=f32)
    return dot(left_high, right_high) + (dot(left_high, right_low) + dot(left_low, right_high))


def group_matrix():
    row = lax.broadcasted_iota(i32, (NPROJ, LANES), 0)
    lane = lax.broadcasted_iota(i32, (NPROJ, LANES), 1)
    return (lane // BOX == row).astype(f32)


def kinetic_yz(field, y_ref, z_ref, shift_y, shift_z):
    along = dot3(y_ref[0] + shift_y * y_ref[1], field)
    wide = jnp.concatenate([field[:128], field[128:]], axis=1)
    across = dot3(wide, z_ref[0] + shift_z * z_ref[1])
    across = jnp.concatenate([across[:, :128], across[:, 128:]], axis=0)
    constant = kinetic_scale * (shift_y * shift_y + shift_z * shift_z)
    return along + across + constant * field


def kinetic_x(field, high_ref, low_ref, shift):
    field_high, field_low = halves(field)
    dot = functools.partial(jnp.dot, preferred_element_type=f32)
    high = high_ref[...]
    moved = dot(high, field_high) + (dot(high, field_low) + dot(low_ref[...], field_high))
    return moved + (kinetic_scale * shift * shift) * field


def pack_body(index_ref, boxes_ref, species_ref, channels_ref, proj_ref, own_ref, near_ref, rows_ref):
    core = index_ref[1] % 2
    sub = lax.broadcasted_iota(i32, (NPROJ, LANES), 0)
    lane = lax.broadcasted_iota(i32, (NPROJ, LANES), 1)
    cell = lane % BOX
    group = lane // BOX
    skew = (group + sub) % 8 * BOX + cell
    shift = (sub - group) % 8
    rows_ref[...] = jnp.zeros_like(rows_ref)
    for atom in range(4):
        last = shift * BOX + (cell + 256 - boxes_ref[2, atom]) % BOX
        for cut in range(BOX):
            start = pl.multiple_of((2 * cut + core) * LANES, LANES)
            tile = proj_ref[atom, :, pl.ds(start, LANES)]
            tile = jnp.take_along_axis(tile, skew, axis=1)
            tile = jnp.take_along_axis(tile, shift, axis=0)
            tile = jnp.take_along_axis(tile, last, axis=1)
            rows_ref[pl.ds(atom * 160 + 8 + cut * 8, 8), :] = tile
    facts = jnp.zeros((NPROJ, LANES), f32)
    for atom in range(4):
        for channel in range(NPROJ):
            here = (sub == channel) & (lane == atom)
            facts = jnp.where(here, channels_ref[atom, channel].astype(f32), facts)
        facts = jnp.where(lane == 4 + atom, species_ref[atom].astype(f32), facts)
        facts = jnp.where(lane == 8 + atom, boxes_ref[1, atom].astype(f32), facts)
        facts = jnp.where(lane == 12 + atom, boxes_ref[2, atom].astype(f32), facts)
    for atom in range(4):
        odd = boxes_ref[0, atom] % 2
        for distance in range(REACH):
            start = pl.multiple_of(atom * 160 + (2 * distance + 1 - odd) * 8, 8)
            piece = rows_ref[pl.ds(start, 16), :]
            if distance == 0:
                near_ref[pl.ds(atom * 16, 16), :] = piece
            else:
                own_ref[pl.ds((distance - 1) * 64 + atom * 16, 16), :] = piece
    own_ref[pl.ds(512, 8), :] = facts


def route_body(index_ref, own_ref, near_ref, passed_ref, out_ref, last_ref):
    place = index_ref[0] % 8
    for target in range(8):

        @pl.when(target == place)
        def _():
            out_ref[target, 0:64, :] = near_ref[...]
            out_ref[target, 64:72, :] = own_ref[512:520, :]

        @pl.when(target > place)
        def _():
            start = pl.multiple_of((target - place - 1) * 64, 64)
            out_ref[target, 0:64, :] = own_ref[pl.ds(start, 64), :]
            out_ref[target, 64:72, :] = own_ref[512:520, :]

        @pl.when(target < place)
        def _():
            start = pl.multiple_of((target - place + 7) * 64, 64)
            out_ref[target, 0:64, :] = passed_ref[pl.ds(start, 64), :]
            out_ref[target, 64:72, :] = passed_ref[512:520, :]

    last_ref[...] = passed_ref[448:520, :]


def pick_body(index_ref, got_ref, last_ref, coupling_ref, proj_ref, table_ref, boxes_ref):
    place = index_ref[0] % 8
    lane = lax.broadcasted_iota(i32, (NPROJ, LANES), 1)
    zero = jnp.zeros((NPROJ, LANES), f32)
    gates, kind, first_y, first_z = zero, zero, zero, zero
    for distance in range(REACH):
        if distance < 8:
            source = (place + 8 - distance) % 8
            proj_ref[pl.ds(distance * 64, 64), :] = got_ref[source, 0:64, :]
            facts = got_ref[source, 64:72, :]
        else:
            proj_ref[pl.ds(distance * 64, 64), :] = last_ref[0:64, :]
            facts = last_ref[64:72, :]
        here = lane // 4 == distance

        def moved(offset):
            return jnp.where(here, pltpu.roll(facts, (4 * distance - offset) % LANES, 1), 0.0)

        gates += moved(0)
        kind += moved(4)
        first_y += moved(8)
        first_z += moved(12)
    gates += pltpu.roll(gates, IMAG, 1)
    kind += pltpu.roll(kind, IMAG, 1)
    for other in range(NPROJ):
        value = zero
        for which in range(KINDS):
            column = coupling_ref[which][:, other : other + 1]
            value = jnp.where(kind == float(which), column, value)
        table_ref[pl.ds(other * 8, 8), :] = value * gates * gates[other : other + 1, :]
    sub = lax.broadcasted_iota(i32, (NPROJ, LANES), 0)
    boxes_ref[...] = jnp.where(sub == 0, first_y, first_z).astype(i32)


def local_body(
    index_ref, vector_ref, real_ref, imag_ref, pot_ref, x_ref, y_ref, z_ref, out_ref, turn_ref, high_ref, low_ref
):
    slab = index_ref[0]
    field = jnp.concatenate([real_ref[...], imag_ref[...]], axis=0)
    out = kinetic_yz(field, y_ref, z_ref, vector_ref[1], vector_ref[2])
    pot = pot_ref[...]
    out_ref[...] = out + jnp.concatenate([pot, pot], axis=0) * field
    row = lax.broadcasted_iota(i32, (128, LANES), 0)
    x = (slab * 2 + row // NY).astype(f32)
    y = (row % NY).astype(f32)
    z = lax.broadcasted_iota(i32, (128, LANES), 1).astype(f32)
    turns = vector_ref[0] * x / NX + vector_ref[1] * y / NY + vector_ref[2] * z / NZ
    turns = turns - jnp.floor(turns + 0.5)
    theta = (2.0 * math.pi) * turns
    turn_ref[0] = jnp.cos(theta)
    turn_ref[1] = jnp.sin(theta)
    high, low = halves(x_ref[0] + vector_ref[0] * x_ref[1])
    high_ref[...] = high
    low_ref[...] = low


def project(boxes_ref, proj_ref, real, imag, turn_ref, field_ref, sums_ref):
    cosine, sine = turn_ref[0], turn_ref[1]
    turned = (cosine * real - sine * imag, sine * real + cosine * imag)
    for part in range(2):
        for plane in range(2):
            base = (part * 2 + plane) * 80
            field_ref[pl.ds(base, 64), :] = turned[part][plane * 64 : plane * 64 + 64]
            field_ref[pl.ds(base + 64, 16), :] = turned[part][plane * 64 : plane * 64 + 16]
    sums_ref[...] = jnp.zeros_like(sums_ref)
    cell = lax.broadcasted_iota(i32, (BOX, LANES), 1) % BOX

    def one(atom, carry):
        first_y = boxes_ref[0, atom]
        first_z = boxes_ref[1, atom]
        pick = (first_z + (cell + LANES - first_z) % BOX) % LANES
        total = [None, None]
        for plane in range(2):
            start = pl.multiple_of(atom * 16 + plane * 8, 8)
            beta = jnp.concatenate([proj_ref[0, pl.ds(start, 8), :], proj_ref[1, pl.ds(start, 8), :]], axis=0)
            for part in range(2):
                rows = field_ref[pl.ds((part * 2 + plane) * 80 + first_y, BOX), :]
                term = beta * jnp.take_along_axis(rows, pick, axis=1)
                total[part] = term if plane == 0 else total[part] + term
        for part in range(2):
            sums_ref[pl.ds(part * IMAG + atom, 1), :] = jnp.sum(total[part], axis=0, keepdims=True)
        return carry

    lax.fori_loop(0, 4 * REACH, one, 0, unroll=4)
    return lax.dot_general(
        group_matrix(), sums_ref[...], (((1,), (1,)), ((), ())), precision=highest, preferred_element_type=f32
    )


def spread(slab, boxes_ref, proj_ref, table_ref, got_ref, turn_ref, place_ref, dual_ref):
    lane = lax.broadcasted_iota(i32, (NPROJ, LANES), 1)
    box = (lane % IMAG) // 4
    coef = jnp.zeros((NPROJ, LANES), f32)
    for offset in range(1 - REACH, REACH):
        source = (slab + SLABS + offset) % SLABS
        share = got_ref[source, 8:16, :]
        if offset != 0:
            share = pltpu.roll(share, (-4 * offset) % LANES, 1)
        sent = box + offset
        coef += jnp.where((box < REACH) & (sent >= 0) & (sent < REACH), share, 0.0)
    dual = jnp.zeros((NPROJ, LANES), f32)
    for other in range(NPROJ):
        dual += table_ref[pl.ds(other * 8, 8), :] * coef[other : other + 1, :]
    dual_ref[...] = lax.dot_general(
        dual, group_matrix(), (((0,), (0,)), ((), ())), precision=highest, preferred_element_type=f32
    )
    place_ref[...] = jnp.zeros_like(place_ref)
    left = lax.broadcasted_iota(i32, (256, 256), 0)
    right = lax.broadcasted_iota(i32, (256, 256), 1)
    gather = ((left // LANES == right // LANES) & (left % BOX == right % BOX)).astype(f32).astype(jnp.bfloat16)
    wide = lax.broadcasted_iota(i32, (8, 2 * LANES), 1) % LANES
    dot = functools.partial(jnp.dot, preferred_element_type=f32)
    for distance in range(REACH):
        rows = []
        for half in range(2):
            for atom in range(4 * distance, 4 * distance + 4):
                beta = proj_ref[half, pl.ds(atom * 16, 16), :]
                real = beta * dual_ref[pl.ds(atom, 1), :]
                imag = beta * dual_ref[pl.ds(IMAG + atom, 1), :]
                rows.append(jnp.concatenate([real, imag], axis=1))
        high, low = halves(jnp.concatenate(rows, axis=0))
        value = dot(high, gather) + dot(low, gather)
        for atom in range(4 * distance, 4 * distance + 4):
            first_y = boxes_ref[0, atom]
            first_z = boxes_ref[1, atom]
            inside = (wide + LANES - first_z) % LANES < BOX
            for plane in range(2):
                parts = []
                for half in range(2):
                    start = half * 64 + (atom % 4) * 16 + plane * 8
                    parts.append(jnp.where(inside, value[start : start + 8], 0.0))
                both = jnp.concatenate(parts, axis=0)
                place_ref[pl.ds(plane * 80 + first_y, BOX), :] += both[:, :LANES]
                place_ref[pl.ds(160 + plane * 80 + first_y, BOX), :] += both[:, LANES:]
    for block in range(4):
        place_ref[pl.ds(block * 80, 16), :] += place_ref[pl.ds(block * 80 + 64, 16), :]
    back_real = jnp.concatenate([place_ref[pl.ds(0, 64), :], place_ref[pl.ds(80, 64), :]], axis=0)
    back_imag = jnp.concatenate([place_ref[pl.ds(160, 64), :], place_ref[pl.ds(240, 64), :]], axis=0)
    cosine, sine = turn_ref[0], turn_ref[1]
    return cosine * back_real + sine * back_imag, cosine * back_imag - sine * back_real


def columns(field_ref, out_ref):
    for y in range(2):
        for part in range(2):
            for plane in range(2):
                row = y * 4 + part * 2 + plane
                start = part * 128 + plane * 64 + y
                out_ref[:, row, :] = field_ref[pl.ds(start, SLABS, stride=2), :]


def unpack(got_ref, first_row, field_ref):
    for y in range(2):
        for part in range(2):
            for plane in range(2):
                row = y * 4 + part * 2 + plane
                start = part * 128 + plane * 64 + y
                field_ref[pl.ds(start, SLABS, stride=2), :] = got_ref[:, first_row + row, :]


def coef_body(boxes_ref, proj_ref, real_ref, imag_ref, turn_ref, out_ref, whole_ref, field_ref, sums_ref):
    real, imag = real_ref[...], imag_ref[...]
    whole_ref[0:128, :] = real
    whole_ref[128:256, :] = imag
    columns(whole_ref, out_ref)
    coef = project(boxes_ref, proj_ref, real, imag, turn_ref, field_ref, sums_ref)
    out_ref[:, 8:16, :] = jnp.broadcast_to(coef[None], (SLABS, 8, LANES))


def rest_body(
    index_ref, vector_ref, boxes_ref, proj_ref, table_ref, got_ref, turn_ref, local_ref, high_ref, low_ref,
    rest_ref, moved_ref, out_ref, place_ref, dual_ref,
):
    field = got_ref[:, 0:8, :].reshape(256, LANES)
    moved = kinetic_x(field, high_ref, low_ref, vector_ref[0])
    moved_ref[...] = moved
    out_ref[:, 8:16, :] = moved.reshape(SLABS, 8, LANES)
    far_real, far_imag = spread(
        index_ref[0], boxes_ref, proj_ref, table_ref, got_ref, turn_ref, place_ref, dual_ref
    )
    rest_ref[0:128, :] = local_ref[0:128, :] + far_real
    rest_ref[128:256, :] = local_ref[128:256, :] + far_imag
    columns(rest_ref, out_ref)


def first_body(
    vector_ref, boxes_ref, proj_ref, got_ref, turn_ref, rest_ref, moved_ref, high_ref, low_ref,
    first_ref, out_ref, field_ref, sums_ref,
):
    field = got_ref[:, 0:8, :].reshape(256, LANES) + moved_ref[...]
    out_ref[:, 0:8, :] = kinetic_x(field, high_ref, low_ref, vector_ref[0]).reshape(SLABS, 8, LANES)
    unpack(got_ref, 8, first_ref)
    real = first_ref[0:128, :] + rest_ref[0:128, :]
    imag = first_ref[128:256, :] + rest_ref[128:256, :]
    first_ref[0:128, :] = real
    first_ref[128:256, :] = imag
    coef = project(boxes_ref, proj_ref, real, imag, turn_ref, field_ref, sums_ref)
    out_ref[:, 8:16, :] = jnp.broadcast_to(coef[None], (SLABS, 8, LANES))


def second_body(vector_ref, first_ref, pot_ref, y_ref, z_ref, out_ref):
    field = first_ref[...]
    pot = pot_ref[...]
    near = kinetic_yz(field, y_ref, z_ref, vector_ref[1], vector_ref[2])
    out_ref[...] = near + jnp.concatenate([pot, pot], axis=0) * field


def final_body(
    index_ref, occupation_ref, boxes_ref, proj_ref, table_ref, got_ref, turn_ref, real_ref, imag_ref, first_ref,
    near_ref, new_real_ref, new_imag_ref, out_ref, field_ref, place_ref, dual_ref,
):
    unpack(got_ref, 0, field_ref)
    far_real, far_imag = spread(
        index_ref[0], boxes_ref, proj_ref, table_ref, got_ref, turn_ref, place_ref, dual_ref
    )
    half = 0.5 * time_step * time_step
    second_real = near_ref[0:128, :] + field_ref[0:128, :] + far_real
    second_imag = near_ref[128:256, :] + field_ref[128:256, :] + far_imag
    new_real = real_ref[...] + time_step * first_ref[128:256, :] - half * second_real
    new_imag = imag_ref[...] - time_step * first_ref[0:128, :] - half * second_imag
    new_real_ref[...] = new_real
    new_imag_ref[...] = new_imag
    weighted = occupation_ref[0] * (new_real * new_real + new_imag * new_imag)
    weighted = weighted.reshape(2, BANDS, 4, LANES)
    for plane in range(2):
        out_ref[:, pl.ds(plane * 4, 4), :] = weighted[plane]


def smem():
    return pl.BlockSpec(memory_space=pltpu.SMEM)


def vmem():
    return pl.BlockSpec(memory_space=pltpu.VMEM)


def call(body, scalars, arrays, outs, scratch=()):
    several = isinstance(outs, tuple)
    return pl.pallas_call(
        body,
        out_shape=outs,
        in_specs=[smem()] * len(scalars) + [vmem()] * len(arrays),
        out_specs=tuple(vmem() for _ in outs) if several else vmem(),
        scratch_shapes=list(scratch),
        compiler_params=pltpu.CompilerParams(vmem_limit_bytes=24 * 1024 * 1024),
    )(*scalars, *arrays)


def shape(*dims, dtype=f32):
    return jax.ShapeDtypeStruct(dims, dtype)


def exchange(value, axis):
    return lax.all_to_all(value, axis, split_axis=0, concat_axis=0, tiled=True)


def per_device(
    psi_real, psi_imag, potential, vector_potential, occupation, projectors, box_offsets, species, channels, coupling
):
    x_table, y_table, z_table = (jnp.asarray(table) for table in tables())
    index = jnp.stack([lax.axis_index("fft"), lax.axis_index("band")]).astype(i32)
    real = psi_real.reshape(128, LANES)
    imag = psi_imag.reshape(128, LANES)
    pot = potential.reshape(128, LANES)
    matrix = jax.ShapeDtypeStruct((256, 256), jnp.bfloat16)
    window = pltpu.VMEM((320, LANES), f32)
    square = pltpu.VMEM((128, LANES), f32)
    whole = pltpu.VMEM((256, LANES), f32)

    own, near = call(
        pack_body, (index, box_offsets, species, channels), (projectors,),
        (shape(520, LANES), shape(64, LANES)), (pltpu.VMEM((640, LANES), f32),),
    )
    passed = lax.ppermute(own, "fft", [(i, (i + 8) % SLABS) for i in range(SLABS)])
    local, turn, high, low = call(
        local_body, (index, vector_potential), (real, imag, pot, x_table, y_table, z_table),
        (shape(256, LANES), shape(2, 128, LANES), matrix, matrix),
    )
    slices, last = call(
        route_body, (index,), (own, near, passed), (shape(8, 72, LANES), shape(72, LANES))
    )
    rows = [list(range(8 * x, 8 * x + 8)) for x in range(4)]
    got = lax.all_to_all(slices, "fft", split_axis=0, concat_axis=0, tiled=True, axis_index_groups=rows)
    picked, table, boxes = call(
        pick_body, (index,), (got, last, coupling),
        (shape(576, LANES), shape(64, LANES), shape(8, LANES, dtype=i32)),
    )
    chips = [[2 * y, 2 * y + 1] for y in range(8)]
    beta = lax.all_gather(picked, "band", axis_index_groups=chips)
    shares = call(
        coef_body, (boxes,), (beta, real, imag, turn), shape(SLABS, 16, LANES), (whole, window, square)
    )
    got = exchange(shares, "fft")
    rest, moved, shares = call(
        rest_body, (index, vector_potential, boxes), (beta, table, got, turn, local, high, low),
        (shape(256, LANES), shape(256, LANES), shape(SLABS, 16, LANES)), (window, square),
    )
    got = exchange(shares, "fft")
    first, shares = call(
        first_body, (vector_potential, boxes), (beta, got, turn, rest, moved, high, low),
        (shape(256, LANES), shape(SLABS, 16, LANES)), (window, square),
    )
    got = exchange(shares, "fft")
    near = call(second_body, (vector_potential,), (first, pot, y_table, z_table), shape(256, LANES))
    new_real, new_imag, weighted = call(
        final_body, (index, occupation, boxes), (beta, table, got, turn, real, imag, first, near),
        (shape(128, LANES), shape(128, LANES), shape(BANDS, 8, LANES)), (whole, window, square),
    )
    density = jnp.sum(exchange(weighted, "band"), axis=0).reshape(2, 4, LANES)
    grid = (1, 2, NY, NZ)
    return new_real.reshape(grid), new_imag.reshape(grid), density


def solution(mesh):
    placed = (
        P("band", "fft", None, None),
        P("band", "fft", None, None),
        P("fft", None, None),
        P(),
        P("band"),
        P("fft", None, None),
        P(None, "fft"),
        P("fft"),
        P("fft", None),
        P(),
    )
    return jax.shard_map(
        per_device,
        mesh=mesh,
        in_specs=placed,
        out_specs=(
            P("band", "fft", None, None),
            P("band", "fft", None, None),
            P("fft", "band", None),
        ),
        check_vma=False,
    )
```

time: 130 us -> 118 us (0.908)
  blocking collectives: 68.9 us -> 52.3 us
  waiting for transfers between devices: 12 us -> 20.8 us
  Pallas kernels: 22.8 us -> 14.9 us
  starting transfers between devices: 19.9 us -> 22.5 us
    all_gather x1, blocking collectives: 22.9 us -> 5.1 us  [per_device(): beta = lax.all_gather(picked, 'band', axis_index_groups=chips)]
    all_to_all x2 -> x1, starting transfers between devices: 19.9 us -> 6.23 us  [exchange(): return lax.all_to_all(value, axis, split_axis=0, concat_axis=0, tiled=True)]
    all_to_all x0 -> x1, starting transfers between devices: none -> 12.3 us  [per_device(): lax.all_to_all(slices, 'fft', split_axis=0, concat_axis=0, tiled=True, ax...]
    pallas_call x9, Pallas kernels: 22.8 us -> 14.9 us  [call(): pl.pallas_call(body, out_shape=outs, in_specs=[smem()] * len(scalars) + [...]
    all_to_all x0 -> x1, waiting for transfers between devices: none -> 7.65 us  [per_device(): lax.all_to_all(slices, 'fft', split_axis=0, concat_axis=0, tiled=True, ax...]
    ppermute x0 -> x1, waiting for transfers between devices: none -> 5.06 us  [per_device(): lax.ppermute(own, 'fft', [(i, (i + 8) % SLABS) for i in range(SLABS)])]
    ppermute x0 -> x1, starting transfers between devices: none -> 3.95 us  [per_device(): lax.ppermute(own, 'fft', [(i, (i + 8) % SLABS) for i in range(SLABS)])]
    all_to_all x2 -> x1, waiting for transfers between devices: 12 us -> 8.13 us  [exchange(): return lax.all_to_all(value, axis, split_axis=0, concat_axis=0, tiled=True)]
  transfers between devices with their start and end apart: 2 -> 3, of which waited for: 2 -> 3; matrix products, arithmetic and copies ran while one was open for 0% -> 0% of each run, Pallas kernels for 6% -> 2%
where the time goes in v2:
time: 118 us; the launch traced here: 117 us
  blocking collectives  52.3 us (44%)
  starting transfers between devices  22.5 us (19%)
  waiting for transfers between devices  20.8 us (18%)
  Pallas kernels  14.9 us (13%)
  local copies, waits for them, and re-layouts  4.58 us (4%)
  between operations  1.42 us (1%)
    all_to_all x3, blocking collectives, exchange(): return lax.all_to_all(value, axis, split_axis=0, concat_axis=0, tiled=True)  47.2 us
    pallas_call x9, Pallas kernels, call(): pl.pallas_call(body, out_shape=outs, in_specs=[smem()] * len(scalars) + [...  14.9 us
    all_to_all x1, starting transfers between devices, per_device(): lax.all_to_all(slices, 'fft', split_axis=0, concat_axis=0, tiled=True, ax...  12.3 us
    all_to_all x1, waiting for transfers between devices, exchange(): return lax.all_to_all(value, axis, split_axis=0, concat_axis=0, tiled=True)  8.13 us
    all_to_all x1, waiting for transfers between devices, per_device(): lax.all_to_all(slices, 'fft', split_axis=0, concat_axis=0, tiled=True, ax...  7.65 us
    all_to_all x1, starting transfers between devices, exchange(): return lax.all_to_all(value, axis, split_axis=0, concat_axis=0, tiled=True)  6.23 us
    all_gather x1, blocking collectives, per_device(): beta = lax.all_gather(picked, 'band', axis_index_groups=chips)  5.1 us
    ppermute x1, waiting for transfers between devices, per_device(): lax.ppermute(own, 'fft', [(i, (i + 8) % SLABS) for i in range(SLABS)])  5.06 us
  transfers between devices with their start and end apart: 3, of which 3 were waited for; matrix products, arithmetic and copies ran while one was open for 0% of the time, Pallas kernels for 2%

profile of v2, /device:TPU:1, one launch (start us, length us, event | category | flops | bytes accessed | tf_op | source)
XLA Modules:
  0.0 117.2 jit_solution(14657306764736756130)
XLA Ops:
  0.6 0.0 copy-start.4
  0.6 0.1 pad_add_fusion.index_ref
  0.7 0.0 copy-start.5
  0.7 1.1 copy-done.5
  1.8 0.0 copy-start.10
  1.8 0.7 copy-done.10
  2.5 0.0 copy-start.11
  2.5 0.7 copy-done.11
  3.2 0.0 copy-start.12
  3.2 0.7 copy-done.12
  3.8 0.0 copy-start.3
  3.8 1.2 %shard_map.148 = (f32[520,128]{1,0:T(8,128)S(1)}, f32[64,128]{1,0:T(8,128)S(1)}) custom-call(s32[2]{0:T(128)S(1)} %pad_add_fusion.index_ref, s32[3,4]{1,0:T(4,128)S(1)} %copy-done.10, s32[4]{0:T(128)S(1)} %copy-done.12, s32[4,8]{1,0:T(4,128)S(1)} %copy-done.11, f32[4,8,4096]{2,1,0:T(8,128)S(1)} %copy-done.5), custom_call_target="tpu_custom_call" | custom-call | tf_op jit(solution)/shard_map/pallas_call | solution.py:406
  5.1 3.9 %collective-permute-start = (f32[520,128]{1,0:T(8,128)S(1)}, f32[520,128]{1,0:T(8,128)S(1)}, u32[]{:S(2)}, u32[]{:S(2)}) collective-permute-start(f32[520,128]{1,0:T(8,128)S(1)} %get-tuple-element.22.own_ref), channel_id=1, source_target_pairs={{0,128},{16,144},{32,160},{48,176},{64,192},{80,208},{96,224},{112... | collective-permute-start | bytes 798728 | tf_op jit(solution)/shard_map/ppermute | solution.py:441
  9.0 5.1 %collective-permute-done.passed_ref = f32[520,128]{1,0:T(8,128)S(1)} collective-permute-done((f32[520,128]{1,0:T(8,128)S(1)}, f32[520,128]{1,0:T(8,128)S(1)}, u32[]{:S(2)}, u32[]{:S(2)}) %collective-permute-start) | collective-permute-done | bytes 266272 | tf_op jit(solution)/shard_map/ppermute | solution.py:441
  14.1 0.0 copy-start
  14.1 0.0 copy-start.1
  14.1 1.4 %shard_map.149 = (f32[8,72,128]{2,1,0:T(8,128)}, f32[72,128]{1,0:T(8,128)S(1)}) custom-call(s32[2]{0:T(128)S(1)} %pad_add_fusion.index_ref, f32[520,128]{1,0:T(8,128)S(1)} %get-tuple-element.22.own_ref, f32[64,128]{1,0:T(8,128)S(1)} %get-tuple-element.23.near_ref, f32[520,128]{1,0:T(8,128)S(1)} %collective-permute-done.passed_ref), custom_call_target="tpu_custom_call" | custom-call | tf_op jit(solution)/shard_map/pallas_call | solution.py:406
  15.5 0.0 copy-start.2
  15.5 12.3 %all-to-all-start = ((f32[8,72,128]{2,1,0:T(8,128)}), f32[8,72,128]{2,1,0:T(8,128)S(1)}, u32[]{:S(2)}, u32[]{:S(2)}) async-start(f32[8,72,128]{2,1,0:T(8,128)} %get-tuple-element.24), calls=%async_computation | async-start | bytes 589824 | tf_op jit(solution)/shard_map/all_to_all | solution.py:450
  27.8 0.0 copy-start.9
  27.8 0.0 copy-done.4
  27.9 0.0 copy-done.3
  27.9 0.0 copy-done
  27.9 0.0 copy-done.1
  27.9 0.0 copy-done.2
  27.9 0.6 copy-done.9
  28.5 0.0 copy-start.6
  28.5 0.8 copy-done.6
  29.3 0.0 copy-start.8
  29.3 1.1 shard_map.151
  30.5 7.7 %all-to-all-done.got_ref = f32[8,72,128]{2,1,0:T(8,128)S(1)} async-done(((f32[8,72,128]{2,1,0:T(8,128)}), f32[8,72,128]{2,1,0:T(8,128)S(1)}, u32[]{:S(2)}, u32[]{:S(2)}) %all-to-all-start) | async-done | bytes 294944 | tf_op jit(solution)/shard_map/all_to_all | solution.py:450
  38.1 0.0 copy-done.8
  38.1 0.7 shard_map.150
  38.9 5.1 %all-gather = f32[1152,128]{1,0:T(8,128)S(1)} all-gather(f32[576,128]{1,0:T(8,128)S(1)} %get-tuple-element.27), channel_id=2, replica_groups={{0,1},{2,3},{4,5},{6,7},{8,9},{10,11},{12,13},{14,15},{16,17},{18,19},{..., dimensions={0}, use_global_device_ids=true | all-gather | bytes 884736 | tf_op jit(solution)/shard_map/all_gather | solution.py:456
  44.0 2.2 %shard_map.152 = f32[32,16,128]{2,1,0:T(8,128)S(1)} custom-call(s32[8,128]{1,0:T(8,128)S(1)} %get-tuple-element.26.boxes_ref, f32[2,576,128]{2,1,0:T(8,128)S(1)} %bitcast.9, f32[128,128]{1,0:T(8,128)S(1)} %bitcast.14, f32[128,128]{1,0:T(8,128)S(1)} %bitcast.17, f32[2,128,128]{2,1,0:T(8,128)S(1)} %get-tuple-element.29.turn_ref), custom_call_target="tpu_custom_call" | custom-call | tf_op jit(solution)/shard_map/pallas_call | solution.py:406
  46.2 12.7 %all_to_all.25.got_ref = f32[32,16,128]{2,1,0:T(8,128)S(1)} all-to-all(f32[32,16,128]{2,1,0:T(8,128)S(1)} %shard_map.152), channel_id=1, replica_groups=mesh['fft'=32,'band'=16] {'fft'}, dimensions={0} | all-to-all | bytes 524288 | tf_op jit(solution)/shard_map/all_to_all | solution.py:421
  58.8 1.7 %shard_map.153 = (f32[256,128]{1,0:T(8,128)S(1)}, f32[256,128]{1,0:T(8,128)S(1)}, f32[32,16,128]{2,1,0:T(8,128)S(1)}) custom-call(s32[2]{0:T(128)S(1)} %pad_add_fusion.index_ref, f32[3]{0:T(128)S(1)} %copy-done.9, s32[8,128]{1,0:T(8,128)S(1)} %get-tuple-element.26.boxes_ref, f32[2,576,128]{2,1,0:T(8,128)S(1)} %bitcast.10, ...), custom_call_target="tpu_custom_call" | custom-call | tf_op jit(solution)/shard_map/pallas_call | solution.py:406
  60.6 16.2 %all_to_all.26.got_ref = f32[32,16,128]{2,1,0:T(8,128)S(1)} all-to-all(f32[32,16,128]{2,1,0:T(8,128)S(1)} %get-tuple-element.33), channel_id=1, replica_groups=mesh['fft'=32,'band'=16] {'fft'}, dimensions={0} | all-to-all | bytes 524288 | tf_op jit(solution)/shard_map/all_to_all | solution.py:421
  76.7 3.3 %shard_map.154 = (f32[256,128]{1,0:T(8,128)S(1)}, f32[32,16,128]{2,1,0:T(8,128)}) custom-call(f32[3]{0:T(128)S(1)} %copy-done.9, s32[8,128]{1,0:T(8,128)S(1)} %get-tuple-element.26.boxes_ref, f32[2,576,128]{2,1,0:T(8,128)S(1)} %bitcast.11, f32[32,16,128]{2,1,0:T(8,128)S(1)} %all_to_all.26.got_ref, f32[2,128,128]{2,1,0:T(8,128)S(1)} %get-tuple-element.29.turn_ref, ...), custom_call_target="tpu_custom_call" | custom-call | tf_op jit(solution)/shard_map/pallas_call | solution.py:406
  80.0 0.0 copy-start.7
  80.0 6.2 %all-to-all-start.3 = ((f32[32,16,128]{2,1,0:T(8,128)}), f32[32,16,128]{2,1,0:T(8,128)S(1)}, u32[]{:S(2)}, u32[]{:S(2)}) async-start(f32[32,16,128]{2,1,0:T(8,128)} %get-tuple-element.36), calls=%async_computation.3 | async-start | bytes 524288 | tf_op jit(solution)/shard_map/all_to_all | solution.py:421
  86.9 0.0 copy-done.7
  86.9 0.9 shard_map.155.near_ref
  87.8 8.1 %all-to-all-done.3.got_ref = f32[32,16,128]{2,1,0:T(8,128)S(1)} async-done(((f32[32,16,128]{2,1,0:T(8,128)}), f32[32,16,128]{2,1,0:T(8,128)S(1)}, u32[]{:S(2)}, u32[]{:S(2)}) %all-to-all-start.3) | async-done | bytes 262176 | tf_op jit(solution)/shard_map/all_to_all | solution.py:421
  95.9 2.3 %shard_map.156 = (f32[128,128]{1,0:T(8,128)}, f32[128,128]{1,0:T(8,128)}, f32[16,8,128]{2,1,0:T(8,128)S(1)}) custom-call(s32[2]{0:T(128)S(1)} %pad_add_fusion.index_ref, f32[1]{0:T(128)S(6)} %copy.16.occupation_ref, s32[8,128]{1,0:T(8,128)S(1)} %get-tuple-element.26.boxes_ref, f32[2,576,128]{2,1,0:T(8,128)S(1)} %bitcast.12, ...), custom_call_target="tpu_custom_call" | custom-call | tf_op jit(solution)/shard_map/pallas_call | solution.py:406
  98.3 18.4 %all_to_all.27 = f32[16,8,128]{2,1,0:T(8,128)S(1)} all-to-all(f32[16,8,128]{2,1,0:T(8,128)S(1)} %get-tuple-element.40), channel_id=1, replica_groups=mesh['fft'=32,'band'=16] {'band'}, dimensions={0} | all-to-all | bytes 131072 | tf_op jit(solution)/shard_map/all_to_all | solution.py:421
  116.6 0.6 reduce_sum.9
Async XLA Ops:
  0.6 27.2 %copy-start.4 = (f32[2,256,256]{2,1,0:T(8,128)S(1)}, f32[2,256,256]{2,1,0:T(8,128)}, u32[]{:S(2)}) copy-start(f32[2,256,256]{2,1,0:T(8,128)} %constant.17.clone.x_ref) | copy-start | bytes 1572868
  0.7 1.1 copy-start.5
  1.8 0.7 copy-start.10
  2.5 0.7 copy-start.11
  3.2 0.7 copy-start.12
  3.8 24.0 %copy-start.3 = (f32[1,2,64,128]{3,2,1,0:T(8,128)S(1)}, f32[1,2,64,128]{3,2,1,0:T(8,128)}, u32[]{:S(2)}) copy-start(f32[1,2,64,128]{3,2,1,0:T(8,128)} %param.14) | copy-start | bytes 196612
  5.1 9.0 %collective-permute-start = (f32[520,128]{1,0:T(8,128)S(1)}, f32[520,128]{1,0:T(8,128)S(1)}, u32[]{:S(2)}, u32[]{:S(2)}) collective-permute-start(f32[520,128]{1,0:T(8,128)S(1)} %get-tuple-element.22.own_ref), channel_id=1, source_target_pairs={{0,128},{16,144},{32,160},{48,176},{64,192},{80,208},{96,224},{112... | collective-permute-start | bytes 798728 | tf_op jit(solution)/shard_map/ppermute | solution.py:441
  14.1 13.8 %copy-start = (f32[2,256,256]{2,1,0:T(8,128)S(1)}, f32[2,256,256]{2,1,0:T(8,128)}, u32[]{:S(2)}) copy-start(f32[2,256,256]{2,1,0:T(8,128)} %constant.18.clone.y_ref) | copy-start | bytes 1572868
  14.1 13.8 %copy-start.1 = (f32[2,256,256]{2,1,0:T(8,128)S(1)}, f32[2,256,256]{2,1,0:T(8,128)}, u32[]{:S(2)}) copy-start(f32[2,256,256]{2,1,0:T(8,128)} %constant.19.clone.z_ref) | copy-start | bytes 1572868
  15.5 12.4 %copy-start.2 = (f32[1,2,64,128]{3,2,1,0:T(8,128)S(1)}, f32[1,2,64,128]{3,2,1,0:T(8,128)}, u32[]{:S(2)}) copy-start(f32[1,2,64,128]{3,2,1,0:T(8,128)} %param.13) | copy-start | bytes 196612
  15.5 22.6 %all-to-all-start = ((f32[8,72,128]{2,1,0:T(8,128)}), f32[8,72,128]{2,1,0:T(8,128)S(1)}, u32[]{:S(2)}, u32[]{:S(2)}) async-start(f32[8,72,128]{2,1,0:T(8,128)} %get-tuple-element.24), calls=%async_computation | async-start | bytes 589824 | tf_op jit(solution)/shard_map/all_to_all | solution.py:450
  27.8 0.7 copy-start.9
  28.5 0.8 copy-start.6
  29.3 8.8 %copy-start.8 = (f32[4,8,8]{2,1,0:T(8,128)S(1)}, f32[4,8,8]{2,1,0:T(8,128)}, u32[]{:S(2)}) copy-start(f32[4,8,8]{2,1,0:T(8,128)} %coupling_ref.1) | copy-start | bytes 3076
  80.0 6.9 %copy-start.7 = (f32[2,64,128]{2,1,0:T(8,128)S(1)}, f32[2,64,128]{2,1,0:T(8,128)}, u32[]{:S(2)}) copy-start(f32[2,64,128]{2,1,0:T(8,128)} %param.15) | copy-start | bytes 196612
  80.0 15.9 %all-to-all-start.3 = ((f32[32,16,128]{2,1,0:T(8,128)}), f32[32,16,128]{2,1,0:T(8,128)S(1)}, u32[]{:S(2)}, u32[]{:S(2)}) async-start(f32[32,16,128]{2,1,0:T(8,128)} %get-tuple-element.36), calls=%async_computation.3 | async-start | bytes 524288 | tf_op jit(solution)/shard_map/all_to_all | solution.py:421

commit v3 on v2

--- a/solution.py
+++ b/solution.py
@@ -103,24 +103,32 @@
     return moved + (kinetic_scale * shift * shift) * field
 
 
-def pack_body(index_ref, boxes_ref, species_ref, channels_ref, proj_ref, own_ref, near_ref, rows_ref):
+def pack_body(
+    index_ref, boxes_hbm, species_hbm, channels_hbm, proj_hbm, real_hbm, imag_hbm, out_ref, both_ref,
+    boxes_ref, species_ref, channels_ref, proj_ref, rows_ref, done,
+):
+    place = index_ref[0] % 8
     core = index_ref[1] % 2
+    copies = [
+        pltpu.make_async_copy(boxes_hbm, boxes_ref, done.at[0]),
+        pltpu.make_async_copy(species_hbm, species_ref, done.at[1]),
+        pltpu.make_async_copy(channels_hbm, channels_ref, done.at[2]),
+    ]
+    copies += [pltpu.make_async_copy(proj_hbm.at[atom], proj_ref.at[atom], done.at[3 + atom]) for atom in range(4)]
+    copies += [
+        pltpu.make_async_copy(real_hbm, both_ref.at[pl.ds(0, 128)], done.at[7]),
+        pltpu.make_async_copy(imag_hbm, both_ref.at[pl.ds(128, 128)], done.at[8]),
+    ]
+    for copy in copies:
+        copy.start()
     sub = lax.broadcasted_iota(i32, (NPROJ, LANES), 0)
     lane = lax.broadcasted_iota(i32, (NPROJ, LANES), 1)
     cell = lane % BOX
     group = lane // BOX
     skew = (group + sub) % 8 * BOX + cell
     shift = (sub - group) % 8
-    rows_ref[...] = jnp.zeros_like(rows_ref)
-    for atom in range(4):
-        last = shift * BOX + (cell + 256 - boxes_ref[2, atom]) % BOX
-        for cut in range(BOX):
-            start = pl.multiple_of((2 * cut + core) * LANES, LANES)
-            tile = proj_ref[atom, :, pl.ds(start, LANES)]
-            tile = jnp.take_along_axis(tile, skew, axis=1)
-            tile = jnp.take_along_axis(tile, shift, axis=0)
-            tile = jnp.take_along_axis(tile, last, axis=1)
-            rows_ref[pl.ds(atom * 160 + 8 + cut * 8, 8), :] = tile
+    for copy in copies[:3]:
+        copy.wait()
     facts = jnp.zeros((NPROJ, LANES), f32)
     for atom in range(4):
         for channel in range(NPROJ):
@@ -129,64 +137,87 @@
         facts = jnp.where(lane == 4 + atom, species_ref[atom].astype(f32), facts)
         facts = jnp.where(lane == 8 + atom, boxes_ref[1, atom].astype(f32), facts)
         facts = jnp.where(lane == 12 + atom, boxes_ref[2, atom].astype(f32), facts)
+        facts = jnp.where(lane == 16 + atom, (boxes_ref[0, atom] % 2).astype(f32), facts)
+    for target in range(8):
+        out_ref[target, 64:72, :] = facts
     for atom in range(4):
+        copies[3 + atom].wait()
+        last = shift * BOX + (cell + 256 - boxes_ref[2, atom]) % BOX
+        for cut in range(BOX):
+            start = pl.multiple_of((2 * cut + core) * LANES, LANES)
+            tile = proj_ref[atom, :, pl.ds(start, LANES)]
+            tile = jnp.take_along_axis(tile, skew, axis=1)
+            tile = jnp.take_along_axis(tile, shift, axis=0)
+            tile = jnp.take_along_axis(tile, last, axis=1)
+            rows_ref[pl.ds(cut * 8, 8), :] = tile
+            if cut == 0:
+                rows_ref[pl.ds(128, 8), :] = tile
         odd = boxes_ref[0, atom] % 2
-        for distance in range(REACH):
-            start = pl.multiple_of(atom * 160 + (2 * distance + 1 - odd) * 8, 8)
-            piece = rows_ref[pl.ds(start, 16), :]
-            if distance == 0:
-                near_ref[pl.ds(atom * 16, 16), :] = piece
-            else:
-                own_ref[pl.ds((distance - 1) * 64 + atom * 16, 16), :] = piece
-    own_ref[pl.ds(512, 8), :] = facts
-
-
-def route_body(index_ref, own_ref, near_ref, passed_ref, out_ref, last_ref):
-    place = index_ref[0] % 8
-    for target in range(8):
-
-        @pl.when(target == place)
-        def _():
-            out_ref[target, 0:64, :] = near_ref[...]
-            out_ref[target, 64:72, :] = own_ref[512:520, :]
-
-        @pl.when(target > place)
-        def _():
-            start = pl.multiple_of((target - place - 1) * 64, 64)
-            out_ref[target, 0:64, :] = own_ref[pl.ds(start, 64), :]
-            out_ref[target, 64:72, :] = own_ref[512:520, :]
-
-        @pl.when(target < place)
-        def _():
-            start = pl.multiple_of((target - place + 7) * 64, 64)
-            out_ref[target, 0:64, :] = passed_ref[pl.ds(start, 64), :]
-            out_ref[target, 64:72, :] = passed_ref[512:520, :]
-
-    last_ref[...] = passed_ref[448:520, :]
-
-
-def pick_body(index_ref, got_ref, last_ref, coupling_ref, proj_ref, table_ref, boxes_ref):
+        for target in range(8):
+            start = (2 * (target - place) - odd + 32) % BOX
+            out_ref[target, pl.ds(atom * 16, 16), :] = rows_ref[pl.ds(pl.multiple_of(start * 8, 8), 16), :]
+    for copy in copies[7:]:
+        copy.wait()
+
+
+def pick_body(index_ref, got_ref, boxes_ref):
     place = index_ref[0] % 8
     lane = lax.broadcasted_iota(i32, (NPROJ, LANES), 1)
+    sub = lax.broadcasted_iota(i32, (NPROJ, LANES), 0)
+    found = jnp.zeros((NPROJ, LANES), f32)
+    for slot in range(8):
+        facts = got_ref[slot, 64:72, :]
+        here = lane // 4 == slot
+        for row, offset in enumerate((8, 12, 16)):
+            found = jnp.where(here & (sub == row), pltpu.roll(facts, (4 * slot - offset) % LANES, 1), found)
+    odd = found[2:3, :].astype(i32)
+    far = (2 * place + sub - 2) < 2 * (lane // 4) + odd
+    boxes_ref[...] = jnp.where(sub < 2, found.astype(i32), jnp.where(far, 320, 0))
+
+
+def merge_body(index_ref, here_ref, passed_ref, coupling_ref, proj_ref, table_ref, boxes_ref):
+    place = index_ref[0] % 8
+    lane = lax.broadcasted_iota(i32, (NPROJ, LANES), 1)
+    sub = lax.broadcasted_iota(i32, (NPROJ, LANES), 0)
     zero = jnp.zeros((NPROJ, LANES), f32)
     gates, kind, first_y, first_z = zero, zero, zero, zero
-    for distance in range(REACH):
-        if distance < 8:
-            source = (place + 8 - distance) % 8
-            proj_ref[pl.ds(distance * 64, 64), :] = got_ref[source, 0:64, :]
-            facts = got_ref[source, 64:72, :]
-        else:
-            proj_ref[pl.ds(distance * 64, 64), :] = last_ref[0:64, :]
-            facts = last_ref[64:72, :]
-        here = lane // 4 == distance
+    for slot in range(REACH):
+        facts = zero
+
+        @pl.when(slot <= place)
+        def _():
+            for half in range(2):
+                proj_ref[half, pl.ds(slot * 64, 64), :] = here_ref[half, min(slot, 7), 0:64, :]
+            boxes_ref[...] = here_ref[0, min(slot, 7), 64:72, :].astype(i32)
+
+        @pl.when(slot > place)
+        def _():
+            for half in range(2):
+                proj_ref[half, pl.ds(slot * 64, 64), :] = passed_ref[half, max(slot - 1, 0), 0:64, :]
+            boxes_ref[...] = passed_ref[0, max(slot - 1, 0), 64:72, :].astype(i32)
+
+        facts = boxes_ref[...].astype(f32)
+        here = lane // 4 == slot
 
         def moved(offset):
-            return jnp.where(here, pltpu.roll(facts, (4 * distance - offset) % LANES, 1), 0.0)
+            return jnp.where(here, pltpu.roll(facts, (4 * slot - offset) % LANES, 1), 0.0)
 
         gates += moved(0)
         kind += moved(4)
         first_y += moved(8)
         first_z += moved(12)
+    for behind in range(2):
+        source = (here_ref, passed_ref)[behind]
+        odds = source[0, place, 64:72, :]
+        for atom in range(4):
+            odd = odds[0:1, 16 + atom : 17 + atom]
+            keep = (odd < 0.5) if behind == 0 else (odd > 0.5)
+            start = pl.multiple_of((place + behind) * 64 + atom * 16, 16)
+            for half in range(2):
+                rows = proj_ref[half, pl.ds(start, 8), :]
+                proj_ref[half, pl.ds(start, 8), :] = jnp.where(keep, rows, 0.0)
+                if behind == 1:
+                    proj_ref[half, pl.ds(start + 8, 8), :] = zero
     gates += pltpu.roll(gates, IMAG, 1)
     kind += pltpu.roll(kind, IMAG, 1)
     for other in range(NPROJ):
@@ -195,40 +226,42 @@
             column = coupling_ref[which][:, other : other + 1]
             value = jnp.where(kind == float(which), column, value)
         table_ref[pl.ds(other * 8, 8), :] = value * gates * gates[other : other + 1, :]
-    sub = lax.broadcasted_iota(i32, (NPROJ, LANES), 0)
     boxes_ref[...] = jnp.where(sub == 0, first_y, first_z).astype(i32)
 
 
 def local_body(
-    index_ref, vector_ref, real_ref, imag_ref, pot_ref, x_ref, y_ref, z_ref, out_ref, turn_ref, high_ref, low_ref
+    index_ref, vector_ref, both_ref, pot_ref, x_ref, y_ref, z_ref, out_ref, turn_ref, high_ref, low_ref
 ):
     slab = index_ref[0]
-    field = jnp.concatenate([real_ref[...], imag_ref[...]], axis=0)
+    field = both_ref[...]
     out = kinetic_yz(field, y_ref, z_ref, vector_ref[1], vector_ref[2])
     pot = pot_ref[...]
     out_ref[...] = out + jnp.concatenate([pot, pot], axis=0) * field
     row = lax.broadcasted_iota(i32, (128, LANES), 0)
-    x = (slab * 2 + row // NY).astype(f32)
     y = (row % NY).astype(f32)
     z = lax.broadcasted_iota(i32, (128, LANES), 1).astype(f32)
-    turns = vector_ref[0] * x / NX + vector_ref[1] * y / NY + vector_ref[2] * z / NZ
-    turns = turns - jnp.floor(turns + 0.5)
-    theta = (2.0 * math.pi) * turns
-    turn_ref[0] = jnp.cos(theta)
-    turn_ref[1] = jnp.sin(theta)
+    for ahead in range(2):
+        x = ((slab + 8 * ahead) % SLABS * 2 + row // NY).astype(f32)
+        turns = vector_ref[0] * x / NX + vector_ref[1] * y / NY + vector_ref[2] * z / NZ
+        turns = turns - jnp.floor(turns + 0.5)
+        theta = (2.0 * math.pi) * turns
+        turn_ref[2 * ahead] = jnp.cos(theta)
+        turn_ref[2 * ahead + 1] = jnp.sin(theta)
     high, low = halves(x_ref[0] + vector_ref[0] * x_ref[1])
     high_ref[...] = high
     low_ref[...] = low
 
 
-def project(boxes_ref, proj_ref, real, imag, turn_ref, field_ref, sums_ref):
-    cosine, sine = turn_ref[0], turn_ref[1]
+def turned_rows(real, imag, cosine, sine, field_ref, first_row):
     turned = (cosine * real - sine * imag, sine * real + cosine * imag)
     for part in range(2):
         for plane in range(2):
-            base = (part * 2 + plane) * 80
+            base = first_row + (part * 2 + plane) * 80
             field_ref[pl.ds(base, 64), :] = turned[part][plane * 64 : plane * 64 + 64]
             field_ref[pl.ds(base + 64, 16), :] = turned[part][plane * 64 : plane * 64 + 16]
+
+
+def project(boxes_ref, proj_ref, wide, far, atoms, field_ref, sums_ref):
     sums_ref[...] = jnp.zeros_like(sums_ref)
     cell = lax.broadcasted_iota(i32, (BOX, LANES), 1) % BOX
 
@@ -238,33 +271,54 @@
         pick = (first_z + (cell + LANES - first_z) % BOX) % LANES
         total = [None, None]
         for plane in range(2):
-            start = pl.multiple_of(atom * 16 + plane * 8, 8)
+            start = pl.multiple_of(atom // 4 * wide + atom % 4 * 16 + plane * 8, 8)
             beta = jnp.concatenate([proj_ref[0, pl.ds(start, 8), :], proj_ref[1, pl.ds(start, 8), :]], axis=0)
+            base = first_y + boxes_ref[2 + plane, atom] if far else first_y
             for part in range(2):
-                rows = field_ref[pl.ds((part * 2 + plane) * 80 + first_y, BOX), :]
+                rows = field_ref[pl.ds((part * 2 + plane) * 80 + base, BOX), :]
                 term = beta * jnp.take_along_axis(rows, pick, axis=1)
                 total[part] = term if plane == 0 else total[part] + term
         for part in range(2):
             sums_ref[pl.ds(part * IMAG + atom, 1), :] = jnp.sum(total[part], axis=0, keepdims=True)
         return carry
 
-    lax.fori_loop(0, 4 * REACH, one, 0, unroll=4)
+    lax.fori_loop(0, atoms, one, 0, unroll=4)
     return lax.dot_general(
         group_matrix(), sums_ref[...], (((1,), (1,)), ((), ())), precision=highest, preferred_element_type=f32
     )
 
 
-def spread(slab, boxes_ref, proj_ref, table_ref, got_ref, turn_ref, place_ref, dual_ref):
-    lane = lax.broadcasted_iota(i32, (NPROJ, LANES), 1)
-    box = (lane % IMAG) // 4
-    coef = jnp.zeros((NPROJ, LANES), f32)
-    for offset in range(1 - REACH, REACH):
-        source = (slab + SLABS + offset) % SLABS
-        share = got_ref[source, 8:16, :]
-        if offset != 0:
-            share = pltpu.roll(share, (-4 * offset) % LANES, 1)
-        sent = box + offset
-        coef += jnp.where((box < REACH) & (sent >= 0) & (sent < REACH), share, 0.0)
+def row_sums(got_ref, row, kept):
+    total = jnp.zeros((NPROJ, LANES), f32)
+    for place in range(8):
+        share = got_ref[row % 4 * 8 + place, 8:16, :]
+        total += share if kept is None else jnp.where(kept(place), share, 0.0)
+    return total
+
+
+def first_coefs(slab, got_ref):
+    group = lax.broadcasted_iota(i32, (NPROJ, LANES), 1) % IMAG // 4
+    own = row_sums(got_ref, slab // 8, None)
+    before = row_sums(got_ref, slab // 8 + 3, None)
+    return jnp.where(group <= slab % 8, own, pltpu.roll(before, 4, 1))
+
+
+def second_coefs(slab, got_ref):
+    group = lax.broadcasted_iota(i32, (NPROJ, LANES), 1) % IMAG // 4
+    row = slab // 8
+
+    def own(place):
+        return group <= place
+
+    def passed(place):
+        return (group > place) & (group < REACH)
+
+    here = row_sums(got_ref, row, own) + pltpu.roll(row_sums(got_ref, row + 1, passed), LANES - 4, 1)
+    before = pltpu.roll(row_sums(got_ref, row + 3, own), 4, 1) + row_sums(got_ref, row, passed)
+    return jnp.where(group <= slab % 8, here, jnp.where(group < REACH, before, 0.0))
+
+
+def spread(coef, boxes_ref, proj_ref, table_ref, turn_ref, place_ref, dual_ref):
     dual = jnp.zeros((NPROJ, LANES), f32)
     for other in range(NPROJ):
         dual += table_ref[pl.ds(other * 8, 8), :] * coef[other : other + 1, :]
@@ -325,12 +379,13 @@
                 field_ref[pl.ds(start, SLABS, stride=2), :] = got_ref[:, first_row + row, :]
 
 
-def coef_body(boxes_ref, proj_ref, real_ref, imag_ref, turn_ref, out_ref, whole_ref, field_ref, sums_ref):
-    real, imag = real_ref[...], imag_ref[...]
-    whole_ref[0:128, :] = real
-    whole_ref[128:256, :] = imag
-    columns(whole_ref, out_ref)
-    coef = project(boxes_ref, proj_ref, real, imag, turn_ref, field_ref, sums_ref)
+def coef_body(boxes_ref, proj_ref, both_ref, next_ref, turn_ref, out_ref, field_ref, sums_ref):
+    columns(both_ref, out_ref)
+    for ahead, ref in enumerate((both_ref, next_ref)):
+        turned_rows(
+            ref[0:128, :], ref[128:256, :], turn_ref[2 * ahead], turn_ref[2 * ahead + 1], field_ref, 320 * ahead
+        )
+    coef = project(boxes_ref, proj_ref, 72, True, 32, field_ref, sums_ref)
     out_ref[:, 8:16, :] = jnp.broadcast_to(coef[None], (SLABS, 8, LANES))
 
 
@@ -342,9 +397,8 @@
     moved = kinetic_x(field, high_ref, low_ref, vector_ref[0])
     moved_ref[...] = moved
     out_ref[:, 8:16, :] = moved.reshape(SLABS, 8, LANES)
-    far_real, far_imag = spread(
-        index_ref[0], boxes_ref, proj_ref, table_ref, got_ref, turn_ref, place_ref, dual_ref
-    )
+    coef = first_coefs(index_ref[0], got_ref)
+    far_real, far_imag = spread(coef, boxes_ref, proj_ref, table_ref, turn_ref, place_ref, dual_ref)
     rest_ref[0:128, :] = local_ref[0:128, :] + far_real
     rest_ref[128:256, :] = local_ref[128:256, :] + far_imag
     columns(rest_ref, out_ref)
@@ -361,7 +415,8 @@
     imag = first_ref[128:256, :] + rest_ref[128:256, :]
     first_ref[0:128, :] = real
     first_ref[128:256, :] = imag
-    coef = project(boxes_ref, proj_ref, real, imag, turn_ref, field_ref, sums_ref)
+    turned_rows(real, imag, turn_ref[0], turn_ref[1], field_ref, 0)
+    coef = project(boxes_ref, proj_ref, 64, False, 4 * REACH, field_ref, sums_ref)
     out_ref[:, 8:16, :] = jnp.broadcast_to(coef[None], (SLABS, 8, LANES))
 
 
@@ -373,18 +428,17 @@
 
 
 def final_body(
-    index_ref, occupation_ref, boxes_ref, proj_ref, table_ref, got_ref, turn_ref, real_ref, imag_ref, first_ref,
-    near_ref, new_real_ref, new_imag_ref, out_ref, field_ref, place_ref, dual_ref,
+    index_ref, occupation_ref, boxes_ref, proj_ref, table_ref, got_ref, turn_ref, both_ref, first_ref, near_ref,
+    new_real_ref, new_imag_ref, out_ref, field_ref, place_ref, dual_ref,
 ):
     unpack(got_ref, 0, field_ref)
-    far_real, far_imag = spread(
-        index_ref[0], boxes_ref, proj_ref, table_ref, got_ref, turn_ref, place_ref, dual_ref
-    )
+    coef = second_coefs(index_ref[0], got_ref)
+    far_real, far_imag = spread(coef, boxes_ref, proj_ref, table_ref, turn_ref, place_ref, dual_ref)
     half = 0.5 * time_step * time_step
     second_real = near_ref[0:128, :] + field_ref[0:128, :] + far_real
     second_imag = near_ref[128:256, :] + field_ref[128:256, :] + far_imag
-    new_real = real_ref[...] + time_step * first_ref[128:256, :] - half * second_real
-    new_imag = imag_ref[...] - time_step * first_ref[0:128, :] - half * second_imag
+    new_real = both_ref[0:128, :] + time_step * first_ref[128:256, :] - half * second_real
+    new_imag = both_ref[128:256, :] - time_step * first_ref[0:128, :] - half * second_imag
     new_real_ref[...] = new_real
     new_imag_ref[...] = new_imag
     weighted = occupation_ref[0] * (new_real * new_real + new_imag * new_imag)
@@ -434,30 +488,41 @@
     square = pltpu.VMEM((128, LANES), f32)
     whole = pltpu.VMEM((256, LANES), f32)
 
-    own, near = call(
-        pack_body, (index, box_offsets, species, channels), (projectors,),
-        (shape(520, LANES), shape(64, LANES)), (pltpu.VMEM((640, LANES), f32),),
-    )
-    passed = lax.ppermute(own, "fft", [(i, (i + 8) % SLABS) for i in range(SLABS)])
-    local, turn, high, low = call(
-        local_body, (index, vector_potential), (real, imag, pot, x_table, y_table, z_table),
-        (shape(256, LANES), shape(2, 128, LANES), matrix, matrix),
-    )
-    slices, last = call(
-        route_body, (index,), (own, near, passed), (shape(8, 72, LANES), shape(72, LANES))
-    )
+    anywhere = pl.BlockSpec(memory_space=pltpu.HBM)
+    slices, both = pl.pallas_call(
+        pack_body,
+        out_shape=(shape(8, 72, LANES), shape(256, LANES)),
+        in_specs=[smem()] + [anywhere] * 6,
+        out_specs=(vmem(), vmem()),
+        scratch_shapes=[
+            pltpu.SMEM((3, 4), i32), pltpu.SMEM((4,), i32), pltpu.SMEM((4, 8), i32),
+            pltpu.VMEM((4, 8, 4096), f32), pltpu.VMEM((136, LANES), f32), pltpu.SemaphoreType.DMA((9,)),
+        ],
+        compiler_params=pltpu.CompilerParams(vmem_limit_bytes=60 * 1024 * 1024),
+    )(index, box_offsets, species, channels, projectors, real, imag)
+    ahead = lax.ppermute(both, "fft", [(i, (i + 24) % SLABS) for i in range(SLABS)])
     rows = [list(range(8 * x, 8 * x + 8)) for x in range(4)]
     got = lax.all_to_all(slices, "fft", split_axis=0, concat_axis=0, tiled=True, axis_index_groups=rows)
-    picked, table, boxes = call(
-        pick_body, (index,), (got, last, coupling),
-        (shape(576, LANES), shape(64, LANES), shape(8, LANES, dtype=i32)),
-    )
+    local, turn, high, low = call(
+        local_body, (index, vector_potential), (both, pot, x_table, y_table, z_table),
+        (shape(256, LANES), shape(4, 128, LANES), matrix, matrix),
+    )
+    got, ahead, local, turn, high, low = lax.optimization_barrier((got, ahead, local, turn, high, low))
     chips = [[2 * y, 2 * y + 1] for y in range(8)]
-    beta = lax.all_gather(picked, "band", axis_index_groups=chips)
+    gathered = lax.all_gather(got, "band", axis_index_groups=chips)
+    corners = call(pick_body, (index,), (got,), shape(8, LANES, dtype=i32))
+    passed = lax.ppermute(got, "fft", [(i, (i + 8) % SLABS) for i in range(SLABS)])
     shares = call(
-        coef_body, (boxes,), (beta, real, imag, turn), shape(SLABS, 16, LANES), (whole, window, square)
-    )
+        coef_body, (corners,), (gathered.reshape(2, 576, LANES), both, ahead, turn), shape(SLABS, 16, LANES),
+        (pltpu.VMEM((640, LANES), f32), square),
+    )
+    shares, passed = lax.optimization_barrier((shares, passed))
+    passed = lax.all_gather(passed, "band", axis_index_groups=chips)
     got = exchange(shares, "fft")
+    beta, table, boxes = call(
+        merge_body, (index,), (gathered, passed, coupling),
+        (shape(2, 576, LANES), shape(64, LANES), shape(8, LANES, dtype=i32)),
+    )
     rest, moved, shares = call(
         rest_body, (index, vector_potential, boxes), (beta, table, got, turn, local, high, low),
         (shape(256, LANES), shape(256, LANES), shape(SLABS, 16, LANES)), (window, square),
@@ -470,7 +535,7 @@
     got = exchange(shares, "fft")
     near = call(second_body, (vector_potential,), (first, pot, y_table, z_table), shape(256, LANES))
     new_real, new_imag, weighted = call(
-        final_body, (index, occupation, boxes), (beta, table, got, turn, real, imag, first, near),
+        final_body, (index, occupation, boxes), (beta, table, got, turn, both, first, near),
         (shape(128, LANES), shape(128, LANES), shape(BANDS, 8, LANES)), (whole, window, square),
     )
     density = jnp.sum(exchange(weighted, "band"), axis=0).reshape(2, 4, LANES)

time: 118 us -> 111 us (0.941)
  blocking collectives: 52.3 us -> 42.1 us
  starting transfers between devices: 22.5 us -> 29.3 us
  local copies, waits for them, and re-layouts: 4.58 us -> 1.07 us
  waiting for transfers between devices: 20.8 us -> 18 us
  Pallas kernels: 14.9 us -> 17.5 us
    all_to_all x3 -> x2, blocking collectives: 47.2 us -> 34.9 us  [exchange(): return lax.all_to_all(value, axis, split_axis=0, concat_axis=0, tiled=True)]
    all_to_all x1 -> x2, waiting for transfers between devices: 8.13 us -> 13.7 us  [exchange(): return lax.all_to_all(value, axis, split_axis=0, concat_axis=0, tiled=True)]
    ppermute x1 -> x2, waiting for transfers between devices: 5.06 us -> 0.01 us  [the longest x1 0.01 us: per_device(): lax.ppermute(both, 'fft', [(i, (i + 24) % SLABS) for i in range(SLABS)])]
    all_to_all x1 -> x2, starting transfers between devices: 6.23 us -> 10.8 us  [exchange(): return lax.all_to_all(value, axis, split_axis=0, concat_axis=0, tiled=True)]
    ppermute x1 -> x2, starting transfers between devices: 3.95 us -> 7.49 us  [the longest x1 4.39 us: per_device(): lax.ppermute(both, 'fft', [(i, (i + 24) % SLABS) for i in range(SLABS)])]
    unnamed x26 -> x16, local copies, waits for them, and re-layouts: 4.58 us -> 1.07 us
    all_to_all x1, waiting for transfers between devices: 7.65 us -> 4.24 us  [per_device(): lax.all_to_all(slices, 'fft', split_axis=0, concat_axis=0, tiled=True, ax...]
    pallas_call x0 -> x1, Pallas kernels: none -> 3.2 us  [per_device(): pl.pallas_call(pack_body, out_shape=(shape(8, 72, LANES), shape(256, LANE...]
  transfers between devices with their start and end apart: 3 -> 5, of which waited for: 3 -> 3; matrix products, arithmetic and copies ran while one was open for 0% -> 0% of each run, Pallas kernels for 2% -> 6%
where the time goes in v3:
time: 111 us
  blocking collectives  42.1 us (38%)
  starting transfers between devices  29.3 us (26%)
  waiting for transfers between devices  18 us (16%)
  Pallas kernels  17.5 us (16%)
  between operations  1.47 us (1%)
  other arithmetic  1.2 us (1%)
    all_to_all x2, blocking collectives, exchange(): return lax.all_to_all(value, axis, split_axis=0, concat_axis=0, tiled=True)  34.9 us
    pallas_call x8, Pallas kernels, call(): pl.pallas_call(body, out_shape=outs, in_specs=[smem()] * len(scalars) + [...  14.3 us
    all_to_all x2, waiting for transfers between devices, exchange(): return lax.all_to_all(value, axis, split_axis=0, concat_axis=0, tiled=True)  13.7 us
    all_to_all x1, starting transfers between devices, per_device(): lax.all_to_all(slices, 'fft', split_axis=0, concat_axis=0, tiled=True, ax...  11 us
    all_to_all x2, starting transfers between devices, exchange(): return lax.all_to_all(value, axis, split_axis=0, concat_axis=0, tiled=True)  10.8 us
    all_gather x1, blocking collectives, per_device(): gathered = lax.all_gather(got, 'band', axis_index_groups=chips)  4.5 us
    ppermute x1, starting transfers between devices, per_device(): lax.ppermute(both, 'fft', [(i, (i + 24) % SLABS) for i in range(SLABS)])  4.39 us
    all_to_all x1, waiting for transfers between devices, per_device(): lax.all_to_all(slices, 'fft', split_axis=0, concat_axis=0, tiled=True, ax...  4.24 us
  transfers between devices with their start and end apart: 5, of which 3 were waited for; matrix products, arithmetic and copies ran while one was open for 0% of the time, Pallas kernels for 6%

profile of v3, /device:TPU:1, one launch (start us, length us, event | category | flops | bytes accessed | tf_op | source)
XLA Modules:
  0.0 110.6 jit_solution(10429791177706274486)
XLA Ops:
  0.6 0.6 pad_add_fusion.index_ref
  1.2 0.0 copy-start
  1.2 0.0 copy-start.1
  1.2 3.2 %shard_map.148 = (f32[8,72,128]{2,1,0:T(8,128)}, f32[256,128]{1,0:T(8,128)}) custom-call(s32[2]{0:T(128)} %pad_add_fusion.index_ref, s32[3,4]{1,0:T(4,128)} %boxes_hbm.1, s32[4]{0:T(128)} %species_hbm.1, s32[4,8]{1,0:T(4,128)} %channels_hbm.1, f32[4,8,4096]{2,1,0:T(8,128)} %proj_hbm.1, f32[128,128]{1,0:T(8,128)} %bitcast.16, f32[128,128]{1,0:T(8,128)} %bitcast.17), custom_call_target="tpu_custom_call" | custom-call | tf_op jit(solution)/shard_map/pallas_call | solution.py:492
  4.4 0.0 copy-start.2
  4.4 0.0 copy-start.4
  4.5 11.0 %all-to-all-start = ((f32[8,72,128]{2,1,0:T(8,128)}), f32[8,72,128]{2,1,0:T(8,128)S(1)}, u32[]{:S(2)}, u32[]{:S(2)}) async-start(f32[8,72,128]{2,1,0:T(8,128)} %get-tuple-element.28), calls=%async_computation | async-start | bytes 589824 | tf_op jit(solution)/shard_map/all_to_all | solution.py:505
  15.5 0.0 copy-done.2
  15.5 0.0 copy-start.5
  15.5 0.0 copy-start.7
  15.5 4.4 %collective-permute-start = (f32[256,128]{1,0:T(8,128)S(1)}, f32[256,128]{1,0:T(8,128)S(1)}, u32[]{:S(2)}, u32[]{:S(2)}) collective-permute-start(f32[256,128]{1,0:T(8,128)S(1)} %copy-done.2), channel_id=1, source_target_pairs={{0,384},{16,400},{32,416},{48,432},{64,448},{80,464},{96,480},{112... | collective-permute-start | bytes 393224 | tf_op jit(solution)/shard_map/ppermute | solution.py:503
  19.9 0.0 copy-done
  19.9 0.0 copy-done.1
  19.9 0.0 copy-done.4
  19.9 0.0 copy-done.5
  19.9 0.0 copy-done.7
  19.9 0.0 copy-start.3
  20.0 1.0 copy-done.3
  21.0 1.4 %shard_map.149 = (f32[256,128]{1,0:T(8,128)S(1)}, f32[4,128,128]{2,1,0:T(8,128)S(1)}, bf16[256,256]{1,0:T(8,128)(2,1)S(1)}, bf16[256,256]{1,0:T(8,128)(2,1)S(1)}) custom-call(s32[2]{0:T(128)S(1)} %copy-done.5, f32[3]{0:T(128)S(1)} %copy-done.7, f32[256,128]{1,0:T(8,128)S(1)} %copy-done.2, f32[128,128]{1,0:T(8,128)S(1)} %bitcast.14, ...), custom_call_target="tpu_custom_call" | custom-call | tf_op jit(solution)/shard_map/pallas_call | solution.py:460
  22.4 0.0 collective-permute-done.next_ref
  22.4 4.2 %all-to-all-done.got_ref = f32[8,72,128]{2,1,0:T(8,128)S(1)} async-done(((f32[8,72,128]{2,1,0:T(8,128)}), f32[8,72,128]{2,1,0:T(8,128)S(1)}, u32[]{:S(2)}, u32[]{:S(2)}) %all-to-all-start) | async-done | bytes 294944 | tf_op jit(solution)/shard_map/all_to_all | solution.py:505
  26.6 3.1 %collective-permute-start.1 = (f32[8,72,128]{2,1,0:T(8,128)S(1)}, f32[8,72,128]{2,1,0:T(8,128)S(1)}, u32[]{:S(2)}, u32[]{:S(2)}) collective-permute-start(f32[8,72,128]{2,1,0:T(8,128)S(1)} %all-to-all-done.got_ref), channel_id=1, source_target_pairs={{0,128},{16,144},{32,160},{48,176},{64,192},{80,208},{96,224},{112... | collective-permute-start | bytes 884744 | tf_op jit(solution)/shard_map/ppermute | solution.py:514
  29.7 0.6 shard_map.150.boxes_ref
  30.4 4.5 %all-gather = f32[16,72,128]{2,1,0:T(8,128)S(1)} all-gather(f32[8,72,128]{2,1,0:T(8,128)S(1)} %all-to-all-done.got_ref), channel_id=2, replica_groups={{0,1},{2,3},{4,5},{6,7},{8,9},{10,11},{12,13},{14,15},{16,17},{18,19},{..., dimensions={0}, use_global_device_ids=true | all-gather | bytes 884736 | tf_op jit(solution)/shard_map/all_gather | solution.py:512
  34.9 2.8 %shard_map.151 = f32[32,16,128]{2,1,0:T(8,128)} custom-call(s32[8,128]{1,0:T(8,128)S(1)} %shard_map.150.boxes_ref, f32[2,576,128]{2,1,0:T(8,128)S(1)} %bitcast.11, f32[256,128]{1,0:T(8,128)S(1)} %copy-done.2, f32[256,128]{1,0:T(8,128)S(1)} %collective-permute-done.next_ref, f32[4,128,128]{2,1,0:T(8,128)S(1)} %get-tuple-element.36.turn_ref), custom_call_target="tpu_custom_call" | custom-call | tf_op jit(solution)/shard_map/pallas_call | solution.py:460
  37.7 0.0 collective-permute-done.1
  37.7 5.1 %all-to-all-start.1 = ((f32[32,16,128]{2,1,0:T(8,128)}), f32[32,16,128]{2,1,0:T(8,128)S(1)}, u32[]{:S(2)}, u32[]{:S(2)}) async-start(f32[32,16,128]{2,1,0:T(8,128)} %shard_map.151), calls=%async_computation.1 | async-start | bytes 524288 | tf_op jit(solution)/shard_map/all_to_all | solution.py:475
  42.8 0.0 copy-start.6
  42.8 2.7 %all-gather.1 = f32[16,72,128]{2,1,0:T(8,128)S(1)} all-gather(f32[8,72,128]{2,1,0:T(8,128)S(1)} %collective-permute-done.1), channel_id=3, replica_groups={{0,1},{2,3},{4,5},{6,7},{8,9},{10,11},{12,13},{14,15},{16,17},{18,19},{..., dimensions={0}, use_global_device_ids=true | all-gather | bytes 884736 | tf_op jit(solution)/shard_map/all_gather | solution.py:520
  45.5 0.0 copy-done.6
  45.5 1.4 %shard_map.152 = (f32[2,576,128]{2,1,0:T(8,128)S(1)}, f32[64,128]{1,0:T(8,128)S(1)}, s32[8,128]{1,0:T(8,128)S(1)}) custom-call(s32[2]{0:T(128)S(1)} %copy-done.5, f32[2,8,72,128]{3,2,1,0:T(8,128)S(1)} %bitcast.12, f32[2,8,72,128]{3,2,1,0:T(8,128)S(1)} %bitcast.13, f32[4,8,8]{2,1,0:T(8,128)S(1)} %copy-done.6), custom_call_target="tpu_custom_call" | custom-call | tf_op jit(solution)/shard_map/pallas_call | solution.py:460
  46.9 5.6 %all-to-all-done.1.got_ref = f32[32,16,128]{2,1,0:T(8,128)S(1)} async-done(((f32[32,16,128]{2,1,0:T(8,128)}), f32[32,16,128]{2,1,0:T(8,128)S(1)}, u32[]{:S(2)}, u32[]{:S(2)}) %all-to-all-start.1) | async-done | bytes 262176 | tf_op jit(solution)/shard_map/all_to_all | solution.py:475
  52.5 1.7 %shard_map.153 = (f32[256,128]{1,0:T(8,128)S(1)}, f32[256,128]{1,0:T(8,128)S(1)}, f32[32,16,128]{2,1,0:T(8,128)S(1)}) custom-call(s32[2]{0:T(128)S(1)} %copy-done.5, f32[3]{0:T(128)S(1)} %copy-done.7, s32[8,128]{1,0:T(8,128)S(1)} %get-tuple-element.38.boxes_ref, f32[2,576,128]{2,1,0:T(8,128)S(1)} %get-tuple-element.39.proj_ref, ...), custom_call_target="tpu_custom_call" | custom-call | tf_op jit(solution)/shard_map/pallas_call | solution.py:460
  54.2 15.8 %all_to_all.25.got_ref = f32[32,16,128]{2,1,0:T(8,128)S(1)} all-to-all(f32[32,16,128]{2,1,0:T(8,128)S(1)} %get-tuple-element.45), channel_id=1, replica_groups=mesh['fft'=32,'band'=16] {'fft'}, dimensions={0} | all-to-all | bytes 524288 | tf_op jit(solution)/shard_map/all_to_all | solution.py:475
  70.0 3.3 %shard_map.154 = (f32[256,128]{1,0:T(8,128)S(1)}, f32[32,16,128]{2,1,0:T(8,128)}) custom-call(f32[3]{0:T(128)S(1)} %copy-done.7, s32[8,128]{1,0:T(8,128)S(1)} %get-tuple-element.38.boxes_ref, f32[2,576,128]{2,1,0:T(8,128)S(1)} %get-tuple-element.39.proj_ref, f32[32,16,128]{2,1,0:T(8,128)S(1)} %all_to_all.25.got_ref, ...), custom_call_target="tpu_custom_call" | custom-call | tf_op jit(solution)/shard_map/pallas_call | solution.py:460
  73.2 5.7 %all-to-all-start.3 = ((f32[32,16,128]{2,1,0:T(8,128)}), f32[32,16,128]{2,1,0:T(8,128)S(1)}, u32[]{:S(2)}, u32[]{:S(2)}) async-start(f32[32,16,128]{2,1,0:T(8,128)} %get-tuple-element.48), calls=%async_computation.3 | async-start | bytes 524288 | tf_op jit(solution)/shard_map/all_to_all | solution.py:475
  79.6 0.9 shard_map.155.near_ref
  80.5 8.1 %all-to-all-done.3.got_ref = f32[32,16,128]{2,1,0:T(8,128)S(1)} async-done(((f32[32,16,128]{2,1,0:T(8,128)}), f32[32,16,128]{2,1,0:T(8,128)S(1)}, u32[]{:S(2)}, u32[]{:S(2)}) %all-to-all-start.3) | async-done | bytes 262176 | tf_op jit(solution)/shard_map/all_to_all | solution.py:475
  88.6 2.3 %shard_map.156 = (f32[128,128]{1,0:T(8,128)}, f32[128,128]{1,0:T(8,128)}, f32[16,8,128]{2,1,0:T(8,128)S(1)}) custom-call(s32[2]{0:T(128)S(1)} %copy-done.5, f32[1]{0:T(128)S(6)} %copy.16.occupation_ref, s32[8,128]{1,0:T(8,128)S(1)} %get-tuple-element.38.boxes_ref, f32[2,576,128]{2,1,0:T(8,128)S(1)} %get-tuple-element.39.proj_ref, ...), custom_call_target="tpu_custom_call" | custom-call | tf_op jit(solution)/shard_map/pallas_call | solution.py:460
  90.9 19.1 %all_to_all.26 = f32[16,8,128]{2,1,0:T(8,128)S(1)} all-to-all(f32[16,8,128]{2,1,0:T(8,128)S(1)} %get-tuple-element.52), channel_id=1, replica_groups=mesh['fft'=32,'band'=16] {'band'}, dimensions={0} | all-to-all | bytes 131072 | tf_op jit(solution)/shard_map/all_to_all | solution.py:475
  110.0 0.6 reduce_sum.9
Async XLA Ops:
  1.2 18.7 %copy-start = (f32[2,256,256]{2,1,0:T(8,128)S(1)}, f32[2,256,256]{2,1,0:T(8,128)}, u32[]{:S(2)}) copy-start(f32[2,256,256]{2,1,0:T(8,128)} %constant.18.clone.y_ref) | copy-start | bytes 1572868
  1.2 18.7 %copy-start.1 = (f32[2,256,256]{2,1,0:T(8,128)S(1)}, f32[2,256,256]{2,1,0:T(8,128)}, u32[]{:S(2)}) copy-start(f32[2,256,256]{2,1,0:T(8,128)} %constant.19.clone.z_ref) | copy-start | bytes 1572868
  4.4 11.0 %copy-start.2 = (f32[256,128]{1,0:T(8,128)S(1)}, f32[256,128]{1,0:T(8,128)}, u32[]{:S(2)}) copy-start(f32[256,128]{1,0:T(8,128)} %get-tuple-element.29.both_ref) | copy-start | bytes 393220
  4.4 15.5 %copy-start.4 = (f32[2,64,128]{2,1,0:T(8,128)S(1)}, f32[2,64,128]{2,1,0:T(8,128)}, u32[]{:S(2)}) copy-start(f32[2,64,128]{2,1,0:T(8,128)} %param.15) | copy-start | bytes 196612
  4.5 22.2 %all-to-all-start = ((f32[8,72,128]{2,1,0:T(8,128)}), f32[8,72,128]{2,1,0:T(8,128)S(1)}, u32[]{:S(2)}, u32[]{:S(2)}) async-start(f32[8,72,128]{2,1,0:T(8,128)} %get-tuple-element.28), calls=%async_computation | async-start | bytes 589824 | tf_op jit(solution)/shard_map/all_to_all | solution.py:505
  15.5 4.5 %copy-start.5 = (s32[2]{0:T(128)S(1)}, s32[2]{0:T(128)}, u32[]{:S(2)}) copy-start(s32[2]{0:T(128)} %pad_add_fusion.index_ref) | copy-start | bytes 28
  15.5 4.4 %copy-start.7 = (f32[3]{0:T(128)S(1)}, f32[3]{0:T(128)}, u32[]{:S(2)}) copy-start(f32[3]{0:T(128)} %vector_ref.7) | copy-start | bytes 40
  15.5 6.9 %collective-permute-start = (f32[256,128]{1,0:T(8,128)S(1)}, f32[256,128]{1,0:T(8,128)S(1)}, u32[]{:S(2)}, u32[]{:S(2)}) collective-permute-start(f32[256,128]{1,0:T(8,128)S(1)} %copy-done.2), channel_id=1, source_target_pairs={{0,384},{16,400},{32,416},{48,432},{64,448},{80,464},{96,480},{112... | collective-permute-start | bytes 393224 | tf_op jit(solution)/shard_map/ppermute | solution.py:503
  19.9 1.0 copy-start.3
  26.6 11.0 %collective-permute-start.1 = (f32[8,72,128]{2,1,0:T(8,128)S(1)}, f32[8,72,128]{2,1,0:T(8,128)S(1)}, u32[]{:S(2)}, u32[]{:S(2)}) collective-permute-start(f32[8,72,128]{2,1,0:T(8,128)S(1)} %all-to-all-done.got_ref), channel_id=1, source_target_pairs={{0,128},{16,144},{32,160},{48,176},{64,192},{80,208},{96,224},{112... | collective-permute-start | bytes 884744 | tf_op jit(solution)/shard_map/ppermute | solution.py:514
  37.7 14.8 %all-to-all-start.1 = ((f32[32,16,128]{2,1,0:T(8,128)}), f32[32,16,128]{2,1,0:T(8,128)S(1)}, u32[]{:S(2)}, u32[]{:S(2)}) async-start(f32[32,16,128]{2,1,0:T(8,128)} %shard_map.151), calls=%async_computation.1 | async-start | bytes 524288 | tf_op jit(solution)/shard_map/all_to_all | solution.py:475
  42.8 2.7 %copy-start.6 = (f32[4,8,8]{2,1,0:T(8,128)S(1)}, f32[4,8,8]{2,1,0:T(8,128)}, u32[]{:S(2)}) copy-start(f32[4,8,8]{2,1,0:T(8,128)} %coupling_ref.1) | copy-start | bytes 3076
  73.2 15.4 %all-to-all-start.3 = ((f32[32,16,128]{2,1,0:T(8,128)}), f32[32,16,128]{2,1,0:T(8,128)S(1)}, u32[]{:S(2)}, u32[]{:S(2)}) async-start(f32[32,16,128]{2,1,0:T(8,128)} %get-tuple-element.48), calls=%async_computation.3 | async-start | bytes 524288 | tf_op jit(solution)/shard_map/all_to_all | solution.py:475

commit v4 on v3

--- a/solution.py
+++ b/solution.py
@@ -104,11 +104,11 @@
 
 
 def pack_body(
-    index_ref, boxes_hbm, species_hbm, channels_hbm, proj_hbm, real_hbm, imag_hbm, out_ref, both_ref,
+    boxes_hbm, species_hbm, channels_hbm, proj_hbm, real_hbm, imag_hbm, out_ref, both_ref,
     boxes_ref, species_ref, channels_ref, proj_ref, rows_ref, done,
 ):
-    place = index_ref[0] % 8
-    core = index_ref[1] % 2
+    place = lax.axis_index("fft") % 8
+    core = lax.axis_index("band") % 2
     copies = [
         pltpu.make_async_copy(boxes_hbm, boxes_ref, done.at[0]),
         pltpu.make_async_copy(species_hbm, species_ref, done.at[1]),
@@ -125,8 +125,8 @@
     lane = lax.broadcasted_iota(i32, (NPROJ, LANES), 1)
     cell = lane % BOX
     group = lane // BOX
-    skew = (group + sub) % 8 * BOX + cell
-    shift = (sub - group) % 8
+    skew = ((group + sub) & 7) * BOX + cell
+    shift = (sub - group) & 7
     for copy in copies[:3]:
         copy.wait()
     facts = jnp.zeros((NPROJ, LANES), f32)
@@ -137,12 +137,12 @@
         facts = jnp.where(lane == 4 + atom, species_ref[atom].astype(f32), facts)
         facts = jnp.where(lane == 8 + atom, boxes_ref[1, atom].astype(f32), facts)
         facts = jnp.where(lane == 12 + atom, boxes_ref[2, atom].astype(f32), facts)
-        facts = jnp.where(lane == 16 + atom, (boxes_ref[0, atom] % 2).astype(f32), facts)
+        facts = jnp.where(lane == 16 + atom, ((boxes_ref[0, atom] & 1)).astype(f32), facts)
     for target in range(8):
         out_ref[target, 64:72, :] = facts
     for atom in range(4):
         copies[3 + atom].wait()
-        last = shift * BOX + (cell + 256 - boxes_ref[2, atom]) % BOX
+        last = shift * BOX + ((cell - boxes_ref[2, atom]) & (BOX - 1))
         for cut in range(BOX):
             start = pl.multiple_of((2 * cut + core) * LANES, LANES)
             tile = proj_ref[atom, :, pl.ds(start, LANES)]
@@ -152,16 +152,16 @@
             rows_ref[pl.ds(cut * 8, 8), :] = tile
             if cut == 0:
                 rows_ref[pl.ds(128, 8), :] = tile
-        odd = boxes_ref[0, atom] % 2
+        odd = (boxes_ref[0, atom] & 1)
         for target in range(8):
-            start = (2 * (target - place) - odd + 32) % BOX
+            start = (2 * (target - place) - odd) & (BOX - 1)
             out_ref[target, pl.ds(atom * 16, 16), :] = rows_ref[pl.ds(pl.multiple_of(start * 8, 8), 16), :]
     for copy in copies[7:]:
         copy.wait()
 
 
-def pick_body(index_ref, got_ref, boxes_ref):
-    place = index_ref[0] % 8
+def pick_body(got_ref, boxes_ref):
+    place = lax.axis_index("fft") % 8
     lane = lax.broadcasted_iota(i32, (NPROJ, LANES), 1)
     sub = lax.broadcasted_iota(i32, (NPROJ, LANES), 0)
     found = jnp.zeros((NPROJ, LANES), f32)
@@ -175,8 +175,8 @@
     boxes_ref[...] = jnp.where(sub < 2, found.astype(i32), jnp.where(far, 320, 0))
 
 
-def merge_body(index_ref, here_ref, passed_ref, coupling_ref, proj_ref, table_ref, boxes_ref):
-    place = index_ref[0] % 8
+def merge_body(here_ref, passed_ref, coupling_ref, proj_ref, table_ref, boxes_ref):
+    place = lax.axis_index("fft") % 8
     lane = lax.broadcasted_iota(i32, (NPROJ, LANES), 1)
     sub = lax.broadcasted_iota(i32, (NPROJ, LANES), 0)
     zero = jnp.zeros((NPROJ, LANES), f32)
@@ -229,14 +229,8 @@
     boxes_ref[...] = jnp.where(sub == 0, first_y, first_z).astype(i32)
 
 
-def local_body(
-    index_ref, vector_ref, both_ref, pot_ref, x_ref, y_ref, z_ref, out_ref, turn_ref, high_ref, low_ref
-):
-    slab = index_ref[0]
-    field = both_ref[...]
-    out = kinetic_yz(field, y_ref, z_ref, vector_ref[1], vector_ref[2])
-    pot = pot_ref[...]
-    out_ref[...] = out + jnp.concatenate([pot, pot], axis=0) * field
+def phase_body(vector_ref, turn_ref):
+    slab = lax.axis_index("fft")
     row = lax.broadcasted_iota(i32, (128, LANES), 0)
     y = (row % NY).astype(f32)
     z = lax.broadcasted_iota(i32, (128, LANES), 1).astype(f32)
@@ -247,6 +241,15 @@
         theta = (2.0 * math.pi) * turns
         turn_ref[2 * ahead] = jnp.cos(theta)
         turn_ref[2 * ahead + 1] = jnp.sin(theta)
+
+
+def local_body(
+    vector_ref, both_ref, pot_ref, x_ref, y_ref, z_ref, out_ref, high_ref, low_ref
+):
+    field = both_ref[...]
+    out = kinetic_yz(field, y_ref, z_ref, vector_ref[1], vector_ref[2])
+    pot = pot_ref[...]
+    out_ref[...] = out + jnp.concatenate([pot, pot], axis=0) * field
     high, low = halves(x_ref[0] + vector_ref[0] * x_ref[1])
     high_ref[...] = high
     low_ref[...] = low
@@ -268,7 +271,7 @@
     def one(atom, carry):
         first_y = boxes_ref[0, atom]
         first_z = boxes_ref[1, atom]
-        pick = (first_z + (cell + LANES - first_z) % BOX) % LANES
+        pick = (first_z + ((cell - first_z) & (BOX - 1))) & (LANES - 1)
         total = [None, None]
         for plane in range(2):
             start = pl.multiple_of(atom // 4 * wide + atom % 4 * 16 + plane * 8, 8)
@@ -282,7 +285,7 @@
             sums_ref[pl.ds(part * IMAG + atom, 1), :] = jnp.sum(total[part], axis=0, keepdims=True)
         return carry
 
-    lax.fori_loop(0, atoms, one, 0, unroll=4)
+    lax.fori_loop(0, atoms, one, 0, unroll=True)
     return lax.dot_general(
         group_matrix(), sums_ref[...], (((1,), (1,)), ((), ())), precision=highest, preferred_element_type=f32
     )
@@ -344,7 +347,7 @@
         for atom in range(4 * distance, 4 * distance + 4):
             first_y = boxes_ref[0, atom]
             first_z = boxes_ref[1, atom]
-            inside = (wide + LANES - first_z) % LANES < BOX
+            inside = ((wide - first_z) & (LANES - 1)) < BOX
             for plane in range(2):
                 parts = []
                 for half in range(2):
@@ -390,14 +393,14 @@
 
 
 def rest_body(
-    index_ref, vector_ref, boxes_ref, proj_ref, table_ref, got_ref, turn_ref, local_ref, high_ref, low_ref,
+    vector_ref, boxes_ref, proj_ref, table_ref, got_ref, turn_ref, local_ref, high_ref, low_ref,
     rest_ref, moved_ref, out_ref, place_ref, dual_ref,
 ):
     field = got_ref[:, 0:8, :].reshape(256, LANES)
     moved = kinetic_x(field, high_ref, low_ref, vector_ref[0])
     moved_ref[...] = moved
     out_ref[:, 8:16, :] = moved.reshape(SLABS, 8, LANES)
-    coef = first_coefs(index_ref[0], got_ref)
+    coef = first_coefs(lax.axis_index("fft"), got_ref)
     far_real, far_imag = spread(coef, boxes_ref, proj_ref, table_ref, turn_ref, place_ref, dual_ref)
     rest_ref[0:128, :] = local_ref[0:128, :] + far_real
     rest_ref[128:256, :] = local_ref[128:256, :] + far_imag
@@ -428,11 +431,11 @@
 
 
 def final_body(
-    index_ref, occupation_ref, boxes_ref, proj_ref, table_ref, got_ref, turn_ref, both_ref, first_ref, near_ref,
+    occupation_ref, boxes_ref, proj_ref, table_ref, got_ref, turn_ref, both_ref, first_ref, near_ref,
     new_real_ref, new_imag_ref, out_ref, field_ref, place_ref, dual_ref,
 ):
     unpack(got_ref, 0, field_ref)
-    coef = second_coefs(index_ref[0], got_ref)
+    coef = second_coefs(lax.axis_index("fft"), got_ref)
     far_real, far_imag = spread(coef, boxes_ref, proj_ref, table_ref, turn_ref, place_ref, dual_ref)
     half = 0.5 * time_step * time_step
     second_real = near_ref[0:128, :] + field_ref[0:128, :] + far_real
@@ -479,7 +482,6 @@
     psi_real, psi_imag, potential, vector_potential, occupation, projectors, box_offsets, species, channels, coupling
 ):
     x_table, y_table, z_table = (jnp.asarray(table) for table in tables())
-    index = jnp.stack([lax.axis_index("fft"), lax.axis_index("band")]).astype(i32)
     real = psi_real.reshape(128, LANES)
     imag = psi_imag.reshape(128, LANES)
     pot = potential.reshape(128, LANES)
@@ -492,39 +494,40 @@
     slices, both = pl.pallas_call(
         pack_body,
         out_shape=(shape(8, 72, LANES), shape(256, LANES)),
-        in_specs=[smem()] + [anywhere] * 6,
+        in_specs=[anywhere] * 6,
         out_specs=(vmem(), vmem()),
         scratch_shapes=[
             pltpu.SMEM((3, 4), i32), pltpu.SMEM((4,), i32), pltpu.SMEM((4, 8), i32),
             pltpu.VMEM((4, 8, 4096), f32), pltpu.VMEM((136, LANES), f32), pltpu.SemaphoreType.DMA((9,)),
         ],
         compiler_params=pltpu.CompilerParams(vmem_limit_bytes=60 * 1024 * 1024),
-    )(index, box_offsets, species, channels, projectors, real, imag)
+    )(box_offsets, species, channels, projectors, real, imag)
     ahead = lax.ppermute(both, "fft", [(i, (i + 24) % SLABS) for i in range(SLABS)])
     rows = [list(range(8 * x, 8 * x + 8)) for x in range(4)]
     got = lax.all_to_all(slices, "fft", split_axis=0, concat_axis=0, tiled=True, axis_index_groups=rows)
-    local, turn, high, low = call(
-        local_body, (index, vector_potential), (both, pot, x_table, y_table, z_table),
-        (shape(256, LANES), shape(4, 128, LANES), matrix, matrix),
-    )
-    got, ahead, local, turn, high, low = lax.optimization_barrier((got, ahead, local, turn, high, low))
+    turn = call(phase_body, (vector_potential,), (), shape(4, 128, LANES))
+    got, ahead, turn = lax.optimization_barrier((got, ahead, turn))
     chips = [[2 * y, 2 * y + 1] for y in range(8)]
     gathered = lax.all_gather(got, "band", axis_index_groups=chips)
-    corners = call(pick_body, (index,), (got,), shape(8, LANES, dtype=i32))
+    corners = call(pick_body, (), (got,), shape(8, LANES, dtype=i32))
     passed = lax.ppermute(got, "fft", [(i, (i + 8) % SLABS) for i in range(SLABS)])
     shares = call(
         coef_body, (corners,), (gathered.reshape(2, 576, LANES), both, ahead, turn), shape(SLABS, 16, LANES),
         (pltpu.VMEM((640, LANES), f32), square),
     )
-    shares, passed = lax.optimization_barrier((shares, passed))
+    shares, passed, both = lax.optimization_barrier((shares, passed, both))
+    local, high, low = call(
+        local_body, (vector_potential,), (both, pot, x_table, y_table, z_table),
+        (shape(256, LANES), matrix, matrix),
+    )
     passed = lax.all_gather(passed, "band", axis_index_groups=chips)
     got = exchange(shares, "fft")
     beta, table, boxes = call(
-        merge_body, (index,), (gathered, passed, coupling),
+        merge_body, (), (gathered, passed, coupling),
         (shape(2, 576, LANES), shape(64, LANES), shape(8, LANES, dtype=i32)),
     )
     rest, moved, shares = call(
-        rest_body, (index, vector_potential, boxes), (beta, table, got, turn, local, high, low),
+        rest_body, (vector_potential, boxes), (beta, table, got, turn, local, high, low),
         (shape(256, LANES), shape(256, LANES), shape(SLABS, 16, LANES)), (window, square),
     )
     got = exchange(shares, "fft")
@@ -535,7 +538,7 @@
     got = exchange(shares, "fft")
     near = call(second_body, (vector_potential,), (first, pot, y_table, z_table), shape(256, LANES))
     new_real, new_imag, weighted = call(
-        final_body, (index, occupation, boxes), (beta, table, got, turn, both, first, near),
+        final_body, (occupation, boxes), (beta, table, got, turn, both, first, near),
         (shape(128, LANES), shape(128, LANES), shape(BANDS, 8, LANES)), (whole, window, square),
     )
     density = jnp.sum(exchange(weighted, "band"), axis=0).reshape(2, 4, LANES)

time: 111 us -> 107 us (0.964)
  Pallas kernels: 17.5 us -> 14.6 us
    pallas_call x8 -> x9, Pallas kernels: 14.3 us -> 12.2 us  [call(): pl.pallas_call(body, out_shape=outs, in_specs=[smem()] * len(scalars) + [...]
    all_to_all x2, waiting for transfers between devices: 13.7 us -> 11.6 us  [exchange(): return lax.all_to_all(value, axis, split_axis=0, concat_axis=0, tiled=True)]
    all_gather x1, blocking collectives: 2.71 us -> 4.07 us  [per_device(): passed = lax.all_gather(passed, 'band', axis_index_groups=chips)]
  transfers between devices with their start and end apart: 5 -> 5, of which waited for: 3 -> 4; matrix products, arithmetic and copies ran while one was open for 0% -> 0% of each run, Pallas kernels for 6% -> 6%
where the time goes in v4:
time: 107 us; the launch traced here: 106 us
  blocking collectives  43.2 us (40%)
  starting transfers between devices  28.7 us (27%)
  waiting for transfers between devices  17.3 us (16%)
  Pallas kernels  14.6 us (14%)
  between operations  1.43 us (1%)
    all_to_all x2, blocking collectives, exchange(): return lax.all_to_all(value, axis, split_axis=0, concat_axis=0, tiled=True)  34.6 us
    pallas_call x9, Pallas kernels, call(): pl.pallas_call(body, out_shape=outs, in_specs=[smem()] * len(scalars) + [...  12.2 us
    all_to_all x2, waiting for transfers between devices, exchange(): return lax.all_to_all(value, axis, split_axis=0, concat_axis=0, tiled=True)  11.6 us
    all_to_all x1, starting transfers between devices, per_device(): lax.all_to_all(slices, 'fft', split_axis=0, concat_axis=0, tiled=True, ax...  11 us
    all_to_all x2, starting transfers between devices, exchange(): return lax.all_to_all(value, axis, split_axis=0, concat_axis=0, tiled=True)  10.2 us
    all_to_all x1, waiting for transfers between devices, per_device(): lax.all_to_all(slices, 'fft', split_axis=0, concat_axis=0, tiled=True, ax...  4.83 us
    all_gather x1, blocking collectives, per_device(): gathered = lax.all_gather(got, 'band', axis_index_groups=chips)  4.5 us
    ppermute x1, starting transfers between devices, per_device(): lax.ppermute(both, 'fft', [(i, (i + 24) % SLABS) for i in range(SLABS)])  4.39 us
  transfers between devices with their start and end apart: 5, of which 4 were waited for; matrix products, arithmetic and copies ran while one was open for 0% of the time, Pallas kernels for 6%

profile of v4, /device:TPU:1, one launch (start us, length us, event | category | flops | bytes accessed | tf_op | source)
XLA Modules:
  0.0 106.2 jit_solution(2175111399995848028)
XLA Ops:
  0.6 2.4 %shard_map.148 = (f32[8,72,128]{2,1,0:T(8,128)}, f32[256,128]{1,0:T(8,128)}) custom-call(s32[3,4]{1,0:T(4,128)} %boxes_hbm.1, s32[4]{0:T(128)} %species_hbm.1, s32[4,8]{1,0:T(4,128)} %channels_hbm.1, f32[4,8,4096]{2,1,0:T(8,128)} %proj_hbm.1, f32[128,128]{1,0:T(8,128)} %bitcast.14, f32[128,128]{1,0:T(8,128)} %bitcast.15), custom_call_target="tpu_custom_call" | custom-call | tf_op jit(solution)/shard_map/pallas_call | solution.py:494
  3.1 0.0 copy-start.2
  3.1 11.0 %all-to-all-start = ((f32[8,72,128]{2,1,0:T(8,128)}), f32[8,72,128]{2,1,0:T(8,128)S(1)}, u32[]{:S(2)}, u32[]{:S(2)}) async-start(f32[8,72,128]{2,1,0:T(8,128)} %get-tuple-element.25), calls=%async_computation | async-start | bytes 589824 | tf_op jit(solution)/shard_map/all_to_all | solution.py:507
  14.1 0.0 copy-start.6
  14.1 0.0 copy-done.2
  14.1 4.4 %collective-permute-start = (f32[256,128]{1,0:T(8,128)S(1)}, f32[256,128]{1,0:T(8,128)S(1)}, u32[]{:S(2)}, u32[]{:S(2)}) collective-permute-start(f32[256,128]{1,0:T(8,128)S(1)} %copy-done.2), channel_id=1, source_target_pairs={{0,384},{16,400},{32,416},{48,432},{64,448},{80,464},{96,480},{112... | collective-permute-start | bytes 393224 | tf_op jit(solution)/shard_map/ppermute | solution.py:505
  18.5 0.0 copy-done.6
  18.5 1.1 %shard_map.149.turn_ref = f32[4,128,128]{2,1,0:T(8,128)S(1)} custom-call(f32[3]{0:T(128)S(1)} %copy-done.6), custom_call_target="tpu_custom_call" | custom-call | tf_op jit(solution)/shard_map/pallas_call | solution.py:463
  19.6 0.8 collective-permute-done.next_ref
  20.4 4.8 %all-to-all-done.got_ref = f32[8,72,128]{2,1,0:T(8,128)S(1)} async-done(((f32[8,72,128]{2,1,0:T(8,128)}), f32[8,72,128]{2,1,0:T(8,128)S(1)}, u32[]{:S(2)}, u32[]{:S(2)}) %all-to-all-start) | async-done | bytes 294944 | tf_op jit(solution)/shard_map/all_to_all | solution.py:507
  25.2 3.1 %collective-permute-start.1 = (f32[8,72,128]{2,1,0:T(8,128)S(1)}, f32[8,72,128]{2,1,0:T(8,128)S(1)}, u32[]{:S(2)}, u32[]{:S(2)}) collective-permute-start(f32[8,72,128]{2,1,0:T(8,128)S(1)} %all-to-all-done.got_ref), channel_id=1, source_target_pairs={{0,128},{16,144},{32,160},{48,176},{64,192},{80,208},{96,224},{112... | collective-permute-start | bytes 884744 | tf_op jit(solution)/shard_map/ppermute | solution.py:513
  28.4 0.1 shard_map.150.boxes_ref
  28.5 4.5 %all-gather = f32[16,72,128]{2,1,0:T(8,128)S(1)} all-gather(f32[8,72,128]{2,1,0:T(8,128)S(1)} %all-to-all-done.got_ref), channel_id=2, replica_groups={{0,1},{2,3},{4,5},{6,7},{8,9},{10,11},{12,13},{14,15},{16,17},{18,19},{..., dimensions={0}, use_global_device_ids=true | all-gather | bytes 884736 | tf_op jit(solution)/shard_map/all_gather | solution.py:511
  33.0 2.1 %shard_map.151 = f32[32,16,128]{2,1,0:T(8,128)} custom-call(s32[8,128]{1,0:T(8,128)S(1)} %shard_map.150.boxes_ref, f32[2,576,128]{2,1,0:T(8,128)S(1)} %bitcast.9, f32[256,128]{1,0:T(8,128)S(1)} %copy-done.2, f32[256,128]{1,0:T(8,128)S(1)} %collective-permute-done.next_ref, f32[4,128,128]{2,1,0:T(8,128)S(1)} %shard_map.149.turn_ref), custom_call_target="tpu_custom_call" | custom-call | tf_op jit(solution)/shard_map/pallas_call | solution.py:463
  35.1 0.0 collective-permute-done.1
  35.1 5.1 %all-to-all-start.1 = ((f32[32,16,128]{2,1,0:T(8,128)}), f32[32,16,128]{2,1,0:T(8,128)S(1)}, u32[]{:S(2)}, u32[]{:S(2)}) async-start(f32[32,16,128]{2,1,0:T(8,128)} %shard_map.151), calls=%async_computation.1 | async-start | bytes 524288 | tf_op jit(solution)/shard_map/all_to_all | solution.py:478
  40.2 0.0 copy-start.5
  40.2 0.0 copy-start.3
  40.2 4.1 %all-gather.1 = f32[16,72,128]{2,1,0:T(8,128)S(1)} all-gather(f32[8,72,128]{2,1,0:T(8,128)S(1)} %collective-permute-done.1), channel_id=3, replica_groups={{0,1},{2,3},{4,5},{6,7},{8,9},{10,11},{12,13},{14,15},{16,17},{18,19},{..., dimensions={0}, use_global_device_ids=true | all-gather | bytes 884736 | tf_op jit(solution)/shard_map/all_gather | solution.py:523
  44.3 0.0 copy-done.5
  44.3 0.0 copy-start
  44.3 0.0 copy-start.1
  44.3 0.0 copy-start.4
  44.3 0.8 shard_map.152
  45.1 0.0 copy-done.3
  45.2 0.2 copy-done
  45.3 0.2 copy-done.1
  45.5 0.0 copy-done.4
  45.5 0.9 shard_map.153
  46.4 3.5 %all-to-all-done.1.got_ref = f32[32,16,128]{2,1,0:T(8,128)S(1)} async-done(((f32[32,16,128]{2,1,0:T(8,128)}), f32[32,16,128]{2,1,0:T(8,128)S(1)}, u32[]{:S(2)}, u32[]{:S(2)}) %all-to-all-start.1) | async-done | bytes 262176 | tf_op jit(solution)/shard_map/all_to_all | solution.py:478
  49.9 1.7 %shard_map.154 = (f32[256,128]{1,0:T(8,128)S(1)}, f32[256,128]{1,0:T(8,128)S(1)}, f32[32,16,128]{2,1,0:T(8,128)S(1)}) custom-call(f32[3]{0:T(128)S(1)} %copy-done.6, s32[8,128]{1,0:T(8,128)S(1)} %get-tuple-element.31.boxes_ref, f32[2,576,128]{2,1,0:T(8,128)S(1)} %get-tuple-element.32.proj_ref, f32[64,128]{1,0:T(8,128)S(1)} %get-tuple-element.33.table_ref, ...), custom_call_target="tpu_custom_call" | custom-call | tf_op jit(solution)/shard_map/pallas_call | solution.py:463
  51.6 15.5 %all_to_all.25.got_ref = f32[32,16,128]{2,1,0:T(8,128)S(1)} all-to-all(f32[32,16,128]{2,1,0:T(8,128)S(1)} %get-tuple-element.39), channel_id=1, replica_groups=mesh['fft'=32,'band'=16] {'fft'}, dimensions={0} | all-to-all | bytes 524288 | tf_op jit(solution)/shard_map/all_to_all | solution.py:478
  67.1 2.3 %shard_map.155 = (f32[256,128]{1,0:T(8,128)S(1)}, f32[32,16,128]{2,1,0:T(8,128)}) custom-call(f32[3]{0:T(128)S(1)} %copy-done.6, s32[8,128]{1,0:T(8,128)S(1)} %get-tuple-element.31.boxes_ref, f32[2,576,128]{2,1,0:T(8,128)S(1)} %get-tuple-element.32.proj_ref, f32[32,16,128]{2,1,0:T(8,128)S(1)} %all_to_all.25.got_ref, f32[4,128,128]{2,1,0:T(8,128)S(1)} %shard_map.149.turn_ref, ...), custom_call_target="tpu_custom_call" | custom-call | tf_op jit(solution)/shard_map/pallas_call | solution.py:463
  69.4 5.1 %all-to-all-start.3 = ((f32[32,16,128]{2,1,0:T(8,128)}), f32[32,16,128]{2,1,0:T(8,128)S(1)}, u32[]{:S(2)}, u32[]{:S(2)}) async-start(f32[32,16,128]{2,1,0:T(8,128)} %get-tuple-element.42), calls=%async_computation.3 | async-start | bytes 524288 | tf_op jit(solution)/shard_map/all_to_all | solution.py:478
  75.2 0.9 shard_map.156.near_ref
  76.1 8.1 %all-to-all-done.3.got_ref = f32[32,16,128]{2,1,0:T(8,128)S(1)} async-done(((f32[32,16,128]{2,1,0:T(8,128)}), f32[32,16,128]{2,1,0:T(8,128)S(1)}, u32[]{:S(2)}, u32[]{:S(2)}) %all-to-all-start.3) | async-done | bytes 262176 | tf_op jit(solution)/shard_map/all_to_all | solution.py:478
  84.2 2.3 %shard_map.157 = (f32[128,128]{1,0:T(8,128)}, f32[128,128]{1,0:T(8,128)}, f32[16,8,128]{2,1,0:T(8,128)S(1)}) custom-call(f32[1]{0:T(128)S(6)} %copy.16.occupation_ref, s32[8,128]{1,0:T(8,128)S(1)} %get-tuple-element.31.boxes_ref, f32[2,576,128]{2,1,0:T(8,128)S(1)} %get-tuple-element.32.proj_ref, f32[64,128]{1,0:T(8,128)S(1)} %get-tuple-element.33.table_ref, ...), custom_call_target="tpu_custom_call" | custom-call | tf_op jit(solution)/shard_map/pallas_call | solution.py:463
  86.5 19.1 %all_to_all.26 = f32[16,8,128]{2,1,0:T(8,128)S(1)} all-to-all(f32[16,8,128]{2,1,0:T(8,128)S(1)} %get-tuple-element.46), channel_id=1, replica_groups=mesh['fft'=32,'band'=16] {'band'}, dimensions={0} | all-to-all | bytes 131072 | tf_op jit(solution)/shard_map/all_to_all | solution.py:478
  105.6 0.6 reduce_sum.9
Async XLA Ops:
  3.1 11.0 %copy-start.2 = (f32[256,128]{1,0:T(8,128)S(1)}, f32[256,128]{1,0:T(8,128)}, u32[]{:S(2)}) copy-start(f32[256,128]{1,0:T(8,128)} %get-tuple-element.35.both_ref) | copy-start | bytes 393220
  3.1 22.2 %all-to-all-start = ((f32[8,72,128]{2,1,0:T(8,128)}), f32[8,72,128]{2,1,0:T(8,128)S(1)}, u32[]{:S(2)}, u32[]{:S(2)}) async-start(f32[8,72,128]{2,1,0:T(8,128)} %get-tuple-element.25), calls=%async_computation | async-start | bytes 589824 | tf_op jit(solution)/shard_map/all_to_all | solution.py:507
  14.1 4.4 %copy-start.6 = (f32[3]{0:T(128)S(1)}, f32[3]{0:T(128)}, u32[]{:S(2)}) copy-start(f32[3]{0:T(128)} %vector_ref.9) | copy-start | bytes 40
  14.1 6.3 %collective-permute-start = (f32[256,128]{1,0:T(8,128)S(1)}, f32[256,128]{1,0:T(8,128)S(1)}, u32[]{:S(2)}, u32[]{:S(2)}) collective-permute-start(f32[256,128]{1,0:T(8,128)S(1)} %copy-done.2), channel_id=1, source_target_pairs={{0,384},{16,400},{32,416},{48,432},{64,448},{80,464},{96,480},{112... | collective-permute-start | bytes 393224 | tf_op jit(solution)/shard_map/ppermute | solution.py:505
  25.2 9.8 %collective-permute-start.1 = (f32[8,72,128]{2,1,0:T(8,128)S(1)}, f32[8,72,128]{2,1,0:T(8,128)S(1)}, u32[]{:S(2)}, u32[]{:S(2)}) collective-permute-start(f32[8,72,128]{2,1,0:T(8,128)S(1)} %all-to-all-done.got_ref), channel_id=1, source_target_pairs={{0,128},{16,144},{32,160},{48,176},{64,192},{80,208},{96,224},{112... | collective-permute-start | bytes 884744 | tf_op jit(solution)/shard_map/ppermute | solution.py:513
  35.1 14.8 %all-to-all-start.1 = ((f32[32,16,128]{2,1,0:T(8,128)}), f32[32,16,128]{2,1,0:T(8,128)S(1)}, u32[]{:S(2)}, u32[]{:S(2)}) async-start(f32[32,16,128]{2,1,0:T(8,128)} %shard_map.151), calls=%async_computation.1 | async-start | bytes 524288 | tf_op jit(solution)/shard_map/all_to_all | solution.py:478
  40.2 4.1 %copy-start.5 = (f32[4,8,8]{2,1,0:T(8,128)S(1)}, f32[4,8,8]{2,1,0:T(8,128)}, u32[]{:S(2)}) copy-start(f32[4,8,8]{2,1,0:T(8,128)} %coupling_ref.1) | copy-start | bytes 3076
  40.2 5.0 %copy-start.3 = (f32[2,256,256]{2,1,0:T(8,128)S(1)}, f32[2,256,256]{2,1,0:T(8,128)}, u32[]{:S(2)}) copy-start(f32[2,256,256]{2,1,0:T(8,128)} %constant.8.clone.x_ref) | copy-start | bytes 1572868
  44.3 1.0 copy-start
  44.3 1.2 %copy-start.1 = (f32[2,256,256]{2,1,0:T(8,128)S(1)}, f32[2,256,256]{2,1,0:T(8,128)}, u32[]{:S(2)}) copy-start(f32[2,256,256]{2,1,0:T(8,128)} %constant.9.clone.y_ref) | copy-start | bytes 1572868
  44.3 1.2 %copy-start.4 = (f32[2,64,128]{2,1,0:T(8,128)S(1)}, f32[2,64,128]{2,1,0:T(8,128)}, u32[]{:S(2)}) copy-start(f32[2,64,128]{2,1,0:T(8,128)} %param.15) | copy-start | bytes 196612
  69.4 14.8 %all-to-all-start.3 = ((f32[32,16,128]{2,1,0:T(8,128)}), f32[32,16,128]{2,1,0:T(8,128)S(1)}, u32[]{:S(2)}, u32[]{:S(2)}) async-start(f32[32,16,128]{2,1,0:T(8,128)} %get-tuple-element.42), calls=%async_computation.3 | async-start | bytes 524288 | tf_op jit(solution)/shard_map/all_to_all | solution.py:478

commit v5 on v4

--- a/solution.py
+++ b/solution.py
@@ -73,34 +73,31 @@
     return high, low
 
 
-def dot3(left, right):
-    left_high, left_low = halves(left)
-    right_high, right_low = halves(right)
-    dot = functools.partial(jnp.dot, preferred_element_type=f32)
-    return dot(left_high, right_high) + (dot(left_high, right_low) + dot(left_low, right_high))
-
-
 def group_matrix():
     row = lax.broadcasted_iota(i32, (NPROJ, LANES), 0)
     lane = lax.broadcasted_iota(i32, (NPROJ, LANES), 1)
     return (lane // BOX == row).astype(f32)
 
 
-def kinetic_yz(field, y_ref, z_ref, shift_y, shift_z):
-    along = dot3(y_ref[0] + shift_y * y_ref[1], field)
+def split_matrix(table_ref, shift, high_ref, low_ref):
+    high_ref[...], low_ref[...] = halves(table_ref[0] + shift * table_ref[1])
+
+
+def dot_split(left, right):
+    dot = functools.partial(jnp.dot, preferred_element_type=f32)
+    return dot(left[0], right[0]) + (dot(left[0], right[1]) + dot(left[1], right[0]))
+
+
+def kinetic_yz(field, y_split, z_split, constant):
+    along = dot_split([ref[...] for ref in y_split], halves(field))
     wide = jnp.concatenate([field[:128], field[128:]], axis=1)
-    across = dot3(wide, z_ref[0] + shift_z * z_ref[1])
+    across = dot_split(halves(wide), [ref[...] for ref in z_split])
     across = jnp.concatenate([across[:, :128], across[:, 128:]], axis=0)
-    constant = kinetic_scale * (shift_y * shift_y + shift_z * shift_z)
     return along + across + constant * field
 
 
-def kinetic_x(field, high_ref, low_ref, shift):
-    field_high, field_low = halves(field)
-    dot = functools.partial(jnp.dot, preferred_element_type=f32)
-    high = high_ref[...]
-    moved = dot(high, field_high) + (dot(high, field_low) + dot(low_ref[...], field_high))
-    return moved + (kinetic_scale * shift * shift) * field
+def kinetic_x(field, high_ref, low_ref, shift_ref):
+    return dot_split((high_ref[...], low_ref[...]), halves(field)) + shift_ref[0:1, :] * field
 
 
 def pack_body(
@@ -229,7 +226,7 @@
     boxes_ref[...] = jnp.where(sub == 0, first_y, first_z).astype(i32)
 
 
-def phase_body(vector_ref, turn_ref):
+def phase_body(vector_ref, occupation_ref, turn_ref, shift_ref):
     slab = lax.axis_index("fft")
     row = lax.broadcasted_iota(i32, (128, LANES), 0)
     y = (row % NY).astype(f32)
@@ -241,18 +238,20 @@
         theta = (2.0 * math.pi) * turns
         turn_ref[2 * ahead] = jnp.cos(theta)
         turn_ref[2 * ahead + 1] = jnp.sin(theta)
-
-
-def local_body(
-    vector_ref, both_ref, pot_ref, x_ref, y_ref, z_ref, out_ref, high_ref, low_ref
-):
+    squares = [kinetic_scale * vector_ref[axis] * vector_ref[axis] for axis in range(3)]
+    sub = lax.broadcasted_iota(i32, (8, LANES), 0)
+    rows = jnp.where(sub == 1, occupation_ref[0], squares[1] + squares[2])
+    shift_ref[...] = jnp.where(sub == 0, squares[0], rows)
+
+
+def local_body(vector_ref, both_ref, pot_ref, x_ref, y_ref, z_ref, out_ref, *split_refs):
+    for axis, table_ref in enumerate((x_ref, y_ref, z_ref)):
+        split_matrix(table_ref, vector_ref[axis], split_refs[2 * axis], split_refs[2 * axis + 1])
     field = both_ref[...]
-    out = kinetic_yz(field, y_ref, z_ref, vector_ref[1], vector_ref[2])
+    constant = kinetic_scale * (vector_ref[1] * vector_ref[1] + vector_ref[2] * vector_ref[2])
+    out = kinetic_yz(field, split_refs[2:4], split_refs[4:6], constant)
     pot = pot_ref[...]
     out_ref[...] = out + jnp.concatenate([pot, pot], axis=0) * field
-    high, low = halves(x_ref[0] + vector_ref[0] * x_ref[1])
-    high_ref[...] = high
-    low_ref[...] = low
 
 
 def turned_rows(real, imag, cosine, sine, field_ref, first_row):
@@ -382,25 +381,37 @@
                 field_ref[pl.ds(start, SLABS, stride=2), :] = got_ref[:, first_row + row, :]
 
 
-def coef_body(boxes_ref, proj_ref, both_ref, next_ref, turn_ref, out_ref, field_ref, sums_ref):
+def fetch(source_ref, boxes_ref, done):
+    copy = pltpu.make_async_copy(source_ref, boxes_ref, done.at[0])
+    copy.start()
+    return copy
+
+
+def coef_body(
+    corner_ref, proj_ref, both_ref, next_ref, turn_ref, out_ref, field_ref, sums_ref, boxes_ref, done
+):
+    copy = fetch(corner_ref, boxes_ref, done)
     columns(both_ref, out_ref)
     for ahead, ref in enumerate((both_ref, next_ref)):
         turned_rows(
             ref[0:128, :], ref[128:256, :], turn_ref[2 * ahead], turn_ref[2 * ahead + 1], field_ref, 320 * ahead
         )
+    copy.wait()
     coef = project(boxes_ref, proj_ref, 72, True, 32, field_ref, sums_ref)
     out_ref[:, 8:16, :] = jnp.broadcast_to(coef[None], (SLABS, 8, LANES))
 
 
 def rest_body(
-    vector_ref, boxes_ref, proj_ref, table_ref, got_ref, turn_ref, local_ref, high_ref, low_ref,
-    rest_ref, moved_ref, out_ref, place_ref, dual_ref,
+    corner_ref, shift_ref, proj_ref, table_ref, got_ref, turn_ref, local_ref, high_ref, low_ref,
+    rest_ref, moved_ref, out_ref, place_ref, dual_ref, boxes_ref, done,
 ):
+    copy = fetch(corner_ref, boxes_ref, done)
     field = got_ref[:, 0:8, :].reshape(256, LANES)
-    moved = kinetic_x(field, high_ref, low_ref, vector_ref[0])
+    moved = kinetic_x(field, high_ref, low_ref, shift_ref)
     moved_ref[...] = moved
     out_ref[:, 8:16, :] = moved.reshape(SLABS, 8, LANES)
     coef = first_coefs(lax.axis_index("fft"), got_ref)
+    copy.wait()
     far_real, far_imag = spread(coef, boxes_ref, proj_ref, table_ref, turn_ref, place_ref, dual_ref)
     rest_ref[0:128, :] = local_ref[0:128, :] + far_real
     rest_ref[128:256, :] = local_ref[128:256, :] + far_imag
@@ -408,43 +419,44 @@
 
 
 def first_body(
-    vector_ref, boxes_ref, proj_ref, got_ref, turn_ref, rest_ref, moved_ref, high_ref, low_ref,
-    first_ref, out_ref, field_ref, sums_ref,
+    corner_ref, shift_ref, proj_ref, got_ref, turn_ref, rest_ref, moved_ref, high_ref, low_ref,
+    first_ref, out_ref, field_ref, sums_ref, boxes_ref, done,
 ):
+    copy = fetch(corner_ref, boxes_ref, done)
     field = got_ref[:, 0:8, :].reshape(256, LANES) + moved_ref[...]
-    out_ref[:, 0:8, :] = kinetic_x(field, high_ref, low_ref, vector_ref[0]).reshape(SLABS, 8, LANES)
+    out_ref[:, 0:8, :] = kinetic_x(field, high_ref, low_ref, shift_ref).reshape(SLABS, 8, LANES)
     unpack(got_ref, 8, first_ref)
     real = first_ref[0:128, :] + rest_ref[0:128, :]
     imag = first_ref[128:256, :] + rest_ref[128:256, :]
     first_ref[0:128, :] = real
     first_ref[128:256, :] = imag
     turned_rows(real, imag, turn_ref[0], turn_ref[1], field_ref, 0)
+    copy.wait()
     coef = project(boxes_ref, proj_ref, 64, False, 4 * REACH, field_ref, sums_ref)
     out_ref[:, 8:16, :] = jnp.broadcast_to(coef[None], (SLABS, 8, LANES))
 
 
-def second_body(vector_ref, first_ref, pot_ref, y_ref, z_ref, out_ref):
-    field = first_ref[...]
-    pot = pot_ref[...]
-    near = kinetic_yz(field, y_ref, z_ref, vector_ref[1], vector_ref[2])
-    out_ref[...] = near + jnp.concatenate([pot, pot], axis=0) * field
-
-
 def final_body(
-    occupation_ref, boxes_ref, proj_ref, table_ref, got_ref, turn_ref, both_ref, first_ref, near_ref,
-    new_real_ref, new_imag_ref, out_ref, field_ref, place_ref, dual_ref,
+    corner_ref, shift_ref, proj_ref, table_ref, got_ref, turn_ref, both_ref, first_ref, pot_ref,
+    y_high_ref, y_low_ref, z_high_ref, z_low_ref,
+    new_real_ref, new_imag_ref, out_ref, field_ref, place_ref, dual_ref, boxes_ref, done,
 ):
+    copy = fetch(corner_ref, boxes_ref, done)
     unpack(got_ref, 0, field_ref)
     coef = second_coefs(lax.axis_index("fft"), got_ref)
+    copy.wait()
     far_real, far_imag = spread(coef, boxes_ref, proj_ref, table_ref, turn_ref, place_ref, dual_ref)
     half = 0.5 * time_step * time_step
-    second_real = near_ref[0:128, :] + field_ref[0:128, :] + far_real
-    second_imag = near_ref[128:256, :] + field_ref[128:256, :] + far_imag
+    first = first_ref[...]
+    near = kinetic_yz(first, (y_high_ref, y_low_ref), (z_high_ref, z_low_ref), shift_ref[2:3, :])
+    pot = pot_ref[...]
+    second_real = near[:128] + pot * first[:128] + field_ref[0:128, :] + far_real
+    second_imag = near[128:] + pot * first[128:] + field_ref[128:256, :] + far_imag
     new_real = both_ref[0:128, :] + time_step * first_ref[128:256, :] - half * second_real
     new_imag = both_ref[128:256, :] - time_step * first_ref[0:128, :] - half * second_imag
     new_real_ref[...] = new_real
     new_imag_ref[...] = new_imag
-    weighted = occupation_ref[0] * (new_real * new_real + new_imag * new_imag)
+    weighted = shift_ref[1:2, :] * (new_real * new_real + new_imag * new_imag)
     weighted = weighted.reshape(2, BANDS, 4, LANES)
     for plane in range(2):
         out_ref[:, pl.ds(plane * 4, 4), :] = weighted[plane]
@@ -458,7 +470,7 @@
     return pl.BlockSpec(memory_space=pltpu.VMEM)
 
 
-def call(body, scalars, arrays, outs, scratch=()):
+def call(body, scalars, arrays, outs, scratch=(), cost=None):
     several = isinstance(outs, tuple)
     return pl.pallas_call(
         body,
@@ -467,6 +479,7 @@
         out_specs=tuple(vmem() for _ in outs) if several else vmem(),
         scratch_shapes=list(scratch),
         compiler_params=pltpu.CompilerParams(vmem_limit_bytes=24 * 1024 * 1024),
+        cost_estimate=cost,
     )(*scalars, *arrays)
 
 
@@ -486,6 +499,8 @@
     imag = psi_imag.reshape(128, LANES)
     pot = potential.reshape(128, LANES)
     matrix = jax.ShapeDtypeStruct((256, 256), jnp.bfloat16)
+    corner = pltpu.SMEM((8, LANES), i32)
+    signal = pltpu.SemaphoreType.DMA((1,))
     window = pltpu.VMEM((320, LANES), f32)
     square = pltpu.VMEM((128, LANES), f32)
     whole = pltpu.VMEM((256, LANES), f32)
@@ -505,20 +520,20 @@
     ahead = lax.ppermute(both, "fft", [(i, (i + 24) % SLABS) for i in range(SLABS)])
     rows = [list(range(8 * x, 8 * x + 8)) for x in range(4)]
     got = lax.all_to_all(slices, "fft", split_axis=0, concat_axis=0, tiled=True, axis_index_groups=rows)
-    turn = call(phase_body, (vector_potential,), (), shape(4, 128, LANES))
-    got, ahead, turn = lax.optimization_barrier((got, ahead, turn))
+    turn, shift = call(phase_body, (vector_potential, occupation), (), (shape(4, 128, LANES), shape(8, LANES)))
+    got, ahead, turn, shift = lax.optimization_barrier((got, ahead, turn, shift))
     chips = [[2 * y, 2 * y + 1] for y in range(8)]
     gathered = lax.all_gather(got, "band", axis_index_groups=chips)
     corners = call(pick_body, (), (got,), shape(8, LANES, dtype=i32))
     passed = lax.ppermute(got, "fft", [(i, (i + 8) % SLABS) for i in range(SLABS)])
     shares = call(
-        coef_body, (corners,), (gathered.reshape(2, 576, LANES), both, ahead, turn), shape(SLABS, 16, LANES),
-        (pltpu.VMEM((640, LANES), f32), square),
+        coef_body, (), (corners, gathered.reshape(2, 576, LANES), both, ahead, turn), shape(SLABS, 16, LANES),
+        (pltpu.VMEM((640, LANES), f32), square, corner, signal),
     )
     shares, passed, both = lax.optimization_barrier((shares, passed, both))
-    local, high, low = call(
+    local, high, low, *yz_split = call(
         local_body, (vector_potential,), (both, pot, x_table, y_table, z_table),
-        (shape(256, LANES), matrix, matrix),
+        (shape(256, LANES),) + (matrix,) * 6,
     )
     passed = lax.all_gather(passed, "band", axis_index_groups=chips)
     got = exchange(shares, "fft")
@@ -527,19 +542,18 @@
         (shape(2, 576, LANES), shape(64, LANES), shape(8, LANES, dtype=i32)),
     )
     rest, moved, shares = call(
-        rest_body, (vector_potential, boxes), (beta, table, got, turn, local, high, low),
-        (shape(256, LANES), shape(256, LANES), shape(SLABS, 16, LANES)), (window, square),
+        rest_body, (), (boxes, shift, beta, table, got, turn, local, high, low),
+        (shape(256, LANES), shape(256, LANES), shape(SLABS, 16, LANES)), (window, square, corner, signal),
     )
     got = exchange(shares, "fft")
     first, shares = call(
-        first_body, (vector_potential, boxes), (beta, got, turn, rest, moved, high, low),
-        (shape(256, LANES), shape(SLABS, 16, LANES)), (window, square),
+        first_body, (), (boxes, shift, beta, got, turn, rest, moved, high, low),
+        (shape(256, LANES), shape(SLABS, 16, LANES)), (window, square, corner, signal),
     )
     got = exchange(shares, "fft")
-    near = call(second_body, (vector_potential,), (first, pot, y_table, z_table), shape(256, LANES))
     new_real, new_imag, weighted = call(
-        final_body, (occupation, boxes), (beta, table, got, turn, both, first, near),
-        (shape(128, LANES), shape(128, LANES), shape(BANDS, 8, LANES)), (whole, window, square),
+        final_body, (), (boxes, shift, beta, table, got, turn, both, first, pot, *yz_split),
+        (shape(128, LANES), shape(128, LANES), shape(BANDS, 8, LANES)), (whole, window, square, corner, signal),
     )
     density = jnp.sum(exchange(weighted, "band"), axis=0).reshape(2, 4, LANES)
     grid = (1, 2, NY, NZ)

time: 107 us -> 106 us (level)
  blocking collectives: 43.2 us -> 57.9 us
  waiting for transfers between devices: 17.3 us -> 8.41 us
  starting transfers between devices: 28.7 us -> 23.6 us
  Pallas kernels: 14.6 us -> 12.8 us
    all_to_all x2 -> x3, blocking collectives: 34.6 us -> 49.3 us  [exchange(): return lax.all_to_all(value, axis, split_axis=0, concat_axis=0, tiled=True)]
    all_to_all x2 -> x1, waiting for transfers between devices: 11.6 us -> 3.4 us  [exchange(): return lax.all_to_all(value, axis, split_axis=0, concat_axis=0, tiled=True)]
    all_to_all x2 -> x1, starting transfers between devices: 10.2 us -> 5.12 us  [exchange(): return lax.all_to_all(value, axis, split_axis=0, concat_axis=0, tiled=True)]
    pallas_call x9 -> x8, Pallas kernels: 12.2 us -> 10.4 us  [call(): pl.pallas_call(body, out_shape=outs, in_specs=[smem()] * len(scalars) + [...]
  transfers between devices with their start and end apart: 5 -> 4, of which waited for: 4 -> 3; matrix products, arithmetic and copies ran while one was open for 0% -> 0% of each run, Pallas kernels for 6% -> 5%
where the time goes in v5:
time: 106 us; the launch traced here: 105 us
  blocking collectives  57.9 us (55%)
  starting transfers between devices  23.6 us (22%)
  Pallas kernels  12.8 us (12%)
  waiting for transfers between devices  8.41 us (8%)
  between operations  1.44 us (1%)
    all_to_all x3, blocking collectives, exchange(): return lax.all_to_all(value, axis, split_axis=0, concat_axis=0, tiled=True)  49.3 us
    all_to_all x1, starting transfers between devices, per_device(): lax.all_to_all(slices, 'fft', split_axis=0, concat_axis=0, tiled=True, ax...  11 us
    pallas_call x8, Pallas kernels, call(): pl.pallas_call(body, out_shape=outs, in_specs=[smem()] * len(scalars) + [...  10.4 us
    all_to_all x1, starting transfers between devices, exchange(): return lax.all_to_all(value, axis, split_axis=0, concat_axis=0, tiled=True)  5.12 us
    all_to_all x1, waiting for transfers between devices, per_device(): lax.all_to_all(slices, 'fft', split_axis=0, concat_axis=0, tiled=True, ax...  4.83 us
    all_gather x1, blocking collectives, per_device(): gathered = lax.all_gather(got, 'band', axis_index_groups=chips)  4.5 us
    ppermute x1, starting transfers between devices, per_device(): lax.ppermute(both, 'fft', [(i, (i + 24) % SLABS) for i in range(SLABS)])  4.39 us
    all_gather x1, blocking collectives, per_device(): passed = lax.all_gather(passed, 'band', axis_index_groups=chips)  4.11 us
  transfers between devices with their start and end apart: 4, of which 3 were waited for; matrix products, arithmetic and copies ran while one was open for 0% of the time, Pallas kernels for 5%

profile of v5, /device:TPU:1, one launch (start us, length us, event | category | flops | bytes accessed | tf_op | source)
XLA Modules:
  0.0 105.2 jit_solution(1745190353974989511)
XLA Ops:
  0.6 2.4 %shard_map.148 = (f32[8,72,128]{2,1,0:T(8,128)}, f32[256,128]{1,0:T(8,128)}) custom-call(s32[3,4]{1,0:T(4,128)} %boxes_hbm.1, s32[4]{0:T(128)} %species_hbm.1, s32[4,8]{1,0:T(4,128)} %channels_hbm.1, f32[4,8,4096]{2,1,0:T(8,128)} %proj_hbm.1, f32[128,128]{1,0:T(8,128)} %bitcast.14, f32[128,128]{1,0:T(8,128)} %bitcast.15), custom_call_target="tpu_custom_call" | custom-call | tf_op jit(solution)/shard_map/pallas_call | solution.py:509
  3.0 0.0 copy-start
  3.1 11.0 %all-to-all-start = ((f32[8,72,128]{2,1,0:T(8,128)}), f32[8,72,128]{2,1,0:T(8,128)S(1)}, u32[]{:S(2)}, u32[]{:S(2)}) async-start(f32[8,72,128]{2,1,0:T(8,128)} %get-tuple-element.32), calls=%async_computation | async-start | bytes 589824 | tf_op jit(solution)/shard_map/all_to_all | solution.py:522
  14.1 0.0 copy-done
  14.1 0.0 copy-start.6
  14.1 4.4 %collective-permute-start = (f32[256,128]{1,0:T(8,128)S(1)}, f32[256,128]{1,0:T(8,128)S(1)}, u32[]{:S(2)}, u32[]{:S(2)}) collective-permute-start(f32[256,128]{1,0:T(8,128)S(1)} %copy-done), channel_id=1, source_target_pairs={{0,384},{16,400},{32,416},{48,432},{64,448},{80,464},{96,480},{112... | collective-permute-start | bytes 393224 | tf_op jit(solution)/shard_map/ppermute | solution.py:520
  19.1 0.0 copy-done.6
  19.1 1.1 %shard_map.149 = (f32[4,128,128]{2,1,0:T(8,128)S(1)}, f32[8,128]{1,0:T(8,128)S(1)}) custom-call(f32[3]{0:T(128)S(1)} %copy-done.6, f32[1]{0:T(128)S(6)} %copy.16.occupation_ref), custom_call_target="tpu_custom_call" | custom-call | tf_op jit(solution)/shard_map/pallas_call | solution.py:475
  20.2 0.2 collective-permute-done.next_ref
  20.4 4.8 %all-to-all-done.got_ref = f32[8,72,128]{2,1,0:T(8,128)S(1)} async-done(((f32[8,72,128]{2,1,0:T(8,128)}), f32[8,72,128]{2,1,0:T(8,128)S(1)}, u32[]{:S(2)}, u32[]{:S(2)}) %all-to-all-start) | async-done | bytes 294944 | tf_op jit(solution)/shard_map/all_to_all | solution.py:522
  25.2 3.1 %collective-permute-start.1 = (f32[8,72,128]{2,1,0:T(8,128)S(1)}, f32[8,72,128]{2,1,0:T(8,128)S(1)}, u32[]{:S(2)}, u32[]{:S(2)}) collective-permute-start(f32[8,72,128]{2,1,0:T(8,128)S(1)} %all-to-all-done.got_ref), channel_id=1, source_target_pairs={{0,128},{16,144},{32,160},{48,176},{64,192},{80,208},{96,224},{112... | collective-permute-start | bytes 884744 | tf_op jit(solution)/shard_map/ppermute | solution.py:528
  28.3 0.1 shard_map.150.corner_ref
  28.5 4.5 %all-gather = f32[16,72,128]{2,1,0:T(8,128)S(1)} all-gather(f32[8,72,128]{2,1,0:T(8,128)S(1)} %all-to-all-done.got_ref), channel_id=2, replica_groups={{0,1},{2,3},{4,5},{6,7},{8,9},{10,11},{12,13},{14,15},{16,17},{18,19},{..., dimensions={0}, use_global_device_ids=true | all-gather | bytes 884736 | tf_op jit(solution)/shard_map/all_gather | solution.py:526
  33.0 2.0 %shard_map.151 = f32[32,16,128]{2,1,0:T(8,128)} custom-call(s32[8,128]{1,0:T(8,128)S(1)} %shard_map.150.corner_ref, f32[2,576,128]{2,1,0:T(8,128)S(1)} %bitcast.9, f32[256,128]{1,0:T(8,128)S(1)} %copy-done, f32[256,128]{1,0:T(8,128)S(1)} %collective-permute-done.next_ref, f32[4,128,128]{2,1,0:T(8,128)S(1)} %get-tuple-element.38.turn_ref), custom_call_target="tpu_custom_call" | custom-call | tf_op jit(solution)/shard_map/pallas_call | solution.py:475
  35.0 0.0 collective-permute-done.1
  35.0 5.1 %all-to-all-start.1 = ((f32[32,16,128]{2,1,0:T(8,128)}), f32[32,16,128]{2,1,0:T(8,128)S(1)}, u32[]{:S(2)}, u32[]{:S(2)}) async-start(f32[32,16,128]{2,1,0:T(8,128)} %shard_map.151), calls=%async_computation.1 | async-start | bytes 524288 | tf_op jit(solution)/shard_map/all_to_all | solution.py:491
  40.1 0.0 copy-start.5
  40.1 0.0 copy-start.3
  40.2 4.1 %all-gather.1 = f32[16,72,128]{2,1,0:T(8,128)S(1)} all-gather(f32[8,72,128]{2,1,0:T(8,128)S(1)} %collective-permute-done.1), channel_id=3, replica_groups={{0,1},{2,3},{4,5},{6,7},{8,9},{10,11},{12,13},{14,15},{16,17},{18,19},{..., dimensions={0}, use_global_device_ids=true | all-gather | bytes 884736 | tf_op jit(solution)/shard_map/all_gather | solution.py:538
  44.3 0.0 copy-done.5
  44.3 0.0 copy-start.1
  44.3 0.0 copy-start.2
  44.3 0.0 copy-start.4
  44.3 0.8 shard_map.152
  45.1 0.0 copy-done.3
  45.1 0.2 copy-done.1
  45.3 0.2 copy-done.2
  45.5 0.0 copy-done.4
  45.5 0.9 shard_map.153
  46.4 3.4 %all-to-all-done.1.got_ref = f32[32,16,128]{2,1,0:T(8,128)S(1)} async-done(((f32[32,16,128]{2,1,0:T(8,128)}), f32[32,16,128]{2,1,0:T(8,128)S(1)}, u32[]{:S(2)}, u32[]{:S(2)}) %all-to-all-start.1) | async-done | bytes 262176 | tf_op jit(solution)/shard_map/all_to_all | solution.py:491
  49.8 1.6 %shard_map.154 = (f32[256,128]{1,0:T(8,128)S(1)}, f32[256,128]{1,0:T(8,128)S(1)}, f32[32,16,128]{2,1,0:T(8,128)S(1)}) custom-call(s32[8,128]{1,0:T(8,128)S(1)} %get-tuple-element.40.corner_ref, f32[8,128]{1,0:T(8,128)S(1)} %get-tuple-element.41.shift_ref, f32[2,576,128]{2,1,0:T(8,128)S(1)} %get-tuple-element.42.proj_ref, ...), custom_call_target="tpu_custom_call" | custom-call | tf_op jit(solution)/shard_map/pallas_call | solution.py:475
  51.5 15.6 %all_to_all.25.got_ref = f32[32,16,128]{2,1,0:T(8,128)S(1)} all-to-all(f32[32,16,128]{2,1,0:T(8,128)S(1)} %get-tuple-element.49), channel_id=1, replica_groups=mesh['fft'=32,'band'=16] {'fft'}, dimensions={0} | all-to-all | bytes 524288 | tf_op jit(solution)/shard_map/all_to_all | solution.py:491
  67.0 1.5 %shard_map.155 = (f32[256,128]{1,0:T(8,128)S(1)}, f32[32,16,128]{2,1,0:T(8,128)S(1)}) custom-call(s32[8,128]{1,0:T(8,128)S(1)} %get-tuple-element.40.corner_ref, f32[8,128]{1,0:T(8,128)S(1)} %get-tuple-element.41.shift_ref, f32[2,576,128]{2,1,0:T(8,128)S(1)} %get-tuple-element.42.proj_ref, f32[32,16,128]{2,1,0:T(8,128)S(1)} %all_to_all.25.got_ref, ...), custom_call_target="tpu_custom_call" | custom-call | tf_op jit(solution)/shard_map/pallas_call | solution.py:475
  68.6 14.7 %all_to_all.26.got_ref = f32[32,16,128]{2,1,0:T(8,128)S(1)} all-to-all(f32[32,16,128]{2,1,0:T(8,128)S(1)} %get-tuple-element.52), channel_id=1, replica_groups=mesh['fft'=32,'band'=16] {'fft'}, dimensions={0} | all-to-all | bytes 524288 | tf_op jit(solution)/shard_map/all_to_all | solution.py:491
  83.3 2.3 %shard_map.156 = (f32[128,128]{1,0:T(8,128)}, f32[128,128]{1,0:T(8,128)}, f32[16,8,128]{2,1,0:T(8,128)S(1)}) custom-call(s32[8,128]{1,0:T(8,128)S(1)} %get-tuple-element.40.corner_ref, f32[8,128]{1,0:T(8,128)S(1)} %get-tuple-element.41.shift_ref, f32[2,576,128]{2,1,0:T(8,128)S(1)} %get-tuple-element.42.proj_ref, f32[64,128]{1,0:T(8,128)S(1)} %get-tuple-element.43.table_ref, ...), custom_call_target="tpu_custom_call" | custom-call | tf_op jit(solution)/shard_map/pallas_call | solution.py:475
  85.6 19.0 %all_to_all.27 = f32[16,8,128]{2,1,0:T(8,128)S(1)} all-to-all(f32[16,8,128]{2,1,0:T(8,128)S(1)} %get-tuple-element.60), channel_id=1, replica_groups=mesh['fft'=32,'band'=16] {'band'}, dimensions={0} | all-to-all | bytes 131072 | tf_op jit(solution)/shard_map/all_to_all | solution.py:491
  104.6 0.6 reduce_sum.9
Async XLA Ops:
  3.0 11.0 %copy-start = (f32[256,128]{1,0:T(8,128)S(1)}, f32[256,128]{1,0:T(8,128)}, u32[]{:S(2)}) copy-start(f32[256,128]{1,0:T(8,128)} %get-tuple-element.45.both_ref) | copy-start | bytes 393220
  3.1 22.2 %all-to-all-start = ((f32[8,72,128]{2,1,0:T(8,128)}), f32[8,72,128]{2,1,0:T(8,128)S(1)}, u32[]{:S(2)}, u32[]{:S(2)}) async-start(f32[8,72,128]{2,1,0:T(8,128)} %get-tuple-element.32), calls=%async_computation | async-start | bytes 589824 | tf_op jit(solution)/shard_map/all_to_all | solution.py:522
  14.1 5.1 %copy-start.6 = (f32[3]{0:T(128)S(1)}, f32[3]{0:T(128)}, u32[]{:S(2)}) copy-start(f32[3]{0:T(128)} %vector_ref.3) | copy-start | bytes 40
  14.1 6.3 %collective-permute-start = (f32[256,128]{1,0:T(8,128)S(1)}, f32[256,128]{1,0:T(8,128)S(1)}, u32[]{:S(2)}, u32[]{:S(2)}) collective-permute-start(f32[256,128]{1,0:T(8,128)S(1)} %copy-done), channel_id=1, source_target_pairs={{0,384},{16,400},{32,416},{48,432},{64,448},{80,464},{96,480},{112... | collective-permute-start | bytes 393224 | tf_op jit(solution)/shard_map/ppermute | solution.py:520
  25.2 9.8 %collective-permute-start.1 = (f32[8,72,128]{2,1,0:T(8,128)S(1)}, f32[8,72,128]{2,1,0:T(8,128)S(1)}, u32[]{:S(2)}, u32[]{:S(2)}) collective-permute-start(f32[8,72,128]{2,1,0:T(8,128)S(1)} %all-to-all-done.got_ref), channel_id=1, source_target_pairs={{0,128},{16,144},{32,160},{48,176},{64,192},{80,208},{96,224},{112... | collective-permute-start | bytes 884744 | tf_op jit(solution)/shard_map/ppermute | solution.py:528
  35.0 14.8 %all-to-all-start.1 = ((f32[32,16,128]{2,1,0:T(8,128)}), f32[32,16,128]{2,1,0:T(8,128)S(1)}, u32[]{:S(2)}, u32[]{:S(2)}) async-start(f32[32,16,128]{2,1,0:T(8,128)} %shard_map.151), calls=%async_computation.1 | async-start | bytes 524288 | tf_op jit(solution)/shard_map/all_to_all | solution.py:491
  40.1 4.1 %copy-start.5 = (f32[4,8,8]{2,1,0:T(8,128)S(1)}, f32[4,8,8]{2,1,0:T(8,128)}, u32[]{:S(2)}) copy-start(f32[4,8,8]{2,1,0:T(8,128)} %coupling_ref.1) | copy-start | bytes 3076
  40.1 5.0 %copy-start.3 = (f32[2,256,256]{2,1,0:T(8,128)S(1)}, f32[2,256,256]{2,1,0:T(8,128)}, u32[]{:S(2)}) copy-start(f32[2,256,256]{2,1,0:T(8,128)} %constant.8.clone.x_ref) | copy-start | bytes 1572868
  44.3 1.0 copy-start.1
  44.3 1.2 %copy-start.2 = (f32[2,256,256]{2,1,0:T(8,128)S(1)}, f32[2,256,256]{2,1,0:T(8,128)}, u32[]{:S(2)}) copy-start(f32[2,256,256]{2,1,0:T(8,128)} %constant.9.clone.y_ref) | copy-start | bytes 1572868
  44.3 1.2 %copy-start.4 = (f32[2,64,128]{2,1,0:T(8,128)S(1)}, f32[2,64,128]{2,1,0:T(8,128)}, u32[]{:S(2)}) copy-start(f32[2,64,128]{2,1,0:T(8,128)} %param.15) | copy-start | bytes 196612

commit v6 on v5

--- a/solution.py
+++ b/solution.py
@@ -439,7 +439,7 @@
 def final_body(
     corner_ref, shift_ref, proj_ref, table_ref, got_ref, turn_ref, both_ref, first_ref, pot_ref,
     y_high_ref, y_low_ref, z_high_ref, z_low_ref,
-    new_real_ref, new_imag_ref, out_ref, field_ref, place_ref, dual_ref, boxes_ref, done,
+    new_ref, out_ref, field_ref, place_ref, dual_ref, boxes_ref, done,
 ):
     copy = fetch(corner_ref, boxes_ref, done)
     unpack(got_ref, 0, field_ref)
@@ -454,12 +454,24 @@
     second_imag = near[128:] + pot * first[128:] + field_ref[128:256, :] + far_imag
     new_real = both_ref[0:128, :] + time_step * first_ref[128:256, :] - half * second_real
     new_imag = both_ref[128:256, :] - time_step * first_ref[0:128, :] - half * second_imag
-    new_real_ref[...] = new_real
-    new_imag_ref[...] = new_imag
+    new_ref[0:128, :] = new_real
+    new_ref[128:256, :] = new_imag
     weighted = shift_ref[1:2, :] * (new_real * new_real + new_imag * new_imag)
     weighted = weighted.reshape(2, BANDS, 4, LANES)
     for plane in range(2):
         out_ref[:, pl.ds(plane * 4, 4), :] = weighted[plane]
+
+
+def tail_body(got_ref, new_ref, density_ref, real_hbm, imag_hbm, done):
+    copies = [
+        pltpu.make_async_copy(new_ref.at[pl.ds(0, 128)], real_hbm, done.at[0]),
+        pltpu.make_async_copy(new_ref.at[pl.ds(128, 128)], imag_hbm, done.at[1]),
+    ]
+    for copy in copies:
+        copy.start()
+    density_ref[...] = jnp.sum(got_ref[...], axis=0)
+    for copy in copies:
+        copy.wait()
 
 
 def smem():
@@ -551,11 +563,19 @@
         (shape(256, LANES), shape(SLABS, 16, LANES)), (window, square, corner, signal),
     )
     got = exchange(shares, "fft")
-    new_real, new_imag, weighted = call(
+    new, weighted = call(
         final_body, (), (boxes, shift, beta, table, got, turn, both, first, pot, *yz_split),
-        (shape(128, LANES), shape(128, LANES), shape(BANDS, 8, LANES)), (whole, window, square, corner, signal),
-    )
-    density = jnp.sum(exchange(weighted, "band"), axis=0).reshape(2, 4, LANES)
+        (shape(256, LANES), shape(BANDS, 8, LANES)), (whole, window, square, corner, signal),
+    )
+    density, new_real, new_imag = pl.pallas_call(
+        tail_body,
+        out_shape=(shape(8, LANES), shape(128, LANES), shape(128, LANES)),
+        in_specs=[vmem()] * 2,
+        out_specs=(vmem(), anywhere, anywhere),
+        scratch_shapes=[pltpu.SemaphoreType.DMA((2,))],
+        compiler_params=pltpu.CompilerParams(vmem_limit_bytes=24 * 1024 * 1024),
+    )(exchange(weighted, "band"), new)
+    density = density.reshape(2, 4, LANES)
     grid = (1, 2, NY, NZ)
     return new_real.reshape(grid), new_imag.reshape(grid), density
 

time: 106 us -> 106 us (level)
    pallas_call x0 -> x1, Pallas kernels: none -> 1.26 us  [per_device(): pl.pallas_call(tail_body, out_shape=(shape(8, LANES), shape(128, LANES),...]
where the time goes in v6:
time: 106 us; the launch traced here: 105 us
  blocking collectives  57.8 us (55%)
  starting transfers between devices  23.6 us (22%)
  Pallas kernels  13.5 us (13%)
  waiting for transfers between devices  8.42 us (8%)
  between operations  1.44 us (1%)
    all_to_all x3, blocking collectives, exchange(): return lax.all_to_all(value, axis, split_axis=0, concat_axis=0, tiled=True)  49.2 us
    all_to_all x1, starting transfers between devices, per_device(): lax.all_to_all(slices, 'fft', split_axis=0, concat_axis=0, tiled=True, ax...  11 us
    pallas_call x8, Pallas kernels, call(): pl.pallas_call(body, out_shape=outs, in_specs=[smem()] * len(scalars) + [...  9.84 us
    all_to_all x1, starting transfers between devices, exchange(): return lax.all_to_all(value, axis, split_axis=0, concat_axis=0, tiled=True)  5.12 us
    all_to_all x1, waiting for transfers between devices, per_device(): lax.all_to_all(slices, 'fft', split_axis=0, concat_axis=0, tiled=True, ax...  4.83 us
    all_gather x1, blocking collectives, per_device(): gathered = lax.all_gather(got, 'band', axis_index_groups=chips)  4.5 us
    ppermute x1, starting transfers between devices, per_device(): lax.ppermute(both, 'fft', [(i, (i + 24) % SLABS) for i in range(SLABS)])  4.39 us
    all_gather x1, blocking collectives, per_device(): passed = lax.all_gather(passed, 'band', axis_index_groups=chips)  4.1 us
  transfers between devices with their start and end apart: 4, of which 3 were waited for; matrix products, arithmetic and copies ran while one was open for 0% of the time, Pallas kernels for 5%

profile of v6, /device:TPU:1, one launch (start us, length us, event | category | flops | bytes accessed | tf_op | source)
XLA Modules:
  0.0 105.2 jit_solution(11667638647237301331)
XLA Ops:
  0.6 2.4 %shard_map.148 = (f32[8,72,128]{2,1,0:T(8,128)}, f32[256,128]{1,0:T(8,128)}) custom-call(s32[3,4]{1,0:T(4,128)} %boxes_hbm.1, s32[4]{0:T(128)} %species_hbm.1, s32[4,8]{1,0:T(4,128)} %channels_hbm.1, f32[4,8,4096]{2,1,0:T(8,128)} %proj_hbm.1, f32[128,128]{1,0:T(8,128)} %bitcast.14, f32[128,128]{1,0:T(8,128)} %bitcast.15), custom_call_target="tpu_custom_call" | custom-call | tf_op jit(solution)/shard_map/pallas_call | solution.py:521
  3.1 0.0 copy-start
  3.1 11.0 %all-to-all-start = ((f32[8,72,128]{2,1,0:T(8,128)}), f32[8,72,128]{2,1,0:T(8,128)S(1)}, u32[]{:S(2)}, u32[]{:S(2)}) async-start(f32[8,72,128]{2,1,0:T(8,128)} %get-tuple-element.34), calls=%async_computation | async-start | bytes 589824 | tf_op jit(solution)/shard_map/all_to_all | solution.py:534
  14.1 0.0 copy-done
  14.1 0.0 copy-start.6
  14.1 4.4 %collective-permute-start = (f32[256,128]{1,0:T(8,128)S(1)}, f32[256,128]{1,0:T(8,128)S(1)}, u32[]{:S(2)}, u32[]{:S(2)}) collective-permute-start(f32[256,128]{1,0:T(8,128)S(1)} %copy-done), channel_id=1, source_target_pairs={{0,384},{16,400},{32,416},{48,432},{64,448},{80,464},{96,480},{112... | collective-permute-start | bytes 393224 | tf_op jit(solution)/shard_map/ppermute | solution.py:532
  19.1 0.0 copy-done.6
  19.1 1.1 %shard_map.149 = (f32[4,128,128]{2,1,0:T(8,128)S(1)}, f32[8,128]{1,0:T(8,128)S(1)}) custom-call(f32[3]{0:T(128)S(1)} %copy-done.6, f32[1]{0:T(128)S(6)} %copy.16.occupation_ref), custom_call_target="tpu_custom_call" | custom-call | tf_op jit(solution)/shard_map/pallas_call | solution.py:487
  20.2 0.2 collective-permute-done.next_ref
  20.4 4.8 %all-to-all-done.got_ref = f32[8,72,128]{2,1,0:T(8,128)S(1)} async-done(((f32[8,72,128]{2,1,0:T(8,128)}), f32[8,72,128]{2,1,0:T(8,128)S(1)}, u32[]{:S(2)}, u32[]{:S(2)}) %all-to-all-start) | async-done | bytes 294944 | tf_op jit(solution)/shard_map/all_to_all | solution.py:534
  25.2 3.1 %collective-permute-start.1 = (f32[8,72,128]{2,1,0:T(8,128)S(1)}, f32[8,72,128]{2,1,0:T(8,128)S(1)}, u32[]{:S(2)}, u32[]{:S(2)}) collective-permute-start(f32[8,72,128]{2,1,0:T(8,128)S(1)} %all-to-all-done.got_ref), channel_id=1, source_target_pairs={{0,128},{16,144},{32,160},{48,176},{64,192},{80,208},{96,224},{112... | collective-permute-start | bytes 884744 | tf_op jit(solution)/shard_map/ppermute | solution.py:540
  28.4 0.1 shard_map.150.corner_ref
  28.5 4.5 %all-gather = f32[16,72,128]{2,1,0:T(8,128)S(1)} all-gather(f32[8,72,128]{2,1,0:T(8,128)S(1)} %all-to-all-done.got_ref), channel_id=2, replica_groups={{0,1},{2,3},{4,5},{6,7},{8,9},{10,11},{12,13},{14,15},{16,17},{18,19},{..., dimensions={0}, use_global_device_ids=true | all-gather | bytes 884736 | tf_op jit(solution)/shard_map/all_gather | solution.py:538
  33.0 2.0 %shard_map.151 = f32[32,16,128]{2,1,0:T(8,128)} custom-call(s32[8,128]{1,0:T(8,128)S(1)} %shard_map.150.corner_ref, f32[2,576,128]{2,1,0:T(8,128)S(1)} %bitcast.9, f32[256,128]{1,0:T(8,128)S(1)} %copy-done, f32[256,128]{1,0:T(8,128)S(1)} %collective-permute-done.next_ref, f32[4,128,128]{2,1,0:T(8,128)S(1)} %get-tuple-element.40.turn_ref), custom_call_target="tpu_custom_call" | custom-call | tf_op jit(solution)/shard_map/pallas_call | solution.py:487
  35.0 0.0 collective-permute-done.1
  35.0 5.1 %all-to-all-start.1 = ((f32[32,16,128]{2,1,0:T(8,128)}), f32[32,16,128]{2,1,0:T(8,128)S(1)}, u32[]{:S(2)}, u32[]{:S(2)}) async-start(f32[32,16,128]{2,1,0:T(8,128)} %shard_map.151), calls=%async_computation.1 | async-start | bytes 524288 | tf_op jit(solution)/shard_map/all_to_all | solution.py:503
  40.1 0.0 copy-start.5
  40.2 0.0 copy-start.3
  40.2 4.1 %all-gather.1 = f32[16,72,128]{2,1,0:T(8,128)S(1)} all-gather(f32[8,72,128]{2,1,0:T(8,128)S(1)} %collective-permute-done.1), channel_id=3, replica_groups={{0,1},{2,3},{4,5},{6,7},{8,9},{10,11},{12,13},{14,15},{16,17},{18,19},{..., dimensions={0}, use_global_device_ids=true | all-gather | bytes 884736 | tf_op jit(solution)/shard_map/all_gather | solution.py:550
  44.3 0.0 copy-done.5
  44.3 0.0 copy-start.1
  44.3 0.0 copy-start.2
  44.3 0.0 copy-start.4
  44.3 0.8 shard_map.152
  45.1 0.0 copy-done.3
  45.1 0.2 copy-done.1
  45.3 0.2 copy-done.2
  45.5 0.0 copy-done.4
  45.5 0.9 shard_map.153
  46.4 3.4 %all-to-all-done.1.got_ref = f32[32,16,128]{2,1,0:T(8,128)S(1)} async-done(((f32[32,16,128]{2,1,0:T(8,128)}), f32[32,16,128]{2,1,0:T(8,128)S(1)}, u32[]{:S(2)}, u32[]{:S(2)}) %all-to-all-start.1) | async-done | bytes 262176 | tf_op jit(solution)/shard_map/all_to_all | solution.py:503
  49.8 1.7 %shard_map.154 = (f32[256,128]{1,0:T(8,128)S(1)}, f32[256,128]{1,0:T(8,128)S(1)}, f32[32,16,128]{2,1,0:T(8,128)S(1)}) custom-call(s32[8,128]{1,0:T(8,128)S(1)} %get-tuple-element.42.corner_ref, f32[8,128]{1,0:T(8,128)S(1)} %get-tuple-element.43.shift_ref, f32[2,576,128]{2,1,0:T(8,128)S(1)} %get-tuple-element.44.proj_ref, ...), custom_call_target="tpu_custom_call" | custom-call | tf_op jit(solution)/shard_map/pallas_call | solution.py:487
  51.5 15.6 %all_to_all.25.got_ref = f32[32,16,128]{2,1,0:T(8,128)S(1)} all-to-all(f32[32,16,128]{2,1,0:T(8,128)S(1)} %get-tuple-element.51), channel_id=1, replica_groups=mesh['fft'=32,'band'=16] {'fft'}, dimensions={0} | all-to-all | bytes 524288 | tf_op jit(solution)/shard_map/all_to_all | solution.py:503
  67.1 1.5 %shard_map.155 = (f32[256,128]{1,0:T(8,128)S(1)}, f32[32,16,128]{2,1,0:T(8,128)S(1)}) custom-call(s32[8,128]{1,0:T(8,128)S(1)} %get-tuple-element.42.corner_ref, f32[8,128]{1,0:T(8,128)S(1)} %get-tuple-element.43.shift_ref, f32[2,576,128]{2,1,0:T(8,128)S(1)} %get-tuple-element.44.proj_ref, f32[32,16,128]{2,1,0:T(8,128)S(1)} %all_to_all.25.got_ref, ...), custom_call_target="tpu_custom_call" | custom-call | tf_op jit(solution)/shard_map/pallas_call | solution.py:487
  68.6 14.6 %all_to_all.26.got_ref = f32[32,16,128]{2,1,0:T(8,128)S(1)} all-to-all(f32[32,16,128]{2,1,0:T(8,128)S(1)} %get-tuple-element.54), channel_id=1, replica_groups=mesh['fft'=32,'band'=16] {'fft'}, dimensions={0} | all-to-all | bytes 524288 | tf_op jit(solution)/shard_map/all_to_all | solution.py:503
  83.2 1.7 %shard_map.156 = (f32[256,128]{1,0:T(8,128)S(1)}, f32[16,8,128]{2,1,0:T(8,128)S(1)}) custom-call(s32[8,128]{1,0:T(8,128)S(1)} %get-tuple-element.42.corner_ref, f32[8,128]{1,0:T(8,128)S(1)} %get-tuple-element.43.shift_ref, f32[2,576,128]{2,1,0:T(8,128)S(1)} %get-tuple-element.44.proj_ref, f32[64,128]{1,0:T(8,128)S(1)} %get-tuple-element.45.table_ref, ...), custom_call_target="tpu_custom_call" | custom-call | tf_op jit(solution)/shard_map/pallas_call | solution.py:487
  84.9 19.0 %all_to_all.27.got_ref = f32[16,8,128]{2,1,0:T(8,128)S(1)} all-to-all(f32[16,8,128]{2,1,0:T(8,128)S(1)} %get-tuple-element.60), channel_id=1, replica_groups=mesh['fft'=32,'band'=16] {'band'}, dimensions={0} | all-to-all | bytes 131072 | tf_op jit(solution)/shard_map/all_to_all | solution.py:503
  103.9 1.3 %shard_map.157 = (f32[8,128]{1,0:T(8,128)}, f32[128,128]{1,0:T(8,128)}, f32[128,128]{1,0:T(8,128)}) custom-call(f32[16,8,128]{2,1,0:T(8,128)S(1)} %all_to_all.27.got_ref, f32[256,128]{1,0:T(8,128)S(1)} %get-tuple-element.61.new_ref), custom_call_target="tpu_custom_call" | custom-call | tf_op jit(solution)/shard_map/pallas_call | solution.py:570
Async XLA Ops:
  3.1 11.0 %copy-start = (f32[256,128]{1,0:T(8,128)S(1)}, f32[256,128]{1,0:T(8,128)}, u32[]{:S(2)}) copy-start(f32[256,128]{1,0:T(8,128)} %get-tuple-element.47.both_ref) | copy-start | bytes 393220
  3.1 22.2 %all-to-all-start = ((f32[8,72,128]{2,1,0:T(8,128)}), f32[8,72,128]{2,1,0:T(8,128)S(1)}, u32[]{:S(2)}, u32[]{:S(2)}) async-start(f32[8,72,128]{2,1,0:T(8,128)} %get-tuple-element.34), calls=%async_computation | async-start | bytes 589824 | tf_op jit(solution)/shard_map/all_to_all | solution.py:534
  14.1 5.1 %copy-start.6 = (f32[3]{0:T(128)S(1)}, f32[3]{0:T(128)}, u32[]{:S(2)}) copy-start(f32[3]{0:T(128)} %vector_ref.3) | copy-start | bytes 40
  14.1 6.3 %collective-permute-start = (f32[256,128]{1,0:T(8,128)S(1)}, f32[256,128]{1,0:T(8,128)S(1)}, u32[]{:S(2)}, u32[]{:S(2)}) collective-permute-start(f32[256,128]{1,0:T(8,128)S(1)} %copy-done), channel_id=1, source_target_pairs={{0,384},{16,400},{32,416},{48,432},{64,448},{80,464},{96,480},{112... | collective-permute-start | bytes 393224 | tf_op jit(solution)/shard_map/ppermute | solution.py:532
  25.2 9.8 %collective-permute-start.1 = (f32[8,72,128]{2,1,0:T(8,128)S(1)}, f32[8,72,128]{2,1,0:T(8,128)S(1)}, u32[]{:S(2)}, u32[]{:S(2)}) collective-permute-start(f32[8,72,128]{2,1,0:T(8,128)S(1)} %all-to-all-done.got_ref), channel_id=1, source_target_pairs={{0,128},{16,144},{32,160},{48,176},{64,192},{80,208},{96,224},{112... | collective-permute-start | bytes 884744 | tf_op jit(solution)/shard_map/ppermute | solution.py:540
  35.0 14.8 %all-to-all-start.1 = ((f32[32,16,128]{2,1,0:T(8,128)}), f32[32,16,128]{2,1,0:T(8,128)S(1)}, u32[]{:S(2)}, u32[]{:S(2)}) async-start(f32[32,16,128]{2,1,0:T(8,128)} %shard_map.151), calls=%async_computation.1 | async-start | bytes 524288 | tf_op jit(solution)/shard_map/all_to_all | solution.py:503
  40.1 4.1 %copy-start.5 = (f32[4,8,8]{2,1,0:T(8,128)S(1)}, f32[4,8,8]{2,1,0:T(8,128)}, u32[]{:S(2)}) copy-start(f32[4,8,8]{2,1,0:T(8,128)} %coupling_ref.1) | copy-start | bytes 3076
  40.2 5.0 %copy-start.3 = (f32[2,256,256]{2,1,0:T(8,128)S(1)}, f32[2,256,256]{2,1,0:T(8,128)}, u32[]{:S(2)}) copy-start(f32[2,256,256]{2,1,0:T(8,128)} %constant.6.clone.x_ref) | copy-start | bytes 1572868
  44.3 1.0 copy-start.1
  44.3 1.2 %copy-start.2 = (f32[2,256,256]{2,1,0:T(8,128)S(1)}, f32[2,256,256]{2,1,0:T(8,128)}, u32[]{:S(2)}) copy-start(f32[2,256,256]{2,1,0:T(8,128)} %constant.7.clone.y_ref) | copy-start | bytes 1572868
  44.3 1.2 %copy-start.4 = (f32[2,64,128]{2,1,0:T(8,128)S(1)}, f32[2,64,128]{2,1,0:T(8,128)}, u32[]{:S(2)}) copy-start(f32[2,64,128]{2,1,0:T(8,128)} %param.15) | copy-start | bytes 196612
